TPU v7x, 256 devices: a whole 4x4x8 slice. The times are simulated.
256 devices in a mesh: patch: 64 (over y_hi, x, z), head: 4 (over y_lo, core).
Axes of the slice: x: 4, y: 4 (y_hi: 2, y_lo: 2; y = y_hi * 2 + y_lo), z: 8, core: 2. Of those that a mesh axis runs over, the one named last changes fastest.
Arguments:
- image_hidden: bfloat16 [2, 4096, 3072], P(None, 'patch', 'head'), may hold values from -6 to 6
- text_kv: bfloat16 [2, 2, 512, 1536], P(None, None, 'patch', 'head'), may hold values from -96 to 96
- prev_kv: bfloat16 [2, 2, 4096, 1536], P(None, None, None, 'head'), may hold values from -12 to 12
- scale_exp: int32 [2, 2, 4096, 12], P(None, None, 'patch', 'head'), may hold values from -8 to 0
- w_qkv: bfloat16 [3072, 3, 1536], P('patch', None, 'head'), may hold values from -0.109375 to 0.109375
- w_out: bfloat16 [1536, 3072], P('head', 'patch'), may hold values from -0.15625 to 0.15625
- mod_table: bfloat16 [28, 3, 3072], P(None, None, 'head'), may hold values from -4 to 4
- timesteps: int32 [2], replicated, may hold values from 0 to 27, as said below
- q_gain: float32 [128], replicated, may hold values from 1 to 1.8
- k_gain: float32 [128], replicated, may hold values from 1 to 1.8
Outputs:
- branch: bfloat16 [2, 4096, 3072], P(None, 'patch', 'head')
Inputs may be any that keep to these rules, and one draw needn't show every extreme that they name: `timesteps`: the images of a batch are at distinct plan points, one of them the last.
All inputs are finite; a program needn't handle non-finite values.
Results may differ from a plain program's by a relative error of at most 0.017.
Values may be sent and summed in bfloat16 or wider, within the bound.
No kernel may reach another device: no remote copies, remote signals or barrier semaphores. Data moves between devices by JAX's collectives and lax.ppermute only.
A program may use at most 192 MiB of HBM per device.

v0:
```python
import jax
import jax.numpy as jnp
from jax import lax
from jax.sharding import PartitionSpec as P

HD = 128


EPSILON = 1e-06
CODE_LIMIT = 448.0


def power_two(exponents, polarity):
    summed_powers = jnp.zeros(exponents.shape, jnp.float32)
    for exponent in range(-8, 1):
        summed_powers = summed_powers + jnp.where(
            exponents == exponent, jnp.float32(2.0 ** (polarity * exponent)), jnp.float32(0.0)
        )
    return summed_powers


def rms_scale(vectors, softmax_scaling):
    return (
        vectors
        * lax.rsqrt(jnp.mean(vectors * vectors, axis=-1, keepdims=True) + EPSILON)
        * softmax_scaling
    )


def restore_rows(code_rows, scale_rows, earlier):
    lead_shape = code_rows.shape[:3]
    head_count = scale_rows.shape[3]
    scaled_codes = (
        code_rows.astype(jnp.float32).reshape(lead_shape + (head_count, -1))
        * scale_rows.astype(jnp.float32)[..., None]
    )
    rebuilt = earlier.astype(jnp.float32).reshape(lead_shape + (head_count, -1)) + scaled_codes
    return rebuilt.astype(jnp.bfloat16).reshape(code_rows.shape)


def attend_block(attention_state, queries, keys_part, values_part):
    running_max, denominator, accumulated = attention_state
    logits = jnp.einsum(
        "brhd,bkhd->bhrk", queries, keys_part, preferred_element_type=jnp.float32
    ) * queries.shape[-1] ** (-0.5)
    raised_max = jnp.maximum(running_max, jnp.max(logits, axis=-1))
    rescale = jnp.exp(running_max - raised_max)
    exponent_terms = jnp.exp(logits - raised_max[..., None])
    denominator = denominator * rescale + jnp.sum(exponent_terms, axis=-1)
    contribution = jnp.einsum(
        "bhrk,bkhd->brhd",
        exponent_terms.astype(jnp.bfloat16),
        values_part,
        preferred_element_type=jnp.float32,
    )
    accumulated = accumulated * jnp.transpose(rescale, (0, 2, 1))[..., None] + contribution
    return (raised_max, denominator, accumulated)


def attend_pair(attention_state, queries, kv_pair):
    images, key_count = (kv_pair.shape[1], kv_pair.shape[2])
    shaped = kv_pair.reshape((2, images, key_count) + queries.shape[2:])
    return attend_block(attention_state, queries, shaped[0], shaped[1])


def per_device(
    image_hidden, text_kv, prev_kv, scale_exp, w_qkv, w_out, mod_table, timesteps, q_gain, k_gain
):
    images, tok_rows = (image_hidden.shape[0], image_hidden.shape[1])
    plan = mod_table.shape[0]
    selector = (timesteps[:, None] == jnp.arange(plan, dtype=jnp.int32)[None, :]).astype(
        jnp.bfloat16
    )
    picked = jnp.einsum(
        "bs,scd->bcd", selector, mod_table, preferred_element_type=jnp.float32
    ).astype(jnp.bfloat16)
    all_features, all_modulation = (
        lax.all_gather(image_hidden, "head", axis=2, tiled=True),
        lax.all_gather(picked, "head", axis=2, tiled=True),
    )
    hidden = all_features.astype(jnp.float32)
    modulation = all_modulation.astype(jnp.float32)
    centre = jnp.mean(hidden, axis=-1, keepdims=True)
    variance = jnp.mean((hidden - centre) * (hidden - centre), axis=-1, keepdims=True)
    normed = (
        (hidden - centre) * lax.rsqrt(variance + EPSILON) * (1.0 + modulation[:, 1:2])
        + modulation[:, 0:1]
    ).astype(jnp.bfloat16)
    local_width = w_qkv.shape[2]
    heads_here = local_width // HD
    projected = jnp.einsum(
        "brd,dce->brce",
        normed,
        lax.all_gather(w_qkv, "patch", axis=0, tiled=True),
        preferred_element_type=jnp.float32,
    )
    split_shape = (images, tok_rows, heads_here, HD)
    queries = rms_scale(projected[:, :, 0].reshape(split_shape), q_gain).astype(jnp.bfloat16)
    fresh_keys = rms_scale(projected[:, :, 1].reshape(split_shape), k_gain)
    fresh_values = projected[:, :, 2].reshape(split_shape)
    own_start = lax.axis_index("patch") * tok_rows
    own_prev = lax.dynamic_slice_in_dim(prev_kv, own_start, tok_rows, 2)
    fresh_pair = jnp.stack([fresh_keys, fresh_values]).reshape(own_prev.shape)
    residual = fresh_pair - own_prev.astype(jnp.float32)
    inverse = jnp.repeat(power_two(scale_exp, -1), HD, axis=3)
    block_codes = jnp.clip(residual * inverse, -CODE_LIMIT, CODE_LIMIT).astype(jnp.bfloat16)
    block_scales = power_two(scale_exp, 1).astype(jnp.bfloat16)
    text_all = lax.all_gather(text_kv, "patch", axis=2, tiled=True)
    start_state = (
        jnp.full((images, heads_here, tok_rows), -jnp.inf, jnp.float32),
        jnp.zeros((images, heads_here, tok_rows), jnp.float32),
        jnp.zeros(split_shape, jnp.float32),
    )
    attention_state = attend_pair(start_state, queries, text_all)
    gathered = (
        lax.all_gather(block_codes, "patch", axis=2, tiled=True),
        lax.all_gather(block_scales, "patch", axis=2, tiled=True),
    )
    attention_state = attend_pair(
        attention_state, queries, restore_rows(gathered[0], gathered[1], prev_kv)
    )
    running_max, denominator, accumulated = attention_state
    attended = (
        (accumulated / jnp.transpose(denominator, (0, 2, 1))[..., None])
        .astype(jnp.bfloat16)
        .reshape(images, tok_rows, local_width)
    )
    head_partial = jnp.einsum(
        "brc,cm->brm",
        attended,
        lax.all_gather(w_out, "patch", axis=1, tiled=True),
        preferred_element_type=jnp.float32,
    )
    summed = lax.psum_scatter(
        head_partial.astype(jnp.bfloat16), "head", scatter_dimension=2, tiled=True
    ).astype(jnp.float32)
    return (picked[:, 2:3, :].astype(jnp.float32) * summed).astype(jnp.bfloat16)


def solution(mesh):
    placed = (
        P(None, "patch", "head"),
        P(None, None, "patch", "head"),
        P(None, None, None, "head"),
        P(None, None, "patch", "head"),
        P("patch", None, "head"),
        P("head", "patch"),
        P(None, None, "head"),
        P(),
        P(),
        P(),
    )
    return jax.shard_map(
        per_device, mesh=mesh, in_specs=placed, out_specs=P(None, "patch", "head"), check_vma=False
    )
```

profile of v0, /device:TPU:7, one launch (start us, length us, event | category | flops | bytes accessed | tf_op | source)
XLA Modules:
  0.0 595.7 jit_solution(2266008806367216604)
XLA Ops:
  6.5 0.0 copy-start
  6.5 0.0 all-gather.5.cloned.1.call-start
  6.5 0.7 all-gather.5.cloned.1.call-update
  7.3 0.0 all-gather.7.cloned.1.call-start
  7.3 1.4 copy.110
  8.7 0.0 all-gather.7.cloned.1.call-update
  8.7 0.0 all-gather.9.cloned.1.call-start
  8.7 9.4 %all_gather.21 = bf16[2,64,3072]{2,1,0:T(8,128)(2,1)S(1)} all-gather(bf16[2,64,768]{2,1,0:T(8,128)(2,1)} %param.10), channel_id=1, replica_groups=mesh['patch'=64,'head'=4] {'head'}, dimensions={2}, use_global_device_ids=true | all-gather | bytes 983040 | tf_op jit(solution)/shard_map/all_gather | solution.py:78
  18.1 0.2 convert_reduce_fusion
  18.3 0.7 add_convert_fusion.1
  19.1 0.0 copy-done
  19.1 0.9 convolution_convert_fusion.1
  20.0 5.2 all_gather.22
  25.2 0.1 copy.119
  25.3 0.3 broadcast_in_dim.110
  25.6 0.2 reshape.95
  25.9 0.4 fusion.12
  26.2 0.7 broadcast_bitcast_fusion
  26.9 125.1 %all-gather.5.cloned.1.call-done = bf16[3072,3,384]{2,0,1:T(8,128)(2,1)} async-done(((bf16[48,3,384]{2,0,1:T(8,128)(2,1)}), bf16[3072,3,384]{2,0,1:T(8,128)(2,1)}) %all-gather.5.cloned.1.call-update) | async-done | bytes 7077904 | tf_op jit(solution)/shard_map/all_gather | solution.py:94
  152.0 4.2 fusion
  156.2 0.1 mul.166
  156.3 0.2 reduce_sum.61
  156.6 0.2 mul.167
  156.8 0.1 mul.168
  157.0 1.7 fusion.36
  158.7 0.0 all-gather.9.cloned.1.call-update
  158.7 0.0 all-gather.11.cloned.1.call-start
  158.7 0.5 all-gather.11.cloned.1.call-update
  159.3 0.0 reduce-scatter.2.cloned.1.call-start
  159.3 16.8 %copy.115 = bf16[2,2,4096,384]{2,3,1,0:T(8,128)(2,1)} copy(bf16[2,2,4096,384]{3,2,1,0:T(8,128)(2,1)} %param.12) | data formatting | bytes 25165824 | tf_op args[2]
  176.1 0.1 copy.121
  176.3 167.0 %all_gather.26 = bf16[2,2,4096,3]{3,1,0,2:T(2,128)(2,1)} all-gather(bf16[2,2,64,3]{3,1,0,2:T(2,128)(2,1)S(1)} %copy.121), channel_id=1, replica_groups=mesh['patch'=64,'head'=4] {'patch'}, dimensions={2}, use_global_device_ids=true | all-gather | bytes 99840 | tf_op jit(solution)/shard_map/all_gather | solution.py:117
  343.3 8.9 %copy.122 = bf16[2,2,4096,3]{2,1,3,0:T(2,128)(2,1)S(1)} copy(bf16[2,2,4096,3]{3,1,0,2:T(2,128)(2,1)} %all_gather.26) | data formatting | bytes 196608 | tf_op jit(solution)/shard_map/all_gather | solution.py:117
  352.2 0.1 copy.123
  352.3 18.0 %copy.125 = f32[2,2,4096,3,128]{4,2,3,1,0:T(8,128)} copy(bf16[2,2,4096,3,128]{2,4,3,1,0:T(8,128)(2,1)} %bitcast.105) | data formatting | bytes 37748736 | tf_op jit(solution)/shard_map/reshape | solution.py:37
  370.2 0.0 copy-start.2
  370.3 0.0 all-gather.7.cloned.1.call-done
  370.3 2.5 fusion.56
  372.7 1.1 copy.130
  373.8 1.1 copy.131
  374.9 0.1 reshape_squeeze.6
  375.0 0.2 multiply_reduce_fusion
  375.3 0.1 copy.108
  375.3 0.0 copy-done.2
  375.3 0.4 fusion.58
  375.7 0.3 fusion.31
  376.0 70.4 %all-gather.9.cloned.1.call-done = bf16[2,2,4096,384]{3,2,1,0:T(8,128)(2,1)} async-done(((bf16[2,2,64,384]{3,2,1,0:T(8,128)(2,1)}), bf16[2,2,4096,384]{3,2,1,0:T(8,128)(2,1)}) %all-gather.9.cloned.1.call-update) | async-done | bytes 12582928 | tf_op jit(solution)/shard_map/all_gather | solution.py:116
  446.4 17.6 %copy.120 = f32[2,2,4096,384]{2,3,1,0:T(8,128)} copy(bf16[2,2,4096,384]{3,2,1,0:T(8,128)(2,1)} %all-gather.9.cloned.1.call-done) | data formatting | bytes 37748736 | tf_op jit(solution)/shard_map/reshape | solution.py:34
  464.0 24.7 %copy.124 = f32[2,2,4096,3,128]{4,2,3,1,0:T(8,128)} copy(f32[2,2,4096,3,128]{2,4,3,1,0:T(8,128)} %bitcast.104) | data formatting | bytes 50331648 | tf_op jit(solution)/shard_map/reshape | solution.py:34
  488.7 17.4 %add_convert_fusion = bf16[2,2,4096,3,128]{4,2,3,1,0:T(8,128)(2,1)S(1)} fusion(f32[2,2,4096,3,128]{4,2,3,1,0:T(8,128)} %copy.125, f32[2,2,4096,3,128]{4,2,3,1,0:T(8,128)} %copy.124, f32[2,2,4096,3]{2,3,1,0:T(4,128)S(1)} %copy.123), kind=kLoop, calls=%fused_computation | loop fusion | flops 18874368 | bytes 63111168 | tf_op jit(solution)/shard_map/convert_element_type | solution.py:38
  506.1 2.5 fusion.59
  508.6 1.0 fusion.5
  509.6 0.0 copy-start.1
  509.6 1.4 fusion.20
  511.1 0.4 fusion.24
  511.5 50.3 %all-gather.11.cloned.1.call-done = bf16[384,3072]{0,1:T(8,128)(2,1)} async-done(((bf16[384,48]{0,1:T(8,128)(2,1)}), bf16[384,3072]{0,1:T(8,128)(2,1)}) %all-gather.11.cloned.1.call-update) | async-done | bytes 2359312 | tf_op jit(solution)/shard_map/all_gather | solution.py:131
  561.8 3.4 convolution_convert_fusion
  565.2 0.0 reduce-scatter.2.cloned.1.call-update
  565.3 22.3 %reduce-scatter.2.cloned.1.call-done = bf16[2,64,768]{2,1,0:T(8,128)(2,1)} async-done(((bf16[2,64,3072]{2,1,0:T(8,128)(2,1)}), bf16[2,64,768]{2,1,0:T(8,128)(2,1)}) %reduce-scatter.2.cloned.1.call-update) | async-done | bytes 196624 | tf_op jit(solution)/shard_map/reduce_scatter | solution.py:134
  587.6 1.6 multiply_convert_fusion
  589.2 0.0 copy-done.1
  (12 shorter events, 0.2 us)
Async XLA Ops:
  6.5 12.5 %copy-start = (bf16[28,3,768]{2,0,1:T(8,128)(2,1)S(1)}, bf16[28,3,768]{2,0,1:T(8,128)(2,1)}, u32[]{:S(2)}) copy-start(bf16[28,3,768]{2,0,1:T(8,128)(2,1)} %param.16) | copy-start | bytes 387076
  6.5 145.4 %all-gather.5.cloned.1.call-start = ((), (), s32[]{:S(2)}) async-start(), calls=%async_computation.1 | async-start | bytes 7188480 | tf_op jit(solution)/shard_map/all_gather | solution.py:94
  7.3 363.0 %all-gather.7.cloned.1.call-start = ((), (), s32[]{:S(2)}) async-start(), calls=%async_computation.2 | async-start | bytes 1597440 | tf_op jit(solution)/shard_map/all_gather | solution.py:108
  8.7 437.7 %all-gather.9.cloned.1.call-start = ((), (), s32[]{:S(2)}) async-start(), calls=%async_computation.3 | async-start | bytes 12779520 | tf_op jit(solution)/shard_map/all_gather | solution.py:116
  158.7 403.2 %all-gather.11.cloned.1.call-start = ((), (), s32[]{:S(2)}) async-start(), calls=%async_computation.4 | async-start | bytes 2396160 | tf_op jit(solution)/shard_map/all_gather | solution.py:131
  159.3 428.3 %reduce-scatter.2.cloned.1.call-start = ((), (), s32[]{:S(2)}) async-start(), calls=%async_computation.5 | async-start | bytes 983040 | tf_op jit(solution)/shard_map/reduce_scatter | solution.py:134
  370.2 5.1 copy-start.2
  509.6 79.6 %copy-start.1 = (bf16[28,3,768]{2,0,1:T(8,128)(2,1)S(1)}, bf16[28,3,768]{2,0,1:T(8,128)(2,1)}, u32[]{:S(2)}) copy-start(bf16[28,3,768]{2,0,1:T(8,128)(2,1)} %param.16) | copy-start | bytes 387076
Sparse Core Ops, SparseCore 0:
  11.1 140.8 all-gather.4
  155.6 113.3 all-gather.6
  272.6 173.7 all-gather.8
  450.0 111.8 all-gather.10
  565.4 22.1 reduce-scatter.1
where the time goes:
time: 599 us; the launch traced here: 596 us
  waiting for transfers between devices  269 us (45%)
  blocking collectives  182 us (30%)
  local copies, waits for them, and re-layouts  94.1 us (16%)
  other arithmetic  23.9 us (4%)
  between operations  13.4 us (2%)
  matrix products  13.2 us (2%)
    all_gather x1, blocking collectives, per_device(): lax.all_gather(block_scales, 'patch', axis=2, tiled=True)  167 us
    all_gather x1, waiting for transfers between devices, per_device(): lax.all_gather(w_qkv, 'patch', axis=0, tiled=True)  125 us
    all_gather x1, waiting for transfers between devices, per_device(): lax.all_gather(block_codes, 'patch', axis=2, tiled=True)  70.4 us
    all_gather x1, waiting for transfers between devices, per_device(): lax.all_gather(w_out, 'patch', axis=1, tiled=True)  50.3 us
    reshape x2, local copies, waits for them, and re-layouts, restore_rows(): code_rows.astype(jnp.float32).reshape(lead_shape + (head_count, -1))  42.3 us
    reduce_scatter x1, waiting for transfers between devices, per_device(): lax.psum_scatter(head_partial.astype(jnp.bfloat16), 'head', scatter_dimen...  22.3 us
    unnamed x10, local copies, waits for them, and re-layouts  20.4 us
    reshape x1, local copies, waits for them, and re-layouts, restore_rows(): earlier.astype(jnp.float32).reshape(lead_shape + (head_count, -1))  18 us
  transfers between devices with their start and end apart: 5, of which 4 were waited for; matrix products, arithmetic and copies ran while one was open for 21% of the time, Pallas kernels for 0%

commit v1 on v0

v1 whole, which is shorter than its diff:
```python
import jax
import jax.numpy as jnp
from jax import lax
from jax.experimental import pallas as pl
from jax.experimental.pallas import tpu as pltpu
from jax.sharding import Mesh, PartitionSpec as P

HD = 128
EPSILON = 1e-06
CODE_LIMIT = 448.0
LOG2E = 1.4426950408889634
VMEM_BYTES = 56 * 1024 * 1024

YX = ("yh", "x")
Z = ("zo", "zi")
H = ("yl", "c")


def call(kernel, out_shapes, operands, scratch=(), flops=0, moved=0):
    return pl.pallas_call(
        kernel,
        out_shape=out_shapes,
        in_specs=[pl.BlockSpec(memory_space=pltpu.VMEM)] * len(operands),
        out_specs=jax.tree.map(lambda _: pl.BlockSpec(memory_space=pltpu.VMEM), out_shapes),
        scratch_shapes=scratch,
        compiler_params=pltpu.CompilerParams(vmem_limit_bytes=VMEM_BYTES),
        cost_estimate=pl.CostEstimate(flops=flops, bytes_accessed=moved, transcendentals=0),
    )(*operands)


def norm_kernel(rows_ref, out_ref):
    features = 4 * 768
    for image in range(2):
        shift = rows_ref[:, 128 + 2 * image : 129 + 2 * image, :].astype(jnp.float32)
        scale = 1.0 + rows_ref[:, 129 + 2 * image : 130 + 2 * image, :].astype(jnp.float32)
        for start in range(0, 64, 16):
            at = image * 64 + start
            hidden = rows_ref[:, at : at + 16, :].astype(jnp.float32)
            centre = jnp.sum(jnp.sum(hidden, axis=0), axis=-1, keepdims=True) / features
            off = hidden - centre[None]
            variance = jnp.sum(jnp.sum(off * off, axis=0), axis=-1, keepdims=True) / features
            normed = (off * lax.rsqrt(variance + EPSILON)[None] * scale + shift).astype(jnp.bfloat16)
            for y in range(2):
                for x in range(4):
                    for place, block in enumerate((4 * y + x, 4 * (1 - y) + x)):
                        piece = normed[block // 2][:, (block % 2) * 384 : (block % 2) * 384 + 384]
                        out_ref[4 * y + x, at : at + 16, place * 384 : place * 384 + 384] = piece


def project_kernel(rows_ref, weights_ref, out_ref):
    weights = weights_ref[...].reshape(384, 1536)
    for x in range(4):
        rows = jnp.concatenate([rows_ref[x], rows_ref[4 + x]], axis=0)
        own, other = rows[:, :384], rows[:, 384:]
        most = jnp.dot(own, weights[:, :512], preferred_element_type=jnp.float32) + jnp.dot(
            other, weights[:, 512:1024], preferred_element_type=jnp.float32
        )
        rest = jnp.dot(own, weights[:, 1024:1152], preferred_element_type=jnp.float32)
        both = jnp.concatenate([most, rest], axis=1).astype(jnp.bfloat16)
        for image in range(2):
            for y in range(2):
                piece = both[y * 128 + image * 64 : y * 128 + image * 64 + 64]
                out_ref[4 * image + x, y * 64 : y * 64 + 64, :] = piece


def rms_scale(vectors, gain):
    return vectors * lax.rsqrt(jnp.mean(vectors * vectors, axis=-1, keepdims=True) + EPSILON) * gain


def restore_kernel(
    part_ref, prev_ref, scale_ref, text_ref, q_gain_ref, k_gain_ref, q_ref, kv_ref
):
    q_gain, k_gain = q_gain_ref[...], k_gain_ref[...]

    def total(sources, at):
        acc = part_ref[sources[0], :, at : at + HD].astype(jnp.float32)
        for source in sources[1:]:
            acc = acc + part_ref[source, :, at : at + HD].astype(jnp.float32)
        return acc

    low, high = (0, 1, 2, 3), (4, 5, 6, 7)
    key_places = ((low, 384), (low + high, 512), (high, 384))

    def restored(fresh, kind, head):
        earlier = prev_ref[kind, :, head * HD : head * HD + HD].astype(jnp.float32)
        lane = kind * 3 + head
        scale = scale_ref[:, lane : lane + 1].astype(jnp.float32)
        limit = CODE_LIMIT * scale
        scaled = jnp.clip(fresh - earlier, -limit, limit).astype(jnp.bfloat16).astype(jnp.float32)
        return (earlier + scaled).astype(jnp.bfloat16)

    for head in range(3):
        lanes = slice(head * HD, head * HD + HD)
        q_ref[:, lanes] = rms_scale(total(low, head * HD), q_gain).astype(jnp.bfloat16)
        keys = restored(rms_scale(total(*key_places[head]), k_gain), 0, head)
        values = restored(total(high, head * HD), 1, head)
        for peer in range(8):
            kv_ref[peer, 0:128, lanes] = keys
            kv_ref[peer, 144:272, lanes] = values
    for peer in range(8):
        kv_ref[peer, 128:144, :] = text_ref[0]
        kv_ref[peer, 272:288, :] = text_ref[1]


def split_three(value):
    first = value.astype(jnp.bfloat16)
    rest = value - first.astype(jnp.float32)
    second = rest.astype(jnp.bfloat16)
    third = (rest - second.astype(jnp.float32)).astype(jnp.bfloat16)
    return first, second, third


def attend_kernel(q0_ref, q1_ref, q2_ref, q3_ref, kv_ref, o0_ref, o1_ref, o2_ref, o3_ref):
    factor = LOG2E * HD**-0.5
    lane = lax.broadcasted_iota(jnp.int32, (128, HD), 1)
    stats = [jnp.zeros((128, HD), jnp.float32) for _ in range(4)]
    for head in range(3):
        lanes = slice(head * HD, head * HD + HD)
        keys = kv_ref[:, 0:144, lanes].reshape(1152, HD)
        values = kv_ref[:, 144:288, lanes].reshape(1152, HD)
        for block, (q_ref, o_ref) in enumerate(
            ((q0_ref, o0_ref), (q1_ref, o1_ref), (q2_ref, o2_ref), (q3_ref, o3_ref))
        ):
            logits = lax.dot_general(
                q_ref[:, lanes], keys, (((1,), (1,)), ((), ())), preferred_element_type=jnp.float32
            )
            peak = jnp.max(logits, axis=-1, keepdims=True)
            terms = jnp.exp2((logits - peak) * factor)
            total = jnp.sum(terms, axis=-1, keepdims=True)
            mixed = jnp.dot(terms.astype(jnp.bfloat16), values, preferred_element_type=jnp.float32)
            o_ref[:, lanes] = (mixed / total).astype(jnp.bfloat16)
            for place, part in enumerate(split_three(peak * factor + jnp.log2(total))):
                stats[block] = jnp.where(
                    lane == head * 3 + place, part.astype(jnp.float32), stats[block]
                )
    for block, o_ref in enumerate((o0_ref, o1_ref, o2_ref, o3_ref)):
        o_ref[:, 384:512] = stats[block].astype(jnp.bfloat16)


def output_kernel(p0_ref, p1_ref, p2_ref, p3_ref, weights_ref, out_ref, attended_ref):
    parts = (p0_ref, p1_ref, p2_ref, p3_ref)
    for head in range(3):
        lanes = slice(head * HD, head * HD + HD)
        sizes = []
        for ref in parts:
            stat = ref[:, 384:512].astype(jnp.float32)
            sizes.append(
                stat[:, head * 3 : head * 3 + 1]
                + stat[:, head * 3 + 1 : head * 3 + 2]
                + stat[:, head * 3 + 2 : head * 3 + 3]
            )
        top = jnp.maximum(jnp.maximum(sizes[0], sizes[1]), jnp.maximum(sizes[2], sizes[3]))
        shares = [jnp.exp2(size - top) for size in sizes]
        whole = shares[0] + shares[1] + shares[2] + shares[3]
        mixed = shares[0] * parts[0][:, lanes].astype(jnp.float32)
        for share, ref in zip(shares[1:], parts[1:]):
            mixed = mixed + share * ref[:, lanes].astype(jnp.float32)
        attended_ref[:, lanes] = (mixed / whole).astype(jnp.bfloat16)
    attended = attended_ref[...]
    for block in range(8):
        sums = lax.dot_general(
            attended,
            weights_ref[block],
            (((1,), (1,)), ((), ())),
            preferred_element_type=jnp.float32,
        ).astype(jnp.bfloat16)
        at = (block % 2) * 384
        for y in range(2):
            out_ref[4 * y + block // 2, :, at : at + 384] = sums[y * 64 : y * 64 + 64]


def gate_kernel(parts_ref, gate_ref, out_ref):
    for image in range(2):
        acc = parts_ref[4 * image].astype(jnp.float32)
        for source in range(1, 4):
            acc = acc + parts_ref[4 * image + source].astype(jnp.float32)
        gate = gate_ref[image : image + 1, :].astype(jnp.float32)
        out_ref[image] = (gate * acc).astype(jnp.bfloat16)


def power_two(exponents):
    summed = jnp.zeros(exponents.shape, jnp.float32)
    for exponent in range(-8, 1):
        summed = summed + jnp.where(exponents == exponent, jnp.float32(2.0**exponent), 0.0)
    return summed


def shape(*dims):
    return jax.ShapeDtypeStruct(dims, jnp.bfloat16)


def per_device(
    image_hidden, text_kv, prev_kv, scale_exp, w_qkv, w_out, mod_table, timesteps, q_gain, k_gain
):
    yh, x = lax.axis_index("yh"), lax.axis_index("x")
    z = lax.axis_index(Z)
    lower = yh == 0
    picked = jnp.stack(
        [lax.dynamic_index_in_dim(mod_table, timesteps[image], 0, False) for image in range(2)]
    )

    by_part = jnp.transpose(w_qkv, (1, 0, 2))
    for_low = jnp.concatenate([by_part[0], by_part[1][:, :HD]], axis=1)
    for_high = jnp.concatenate([by_part[2], by_part[1][:, 2 * HD :]], axis=1)
    kept, sent = jnp.where(lower, for_low, for_high), jnp.where(lower, for_high, for_low)
    scales = jnp.transpose(power_two(scale_exp), (1, 2, 0, 3)).reshape(2, 64, 6).astype(jnp.bfloat16)
    scales = jnp.pad(scales, ((0, 0), (0, 0), (0, HD - 6)))
    own_scales = lax.dynamic_index_in_dim(scales, yh, 0, False)
    own_text = lax.dynamic_index_in_dim(text_kv, yh, 1, False)
    far_scales = lax.dynamic_index_in_dim(scales, 1 - yh, 0, False)
    far_text = lax.dynamic_index_in_dim(text_kv, 1 - yh, 1, False)
    package = jnp.concatenate(
        [
            sent,
            jnp.pad(far_text.reshape(16, 384), ((0, 0), (0, HD))),
            jnp.pad(far_scales, ((0, 0), (0, 512 - HD))),
        ],
        axis=0,
    )
    package = lax.ppermute(package, "yh", [(0, 1), (1, 0)])
    received, got_text, got_scales = package[:48], package[48:64, :384], package[64:, :HD]
    both_scales = jnp.where(
        lower,
        jnp.concatenate([own_scales, got_scales]),
        jnp.concatenate([got_scales, own_scales]),
    )
    both_text = jnp.concatenate([own_text, got_text.reshape(2, 8, 384)], axis=1)

    line = jnp.concatenate(
        [kept, received, by_part[1][:, HD : 2 * HD], jnp.transpose(w_out)], axis=1
    )
    weights = lax.all_to_all(jnp.broadcast_to(line, (8, 48, 1536)), Z, 0, 0, tiled=True)

    rows = jnp.concatenate(
        [
            image_hidden.reshape(128, 768),
            picked[:, :2].reshape(4, 768),
            jnp.zeros((12, 768), jnp.bfloat16),
        ],
        axis=0,
    )
    rows = lax.all_gather(rows, H, axis=0)
    normed = call(norm_kernel, shape(8, 128, 768), (rows,))
    normed = lax.all_to_all(normed, YX, 0, 0, tiled=True)

    partial = call(
        project_kernel, shape(8, 128, 640), (normed, weights), flops=2 * 1024 * 768 * 576
    )
    partial = lax.all_to_all(partial, YX, 0, 0, tiled=True)

    w_columns = weights[:, :, 1152:].reshape(384, 384)
    w_columns = lax.all_to_all(jnp.broadcast_to(w_columns, (8, 384, 384)), YX, 0, 0, tiled=True)

    own_prev = lax.dynamic_index_in_dim(prev_kv, yh, 1, False)
    first = (8 * x + z) * 64
    earlier = jnp.concatenate(
        [
            lax.dynamic_slice_in_dim(own_prev, first, 64, 1),
            lax.dynamic_slice_in_dim(own_prev, first + 2048, 64, 1),
        ],
        axis=1,
    )
    queries, kv_pair = call(
        restore_kernel,
        (shape(128, 384), shape(8, 288, 384)),
        (partial, earlier, both_scales, both_text, q_gain.reshape(1, HD), k_gain.reshape(1, HD)),
    )
    far_queries = [
        lax.ppermute(queries, "zo", [(i, (i + k) % 4) for i in range(4)]) for k in (1, 2, 3)
    ]
    kv_pair = lax.all_to_all(kv_pair, ("x", "zi"), 0, 0, tiled=True)
    mixed = call(
        attend_kernel,
        (shape(128, 512),) * 4,
        (queries, *far_queries, kv_pair),
        flops=4 * 512 * 1152 * 384,
    )
    mixed = [mixed[0]] + [
        lax.ppermute(mixed[k], "zo", [(i, (i - k) % 4) for i in range(4)]) for k in (1, 2, 3)
    ]
    products = call(
        output_kernel,
        shape(8, 64, 768),
        (*mixed, w_columns),
        scratch=[pltpu.VMEM((128, 384), jnp.bfloat16)],
        flops=2 * 128 * 384 * 3072,
    )
    products = lax.all_to_all(products, ("yh",) + H, 0, 0, tiled=True)
    return call(gate_kernel, shape(2, 64, 768), (products, picked[:, 2]))


def solution(mesh):
    names = ("yh", "x", "zo", "zi", "yl", "c")
    fine = Mesh(mesh.devices.reshape(2, 4, 4, 2, 2, 2), names)
    patch, head = ("yh", "x", "zo", "zi"), ("yl", "c")
    placed = (
        P(None, patch, head),
        P(None, None, patch, head),
        P(None, None, None, head),
        P(None, None, patch, head),
        P(patch, None, head),
        P(head, patch),
        P(None, None, head),
        P(),
        P(),
        P(),
    )
    return jax.shard_map(
        per_device, mesh=fine, in_specs=placed, out_specs=P(None, patch, head), check_vma=False
    )
```

time: 599 us -> 217 us (0.36)
  waiting for transfers between devices: 269 us -> 76.8 us
  blocking collectives: 182 us -> 48.6 us
  local copies, waits for them, and re-layouts: 94.1 us -> 8.88 us
  starting transfers between devices: 0.16 us -> 48 us
  Pallas kernels: 0 us -> 24.1 us
  other arithmetic: 23.9 us -> 3.64 us
  matrix products: 13.2 us -> 0 us
  between operations: 13.4 us -> 3.97 us
    all_gather x4 -> x0, waiting for transfers between devices: 246 us -> none  [the longest x1 125 us: per_device(): lax.all_gather(w_qkv, 'patch', axis=0, tiled=True)]
    all_gather x3 -> x1, blocking collectives: 182 us -> 10.2 us  [per_device(): rows = lax.all_gather(rows, H, axis=0)]
    reshape x4 -> x2, local copies, waits for them, and re-layouts: 60.5 us -> 0.01 us  [the longest x1 0.01 us: per_device(): picked[:, :2].reshape(4, 768)]
    all_to_all x0 -> x5, waiting for transfers between devices: none -> 48.4 us  [the longest x1 21.2 us: per_device(): kv_pair = lax.all_to_all(kv_pair, ('x', 'zi'), 0, 0, tiled=True)]
    all_to_all x0 -> x1, blocking collectives: none -> 38.5 us  [per_device(): lax.all_to_all(jnp.broadcast_to(line, (8, 48, 1536)), Z, 0, 0, tiled=True)]
    all_to_all x0 -> x5, starting transfers between devices: none -> 34.7 us  [the longest x1 9.37 us: per_device(): kv_pair = lax.all_to_all(kv_pair, ('x', 'zi'), 0, 0, tiled=True)]
    ppermute x0 -> x7, waiting for transfers between devices: none -> 28.5 us  [the longest x1 20.6 us: per_device(): package = lax.ppermute(package, 'yh', [(0, 1), (1, 0)])]
    pallas_call x0 -> x6, Pallas kernels: none -> 24.1 us  [call(): pl.pallas_call(kernel, out_shape=out_shapes, in_specs=[pl.BlockSpec(memor...]
  transfers between devices with their start and end apart: 5 -> 12, of which waited for: 4 -> 10; matrix products, arithmetic and copies ran while one was open for 21% -> 2% of each run, Pallas kernels for 0% -> 3%
where the time goes in v1:
time: 217 us; the launch traced here: 214 us
  waiting for transfers between devices  76.8 us (35%)
  blocking collectives  48.6 us (22%)
  starting transfers between devices  48 us (22%)
  Pallas kernels  24.1 us (11%)
  local copies, waits for them, and re-layouts  8.88 us (4%)
  between operations  3.97 us (2%)
  other arithmetic  3.64 us (2%)
    all_to_all x1, blocking collectives, per_device(): lax.all_to_all(jnp.broadcast_to(line, (8, 48, 1536)), Z, 0, 0, tiled=True)  38.5 us
    pallas_call x6, Pallas kernels, call(): pl.pallas_call(kernel, out_shape=out_shapes, in_specs=[pl.BlockSpec(memor...  24.1 us
    all_to_all x1, waiting for transfers between devices, per_device(): kv_pair = lax.all_to_all(kv_pair, ('x', 'zi'), 0, 0, tiled=True)  21.2 us
    ppermute x1, waiting for transfers between devices, per_device(): package = lax.ppermute(package, 'yh', [(0, 1), (1, 0)])  20.6 us
    all_to_all x1, waiting for transfers between devices, per_device(): products = lax.all_to_all(products, ('yh',) + H, 0, 0, tiled=True)  11.7 us
    all_to_all x1, waiting for transfers between devices, per_device(): partial = lax.all_to_all(partial, YX, 0, 0, tiled=True)  11.5 us
    all_gather x1, blocking collectives, per_device(): rows = lax.all_gather(rows, H, axis=0)  10.2 us
    all_to_all x1, starting transfers between devices, per_device(): kv_pair = lax.all_to_all(kv_pair, ('x', 'zi'), 0, 0, tiled=True)  9.37 us
  transfers between devices with their start and end apart: 12, of which 10 were waited for; matrix products, arithmetic and copies ran while one was open for 2% of the time, Pallas kernels for 3%

profile of v1, /device:TPU:7, one launch (start us, length us, event | category | flops | bytes accessed | tf_op | source)
XLA Modules:
  0.0 214.0 jit_solution(8217147707975048191)
XLA Ops:
  0.0 1.3 fusion.19
  5.1 0.9 constant_dynamic-slice_fusion
  6.1 0.1 pad.36.clone
  6.1 1.0 maximum_maximum_fusion
  7.2 10.2 %all-gather = bf16[576,768]{1,0:T(8,128)(2,1)} all-gather(bf16[144,768]{1,0:T(8,128)(2,1)S(1)} %maximum_maximum_fusion), channel_id=2, replica_groups=mesh['yh'=2,'x'=4,'zo'=4,'zi'=2,'yl'=2,'c'=2] {'yl','c'}, dimensions={0}, use_global_device_ids=true | all-gather | bytes 1105920 | tf_op jit(solution)/shard_map/all_gather | solution.py:242
  17.3 3.0 %shard_map.100 = bf16[8,128,768]{2,1,0:T(8,128)(2,1)} custom-call(bf16[4,144,768]{2,1,0:T(8,128)(2,1)} %bitcast.35), custom_call_target="tpu_custom_call" | custom-call | tf_op jit(solution)/shard_map/pallas_call | solution.py:20
  20.3 0.0 copy-start.11
  20.3 0.0 copy-start.10
  20.4 6.7 %all-to-all-start = ((bf16[8,128,768]{2,1,0:T(8,128)(2,1)}), bf16[8,128,768]{2,1,0:T(8,128)(2,1)S(1)}, u32[]{:S(2)}, u32[]{:S(2)}) async-start(bf16[8,128,768]{2,1,0:T(8,128)(2,1)} %shard_map.100), calls=%async_computation | async-start | bytes 3145728 | tf_op jit(solution)/shard_map/all_to_all | solution.py:244
  27.0 0.0 copy-done.11
  27.1 0.1 copy.13
  27.2 0.0 copy-done.10
  27.3 0.0 copy-done.8
  27.4 2.8 %collective-permute-start = (bf16[128,512]{1,0:T(8,128)(2,1)S(1)}, bf16[128,512]{1,0:T(8,128)(2,1)S(1)}, u32[]{:S(2)}, u32[]{:S(2)}) collective-permute-start(bf16[128,512]{1,0:T(8,128)(2,1)S(1)} %fusion.4), channel_id=1, source_target_pairs={{0,128},{128,0},{1,129},{129,1},{2,130},{130,2},{3,131},{131,3},{4... | collective-permute-start | bytes 393224 | tf_op jit(solution)/shard_map/ppermute | solution.py:220
  30.1 20.6 %collective-permute-done = bf16[128,512]{1,0:T(8,128)(2,1)S(1)} collective-permute-done((bf16[128,512]{1,0:T(8,128)(2,1)S(1)}, bf16[128,512]{1,0:T(8,128)(2,1)S(1)}, u32[]{:S(2)}, u32[]{:S(2)}) %collective-permute-start) | collective-permute-done | bytes 131104 | tf_op jit(solution)/shard_map/ppermute | solution.py:220
  50.8 0.0 copy-done.9
  50.8 0.0 all-to-all-done.rows_ref
  50.8 0.0 copy-start.1
  50.8 0.1 broadcast_in_dim.60
  50.9 38.5 %all_to_all.30.weights_ref = bf16[8,48,1536]{2,1,0:T(8,128)(2,1)} all-to-all(bf16[8,48,1536]{2,1,0:T(8,128)(2,1)S(1)} %broadcast_in_dim.60), channel_id=1, replica_groups=mesh['yh'=2,'x'=4,'zo'=4,'zi'=2,'yl'=2,'c'=2] {'zo','zi'}, dimensions={0} | all-to-all | bytes 2359296 | tf_op jit(solution)/shard_map/all_to_all | solution.py:232
  89.4 0.0 copy-done.1
  89.4 4.3 %shard_map.101 = bf16[8,128,640]{2,1,0:T(8,128)(2,1)} custom-call(bf16[8,128,768]{2,1,0:T(8,128)(2,1)} %copy-done.1, bf16[8,48,1536]{2,1,0:T(8,128)(2,1)} %all_to_all.30.weights_ref), custom_call_target="tpu_custom_call" | custom-call | flops 905969664 | tf_op jit(solution)/shard_map/pallas_call | solution.py:20
  93.6 4.3 %all-to-all-start.2 = ((bf16[8,128,640]{2,1,0:T(8,128)(2,1)}), bf16[8,128,640]{2,1,0:T(8,128)(2,1)S(1)}, u32[]{:S(2)}, u32[]{:S(2)}) async-start(bf16[8,128,640]{2,1,0:T(8,128)(2,1)} %shard_map.101), calls=%async_computation.2 | async-start | bytes 2621440 | tf_op jit(solution)/shard_map/all_to_all | solution.py:249
  97.9 1.0 dynamic-slice_bitcast_fusion.1
  98.9 0.7 pad_maximum_fusion.prev_ref
  99.6 0.6 pad_maximum_fusion.4.text_ref
  100.2 0.6 maximum_select_fusion.scale_ref
  100.8 11.5 %all-to-all-done.2.part_ref = bf16[8,128,640]{2,1,0:T(8,128)(2,1)S(1)} async-done(((bf16[8,128,640]{2,1,0:T(8,128)(2,1)}), bf16[8,128,640]{2,1,0:T(8,128)(2,1)S(1)}, u32[]{:S(2)}, u32[]{:S(2)}) %all-to-all-start.2) | async-done | bytes 1310752 | tf_op jit(solution)/shard_map/all_to_all | solution.py:249
  112.3 1.1 copy-done.2
  113.4 3.2 %shard_map.102 = (bf16[128,384]{1,0:T(8,128)(2,1)}, bf16[8,288,384]{2,1,0:T(8,128)(2,1)}) custom-call(bf16[8,128,640]{2,1,0:T(8,128)(2,1)} %copy-done.2, bf16[2,128,384]{2,1,0:T(8,128)(2,1)} %pad_maximum_fusion.prev_ref, bf16[128,128]{1,0:T(8,128)(2,1)} %maximum_select_fusion.scale_ref, bf16[2,16,384]{2,1,0:T(8,128)(2,1)} %pad_maximum_fusion.4.text_ref, ...), custom_call_target="tpu_custom_call" | custom-call | tf_op jit(solution)/shard_map/pallas_call | solution.py:20
  116.5 9.4 %all-to-all-start.3 = ((bf16[8,288,384]{2,1,0:T(8,128)(2,1)}), bf16[8,288,384]{2,1,0:T(8,128)(2,1)S(1)}, u32[]{:S(2)}, u32[]{:S(2)}) async-start(bf16[8,288,384]{2,1,0:T(8,128)(2,1)} %get-tuple-element.12), calls=%async_computation.3 | async-start | bytes 3538944 | tf_op jit(solution)/shard_map/all_to_all | solution.py:271
  125.9 21.2 %all-to-all-done.3.kv_ref = bf16[8,288,384]{2,1,0:T(8,128)(2,1)S(1)} async-done(((bf16[8,288,384]{2,1,0:T(8,128)(2,1)}), bf16[8,288,384]{2,1,0:T(8,128)(2,1)S(1)}, u32[]{:S(2)}, u32[]{:S(2)}) %all-to-all-start.3) | async-done | bytes 1769504 | tf_op jit(solution)/shard_map/all_to_all | solution.py:271
  147.1 0.0 slice-done
  147.1 1.8 broadcast_in_dim.61
  148.9 0.2 copy-done.4
  149.1 5.0 %all-to-all-start.4 = ((bf16[8,384,384]{2,1,0:T(8,128)(2,1)}), bf16[8,384,384]{2,1,0:T(8,128)(2,1)S(1)}, u32[]{:S(2)}, u32[]{:S(2)}) async-start(bf16[8,384,384]{2,1,0:T(8,128)(2,1)} %broadcast_in_dim.61), calls=%async_computation.4 | async-start | bytes 4718592 | tf_op jit(solution)/shard_map/all_to_all | solution.py:252
  154.1 0.0 copy-done.12
  154.1 1.1 collective-permute-start.3
  155.2 1.7 collective-permute-start.2
  156.9 0.9 collective-permute-start.1
  157.9 2.0 collective-permute-done.3.q3_ref
  159.9 4.1 %collective-permute-done.2.q2_ref = bf16[128,384]{1,0:T(8,128)(2,1)S(1)} collective-permute-done((bf16[128,384]{1,0:T(8,128)(2,1)S(1)}, bf16[128,384]{1,0:T(8,128)(2,1)S(1)}, u32[]{:S(2)}, u32[]{:S(2)}) %collective-permute-start.2) | collective-permute-done | bytes 98336 | tf_op jit(solution)/shard_map/ppermute | solution.py:269
  163.9 0.6 collective-permute-done.1.q1_ref
  164.5 0.0 copy-done.13
  164.5 0.0 copy-done.14
  164.5 0.6 copy-done.15
  165.2 7.4 %shard_map.103 = (bf16[128,512]{1,0:T(8,128)(2,1)}, bf16[128,512]{1,0:T(8,128)(2,1)}, bf16[128,512]{1,0:T(8,128)(2,1)}, bf16[128,512]{1,0:T(8,128)(2,1)}) custom-call(bf16[128,384]{1,0:T(8,128)(2,1)} %get-tuple-element.11.q0_ref, bf16[128,384]{1,0:T(8,128)(2,1)} %copy-done.15, bf16[128,384]{1,0:T(8,128)(2,1)} %copy-done.14, bf16[128,384]{1,0:T(8,128)(2,1)} %copy-done.13, ...), custom_call_target="tpu_custom_call" | custom-call | flops 905969664 | tf_op jit(solution)/shard_map/pallas_call | solution.py:20
  172.6 2.9 %collective-permute-start.4 = (bf16[128,512]{1,0:T(8,128)(2,1)}, bf16[128,512]{1,0:T(8,128)(2,1)S(1)}, u32[]{:S(2)}, u32[]{:S(2)}) collective-permute-start(bf16[128,512]{1,0:T(8,128)(2,1)} %get-tuple-element.14), channel_id=1, source_target_pairs={{0,24},{8,0},{16,8},{24,16},{1,25},{9,1},{17,9},{25,17},{2,26},{10... | collective-permute-start | bytes 393224 | tf_op jit(solution)/shard_map/ppermute | solution.py:279
  175.5 1.6 collective-permute-start.5
  177.1 2.3 %collective-permute-start.6 = (bf16[128,512]{1,0:T(8,128)(2,1)}, bf16[128,512]{1,0:T(8,128)(2,1)S(1)}, u32[]{:S(2)}, u32[]{:S(2)}) collective-permute-start(bf16[128,512]{1,0:T(8,128)(2,1)} %get-tuple-element.16), channel_id=1, source_target_pairs={{0,8},{8,16},{16,24},{24,0},{1,9},{9,17},{17,25},{25,1},{2,10},{10... | collective-permute-start | bytes 393224 | tf_op jit(solution)/shard_map/ppermute | solution.py:279
  179.4 4.0 %all-to-all-done.4.weights_ref = bf16[8,384,384]{2,1,0:T(8,128)(2,1)S(1)} async-done(((bf16[8,384,384]{2,1,0:T(8,128)(2,1)}), bf16[8,384,384]{2,1,0:T(8,128)(2,1)S(1)}, u32[]{:S(2)}, u32[]{:S(2)}) %all-to-all-start.4) | async-done | bytes 2359328 | tf_op jit(solution)/shard_map/all_to_all | solution.py:252
  183.5 0.0 collective-permute-done.4.p1_ref
  183.5 0.1 collective-permute-done.5.p2_ref
  183.6 1.1 collective-permute-done.6.p3_ref
  184.7 0.2 copy-done
  184.9 0.0 copy-done.5
  184.9 0.1 copy-done.6
  185.0 0.3 copy-done.7
  185.3 4.3 %shard_map.104 = bf16[8,64,768]{2,1,0:T(8,128)(2,1)} custom-call(bf16[128,512]{1,0:T(8,128)(2,1)} %get-tuple-element.13.p0_ref, bf16[128,512]{1,0:T(8,128)(2,1)} %copy-done.5, bf16[128,512]{1,0:T(8,128)(2,1)} %copy-done.6, bf16[128,512]{1,0:T(8,128)(2,1)} %copy-done.7, bf16[8,384,384]{2,1,0:T(8,128)(2,1)} %copy-done), custom_call_target="tpu_custom_call" | custom-call | flops 301989888 | tf_op jit(solution)/shard_map/pallas_call | solution.py:20
  189.6 9.3 %all-to-all-start.5 = ((bf16[8,64,768]{2,1,0:T(8,128)(2,1)}), bf16[8,64,768]{2,1,0:T(8,128)(2,1)S(1)}, u32[]{:S(2)}, u32[]{:S(2)}) async-start(bf16[8,64,768]{2,1,0:T(8,128)(2,1)} %shard_map.104), calls=%async_computation.5 | async-start | bytes 1572864 | tf_op jit(solution)/shard_map/all_to_all | solution.py:288
  198.9 0.6 fusion.17.gate_ref
  199.5 11.7 %all-to-all-done.5.parts_ref = bf16[8,64,768]{2,1,0:T(8,128)(2,1)S(1)} async-done(((bf16[8,64,768]{2,1,0:T(8,128)(2,1)}), bf16[8,64,768]{2,1,0:T(8,128)(2,1)S(1)}, u32[]{:S(2)}, u32[]{:S(2)}) %all-to-all-start.5) | async-done | bytes 786464 | tf_op jit(solution)/shard_map/all_to_all | solution.py:288
  211.2 0.9 copy-done.3
  212.1 1.9 shard_map.105
  (29 shorter events, 0.2 us)
Async XLA Ops:
  20.3 6.7 %copy-start.11 = (s32[2,2,64,3]{2,1,3,0:T(2,128)S(1)}, s32[2,2,64,3]{2,1,3,0:T(2,128)}, u32[]{:S(2)}) copy-start(s32[2,2,64,3]{2,1,3,0:T(2,128)} %param.13) | copy-start | bytes 9220
  20.3 6.9 %copy-start.10 = (bf16[2,2,8,384]{3,2,1,0:T(8,128)(2,1)S(1)}, bf16[2,2,8,384]{3,2,1,0:T(8,128)(2,1)}, u32[]{:S(2)}) copy-start(bf16[2,2,8,384]{3,2,1,0:T(8,128)(2,1)} %param.11) | copy-start | bytes 73732
  20.3 6.9 %copy-start.8 = (bf16[48,3,384]{2,0,1:T(8,128)(2,1)S(1)}, bf16[48,3,384]{2,0,1:T(8,128)(2,1)}, u32[]{:S(2)}) copy-start(bf16[48,3,384]{2,0,1:T(8,128)(2,1)} %param.14) | copy-start | bytes 331780
  20.3 30.4 %copy-start.9 = (bf16[384,48]{0,1:T(8,128)(2,1)S(1)}, bf16[384,48]{0,1:T(8,128)(2,1)}, u32[]{:S(2)}) copy-start(bf16[384,48]{0,1:T(8,128)(2,1)} %param.15) | copy-start | bytes 110596
  20.4 30.4 %all-to-all-start = ((bf16[8,128,768]{2,1,0:T(8,128)(2,1)}), bf16[8,128,768]{2,1,0:T(8,128)(2,1)S(1)}, u32[]{:S(2)}, u32[]{:S(2)}) async-start(bf16[8,128,768]{2,1,0:T(8,128)(2,1)} %shard_map.100), calls=%async_computation | async-start | bytes 3145728 | tf_op jit(solution)/shard_map/all_to_all | solution.py:244
  27.4 23.4 %collective-permute-start = (bf16[128,512]{1,0:T(8,128)(2,1)S(1)}, bf16[128,512]{1,0:T(8,128)(2,1)S(1)}, u32[]{:S(2)}, u32[]{:S(2)}) collective-permute-start(bf16[128,512]{1,0:T(8,128)(2,1)S(1)} %fusion.4), channel_id=1, source_target_pairs={{0,128},{128,0},{1,129},{129,1},{2,130},{130,2},{3,131},{131,3},{4... | collective-permute-start | bytes 393224 | tf_op jit(solution)/shard_map/ppermute | solution.py:220
  50.8 38.6 %copy-start.1 = (bf16[8,128,768]{2,1,0:T(8,128)(2,1)}, bf16[8,128,768]{2,1,0:T(8,128)(2,1)S(1)}, u32[]{:S(2)}) copy-start(bf16[8,128,768]{2,1,0:T(8,128)(2,1)S(1)} %all-to-all-done.rows_ref) | copy-start | bytes 4718596
  93.6 18.7 %all-to-all-start.2 = ((bf16[8,128,640]{2,1,0:T(8,128)(2,1)}), bf16[8,128,640]{2,1,0:T(8,128)(2,1)S(1)}, u32[]{:S(2)}, u32[]{:S(2)}) async-start(bf16[8,128,640]{2,1,0:T(8,128)(2,1)} %shard_map.101), calls=%async_computation.2 | async-start | bytes 2621440 | tf_op jit(solution)/shard_map/all_to_all | solution.py:249
  112.3 1.1 copy-start.2
  116.5 30.6 %slice-start = ((bf16[8,48,1536]{2,1,0:T(8,128)(2,1)}), bf16[8,48,384]{2,1,0:T(8,128)(2,1)S(1)}, s32[]{:S(2)}) async-start(bf16[8,48,1536]{2,1,0:T(8,128)(2,1)} %all_to_all.30.weights_ref), calls=%async_computation.6 | async-start | bytes 589824 | tf_op jit(solution)/shard_map/slice | solution.py:251
  116.5 30.5 %all-to-all-start.3 = ((bf16[8,288,384]{2,1,0:T(8,128)(2,1)}), bf16[8,288,384]{2,1,0:T(8,128)(2,1)S(1)}, u32[]{:S(2)}, u32[]{:S(2)}) async-start(bf16[8,288,384]{2,1,0:T(8,128)(2,1)} %get-tuple-element.12), calls=%async_computation.3 | async-start | bytes 3538944 | tf_op jit(solution)/shard_map/all_to_all | solution.py:271
  147.1 2.0 copy-start.4
  148.9 5.3 %copy-start.12 = (bf16[128,384]{1,0:T(8,128)(2,1)S(1)}, bf16[128,384]{1,0:T(8,128)(2,1)}, u32[]{:S(2)}) copy-start(bf16[128,384]{1,0:T(8,128)(2,1)} %get-tuple-element.11.q0_ref) | copy-start | bytes 294916
  149.1 34.3 %all-to-all-start.4 = ((bf16[8,384,384]{2,1,0:T(8,128)(2,1)}), bf16[8,384,384]{2,1,0:T(8,128)(2,1)S(1)}, u32[]{:S(2)}, u32[]{:S(2)}) async-start(bf16[8,384,384]{2,1,0:T(8,128)(2,1)} %broadcast_in_dim.61), calls=%async_computation.4 | async-start | bytes 4718592 | tf_op jit(solution)/shard_map/all_to_all | solution.py:252
  154.1 5.7 %collective-permute-start.3 = (bf16[128,384]{1,0:T(8,128)(2,1)S(1)}, bf16[128,384]{1,0:T(8,128)(2,1)S(1)}, u32[]{:S(2)}, u32[]{:S(2)}) collective-permute-start(bf16[128,384]{1,0:T(8,128)(2,1)S(1)} %copy-done.12), channel_id=1, source_target_pairs={{0,24},{8,0},{16,8},{24,16},{1,25},{9,1},{17,9},{25,17},{2,26},{10... | collective-permute-start | bytes 294920 | tf_op jit(solution)/shard_map/ppermute | solution.py:269
  155.2 8.7 %collective-permute-start.2 = (bf16[128,384]{1,0:T(8,128)(2,1)S(1)}, bf16[128,384]{1,0:T(8,128)(2,1)S(1)}, u32[]{:S(2)}, u32[]{:S(2)}) collective-permute-start(bf16[128,384]{1,0:T(8,128)(2,1)S(1)} %copy-done.12), channel_id=1, source_target_pairs={{0,16},{8,24},{16,0},{24,8},{1,17},{9,25},{17,1},{25,9},{2,18},{10... | collective-permute-start | bytes 294920 | tf_op jit(solution)/shard_map/ppermute | solution.py:269
  156.9 7.6 %collective-permute-start.1 = (bf16[128,384]{1,0:T(8,128)(2,1)S(1)}, bf16[128,384]{1,0:T(8,128)(2,1)S(1)}, u32[]{:S(2)}, u32[]{:S(2)}) collective-permute-start(bf16[128,384]{1,0:T(8,128)(2,1)S(1)} %copy-done.12), channel_id=1, source_target_pairs={{0,8},{8,16},{16,24},{24,0},{1,9},{9,17},{17,25},{25,1},{2,10},{10... | collective-permute-start | bytes 294920 | tf_op jit(solution)/shard_map/ppermute | solution.py:269
  159.8 4.7 %copy-start.13 = (bf16[128,384]{1,0:T(8,128)(2,1)}, bf16[128,384]{1,0:T(8,128)(2,1)S(1)}, u32[]{:S(2)}) copy-start(bf16[128,384]{1,0:T(8,128)(2,1)S(1)} %collective-permute-done.3.q3_ref) | copy-start | bytes 294916
  163.9 0.6 copy-start.14
  164.5 0.6 copy-start.15
  172.6 10.9 %collective-permute-start.4 = (bf16[128,512]{1,0:T(8,128)(2,1)}, bf16[128,512]{1,0:T(8,128)(2,1)S(1)}, u32[]{:S(2)}, u32[]{:S(2)}) collective-permute-start(bf16[128,512]{1,0:T(8,128)(2,1)} %get-tuple-element.14), channel_id=1, source_target_pairs={{0,24},{8,0},{16,8},{24,16},{1,25},{9,1},{17,9},{25,17},{2,26},{10... | collective-permute-start | bytes 393224 | tf_op jit(solution)/shard_map/ppermute | solution.py:279
  175.5 8.0 %collective-permute-start.5 = (bf16[128,512]{1,0:T(8,128)(2,1)}, bf16[128,512]{1,0:T(8,128)(2,1)S(1)}, u32[]{:S(2)}, u32[]{:S(2)}) collective-permute-start(bf16[128,512]{1,0:T(8,128)(2,1)} %get-tuple-element.15), channel_id=1, source_target_pairs={{0,16},{8,24},{16,0},{24,8},{1,17},{9,25},{17,1},{25,9},{2,18},{10... | collective-permute-start | bytes 393224 | tf_op jit(solution)/shard_map/ppermute | solution.py:279
  177.1 7.6 %collective-permute-start.6 = (bf16[128,512]{1,0:T(8,128)(2,1)}, bf16[128,512]{1,0:T(8,128)(2,1)S(1)}, u32[]{:S(2)}, u32[]{:S(2)}) collective-permute-start(bf16[128,512]{1,0:T(8,128)(2,1)} %get-tuple-element.16), channel_id=1, source_target_pairs={{0,8},{8,16},{16,24},{24,0},{1,9},{9,17},{17,25},{25,1},{2,10},{10... | collective-permute-start | bytes 393224 | tf_op jit(solution)/shard_map/ppermute | solution.py:279
  183.5 1.4 copy-start
  183.5 1.5 copy-start.5
  183.6 1.4 copy-start.6
  184.7 0.6 copy-start.7
  189.6 21.6 %all-to-all-start.5 = ((bf16[8,64,768]{2,1,0:T(8,128)(2,1)}), bf16[8,64,768]{2,1,0:T(8,128)(2,1)S(1)}, u32[]{:S(2)}, u32[]{:S(2)}) async-start(bf16[8,64,768]{2,1,0:T(8,128)(2,1)} %shard_map.104), calls=%async_computation.5 | async-start | bytes 1572864 | tf_op jit(solution)/shard_map/all_to_all | solution.py:288
  211.2 0.9 copy-start.3

commit v2 on v1

v2 whole, which is shorter than its diff:
```python
import jax
import jax.numpy as jnp
from jax import lax
from jax.experimental import pallas as pl
from jax.experimental.pallas import tpu as pltpu
from jax.sharding import Mesh, PartitionSpec as P

HD = 128
EPSILON = 1e-06
CODE_LIMIT = 448.0
LOG2E = 1.4426950408889634
VMEM_BYTES = 16 * 1024 * 1024

YX = ("yh", "x")
Z = ("zo", "zi")
H = ("yl", "c")


def call(kernel, out_shapes, operands, scratch=(), scalars=(), flops=0, limit=VMEM_BYTES):
    return pl.pallas_call(
        kernel,
        out_shape=out_shapes,
        in_specs=[
            pl.BlockSpec(memory_space=pltpu.SMEM if at in scalars else pltpu.VMEM)
            for at in range(len(operands))
        ],
        out_specs=jax.tree.map(lambda _: pl.BlockSpec(memory_space=pltpu.VMEM), out_shapes),
        scratch_shapes=scratch,
        compiler_params=pltpu.CompilerParams(vmem_limit_bytes=limit),
        cost_estimate=pl.CostEstimate(flops=flops, bytes_accessed=0, transcendentals=0),
    )(*operands)


def pack_kernel(hidden_ref, table_ref, steps_ref, rows_ref, gate_ref):
    rows_ref[0:128, :] = hidden_ref[...]
    plan = table_ref.shape[1]
    point = lax.broadcasted_iota(jnp.int32, (plan, 768), 0)
    row = lax.broadcasted_iota(jnp.int32, (16, 768), 0)
    modulation = jnp.zeros((16, 768), jnp.float32)
    gates = jnp.zeros((16, 768), jnp.float32)
    for image in range(2):
        chosen = point == steps_ref[image]
        for part in range(3):
            line = jnp.sum(
                jnp.where(chosen, table_ref[part].astype(jnp.float32), 0.0), axis=0, keepdims=True
            )
            if part < 2:
                modulation = jnp.where(row == 2 * image + part, line, modulation)
            else:
                gates = jnp.where(row == image, line, gates)
    rows_ref[128:144, :] = modulation.astype(jnp.bfloat16)
    gate_ref[...] = gates


def norm_kernel(rows_ref, out_ref):
    features = 4 * 768
    for image in range(2):
        shift = rows_ref[:, 128 + 2 * image : 129 + 2 * image, :].astype(jnp.float32)
        scale = 1.0 + rows_ref[:, 129 + 2 * image : 130 + 2 * image, :].astype(jnp.float32)
        for start in range(0, 64, 16):
            at = image * 64 + start
            hidden = rows_ref[:, at : at + 16, :].astype(jnp.float32)
            centre = jnp.sum(jnp.sum(hidden, axis=0), axis=-1, keepdims=True) / features
            off = hidden - centre[None]
            variance = jnp.sum(jnp.sum(off * off, axis=0), axis=-1, keepdims=True) / features
            normed = (off * lax.rsqrt(variance + EPSILON)[None] * scale + shift).astype(jnp.bfloat16)
            for y in range(2):
                for x in range(4):
                    for place, block in enumerate((4 * y + x, 4 * (1 - y) + x)):
                        piece = normed[block // 2][:, (block % 2) * 384 : (block % 2) * 384 + 384]
                        out_ref[4 * y + x, at : at + 16, place * 384 : place * 384 + 384] = piece


def project_kernel(rows_ref, weights_ref, out_ref, columns_ref):
    weights = weights_ref[...].reshape(384, 1536)
    columns_ref[...] = weights[:, 1152:]
    for x in range(4):
        rows = jnp.concatenate([rows_ref[x], rows_ref[4 + x]], axis=0)
        own, other = rows[:, :384], rows[:, 384:]
        most = jnp.dot(own, weights[:, :512], preferred_element_type=jnp.float32) + jnp.dot(
            other, weights[:, 512:1024], preferred_element_type=jnp.float32
        )
        rest = jnp.dot(own, weights[:, 1024:1152], preferred_element_type=jnp.float32)
        both = jnp.concatenate([most, rest], axis=1).astype(jnp.bfloat16)
        for image in range(2):
            for y in range(2):
                piece = both[y * 128 + image * 64 : y * 128 + image * 64 + 64]
                out_ref[4 * image + x, y * 64 : y * 64 + 64, :] = piece


def rms_scale(vectors, gain):
    return vectors * lax.rsqrt(jnp.mean(vectors * vectors, axis=-1, keepdims=True) + EPSILON) * gain


def summed(part_ref, sources, at):
    acc = part_ref[sources[0], :, at : at + HD].astype(jnp.float32)
    for source in sources[1:]:
        acc = acc + part_ref[source, :, at : at + HD].astype(jnp.float32)
    return acc


LOW, HIGH = (0, 1, 2, 3), (4, 5, 6, 7)


def query_kernel(part_ref, q_gain_ref, q_ref):
    for head in range(3):
        lanes = slice(head * HD, head * HD + HD)
        q_ref[:, lanes] = rms_scale(summed(part_ref, LOW, head * HD), q_gain_ref[...]).astype(
            jnp.bfloat16
        )


def restore_kernel(part_ref, prev_ref, kept_ref, got_ref, k_gain_ref, y_ref, kv_ref):
    lower = y_ref[0] == 0
    key_places = ((LOW, 384), (LOW + HIGH, 512), (HIGH, 384))
    kept, got = (ref[16:80, 0:HD].astype(jnp.float32) for ref in (kept_ref, got_ref))
    scales = jnp.concatenate([jnp.where(lower, kept, got), jnp.where(lower, got, kept)], axis=0)

    def restored(fresh, kind, head):
        earlier = prev_ref[kind, :, head * HD : head * HD + HD].astype(jnp.float32)
        lane = kind * 3 + head
        scale = scales[:, lane : lane + 1]
        limit = CODE_LIMIT * scale
        scaled = jnp.clip(fresh - earlier, -limit, limit).astype(jnp.bfloat16).astype(jnp.float32)
        return (earlier + scaled).astype(jnp.bfloat16)

    for head in range(3):
        lanes = slice(head * HD, head * HD + HD)
        keys = restored(rms_scale(summed(part_ref, *key_places[head]), k_gain_ref[...]), 0, head)
        values = restored(summed(part_ref, HIGH, head * HD), 1, head)
        for peer in range(8):
            kv_ref[peer, 0:128, lanes] = keys
            kv_ref[peer, 144:272, lanes] = values
    own, far = (ref[0:16, :].astype(jnp.float32) for ref in (kept_ref, got_ref))
    for kind in range(2):
        text = jnp.concatenate([own[8 * kind : 8 * kind + 8], far[8 * kind : 8 * kind + 8]], axis=0)
        text = text.astype(jnp.bfloat16)
        for peer in range(8):
            kv_ref[peer, 128 + 144 * kind : 144 + 144 * kind, :] = text


def split_three(value):
    first = value.astype(jnp.bfloat16)
    rest = value - first.astype(jnp.float32)
    second = rest.astype(jnp.bfloat16)
    third = (rest - second.astype(jnp.float32)).astype(jnp.bfloat16)
    return first, second, third


def attend_kernel(q0_ref, q1_ref, q2_ref, q3_ref, kv_ref, o0_ref, o1_ref, o2_ref, o3_ref):
    factor = LOG2E * HD**-0.5
    lane = lax.broadcasted_iota(jnp.int32, (128, HD), 1)
    stats = [jnp.zeros((128, HD), jnp.float32) for _ in range(4)]
    for head in range(3):
        lanes = slice(head * HD, head * HD + HD)
        keys = kv_ref[:, 0:144, lanes].reshape(1152, HD)
        values = kv_ref[:, 144:288, lanes].reshape(1152, HD)
        for block, (q_ref, o_ref) in enumerate(
            ((q0_ref, o0_ref), (q1_ref, o1_ref), (q2_ref, o2_ref), (q3_ref, o3_ref))
        ):
            logits = lax.dot_general(
                q_ref[:, lanes], keys, (((1,), (1,)), ((), ())), preferred_element_type=jnp.float32
            )
            peak = jnp.max(logits, axis=-1, keepdims=True)
            terms = jnp.exp2((logits - peak) * factor)
            total = jnp.sum(terms, axis=-1, keepdims=True)
            mixed = jnp.dot(terms.astype(jnp.bfloat16), values, preferred_element_type=jnp.float32)
            o_ref[:, lanes] = (mixed / total).astype(jnp.bfloat16)
            for place, part in enumerate(split_three(peak * factor + jnp.log2(total))):
                stats[block] = jnp.where(
                    lane == head * 3 + place, part.astype(jnp.float32), stats[block]
                )
    for block, o_ref in enumerate((o0_ref, o1_ref, o2_ref, o3_ref)):
        o_ref[:, 384:512] = stats[block].astype(jnp.bfloat16)


def combine_kernel(p0_ref, p1_ref, p2_ref, p3_ref, y_ref, kept_ref, sent_ref):
    parts = (p0_ref, p1_ref, p2_ref, p3_ref)
    lower = y_ref[0] == 0
    stats = [ref[:, 384:512].astype(jnp.float32) for ref in parts]
    for head in range(3):
        lanes = slice(head * HD, head * HD + HD)
        sizes = [
            stat[:, head * 3 : head * 3 + 1]
            + stat[:, head * 3 + 1 : head * 3 + 2]
            + stat[:, head * 3 + 2 : head * 3 + 3]
            for stat in stats
        ]
        top = jnp.maximum(jnp.maximum(sizes[0], sizes[1]), jnp.maximum(sizes[2], sizes[3]))
        shares = [jnp.exp2(size - top) for size in sizes]
        whole = shares[0] + shares[1] + shares[2] + shares[3]
        mixed = shares[0] * parts[0][:, lanes].astype(jnp.float32)
        for share, ref in zip(shares[1:], parts[1:]):
            mixed = mixed + share * ref[:, lanes].astype(jnp.float32)
        mixed = (mixed / whole).astype(jnp.bfloat16)
        kept_ref[:, lanes] = jnp.where(lower, mixed[:64], mixed[64:])
        sent_ref[:, lanes] = jnp.where(lower, mixed[64:], mixed[:64])


def output_kernel(attended_ref, weights_ref, gate_ref, out_ref):
    for half in range(2):
        lanes = slice(half * 384, half * 384 + 384)
        sums = jnp.zeros((128, 384), jnp.float32)
        for group in range(4):
            sums = sums + lax.dot_general(
                attended_ref[group],
                weights_ref[half, group],
                (((1,), (1,)), ((), ())),
                preferred_element_type=jnp.float32,
            )
        for image in range(2):
            rows = gate_ref[image : image + 1, lanes] * sums[64 * image : 64 * image + 64]
            out_ref[image, :, lanes] = rows.astype(jnp.bfloat16)


def power_two(exponents):
    summed = jnp.zeros(exponents.shape, jnp.float32)
    for exponent in range(-8, 1):
        summed = summed + jnp.where(exponents == exponent, jnp.float32(2.0**exponent), 0.0)
    return summed


def shape(*dims):
    return jax.ShapeDtypeStruct(dims, jnp.bfloat16)


def column_moves():
    moves = []
    for y in range(2):
        for x in range(4):
            for head in range(4):
                moves.append(((y * 4 + x) * 4 + head, ((x % 2) * 4 + head) * 4 + 2 * y + x // 2))
    return moves


def per_device(
    image_hidden, text_kv, prev_kv, scale_exp, w_qkv, w_out, mod_table, timesteps, q_gain, k_gain
):
    yh, x = lax.axis_index("yh"), lax.axis_index("x")
    z = lax.axis_index(Z)
    lower = yh == 0
    y_at = yh.reshape(1)
    by_part = jnp.transpose(w_qkv, (1, 0, 2))
    for_low = jnp.concatenate([by_part[0], by_part[1][:, :HD]], axis=1)
    for_high = jnp.concatenate([by_part[2], by_part[1][:, 2 * HD :]], axis=1)
    kept, sent = jnp.where(lower, for_low, for_high), jnp.where(lower, for_high, for_low)
    swap = [(0, 1), (1, 0)]
    got = lax.ppermute(sent, "yh", swap)
    columns = lax.ppermute(jnp.transpose(w_out), ("yh", "x") + H, column_moves())

    rows, gates = call(
        pack_kernel,
        (shape(144, 768), jax.ShapeDtypeStruct((16, 768), jnp.float32)),
        (image_hidden.reshape(128, 768), jnp.transpose(mod_table, (1, 0, 2)), timesteps),
        scalars=(2,),
        limit=4 * VMEM_BYTES - 8 * 1024 * 1024,
    )

    line = jnp.concatenate([kept, got, by_part[1][:, HD : 2 * HD], columns], axis=1)
    line, rows = lax.optimization_barrier((line, rows))
    weights = lax.all_gather(line, Z, axis=0)

    scales = jnp.transpose(power_two(scale_exp), (1, 2, 0, 3)).reshape(2, 64, 6).astype(jnp.bfloat16)
    scales = jnp.pad(scales, ((0, 0), (0, 0), (0, 384 - 6)))
    text = jnp.transpose(text_kv, (1, 0, 2, 3)).reshape(2, 16, 384)
    package = jnp.concatenate([text, scales], axis=1)
    own_package = jnp.where(lower, package[0], package[1])
    far_package = lax.ppermute(jnp.where(lower, package[1], package[0]), "yh", swap)

    rows = lax.all_gather(rows, H, axis=0)
    rows, far_package = lax.optimization_barrier((rows, far_package))
    normed = call(norm_kernel, shape(8, 128, 768), (rows,))
    normed = lax.all_to_all(normed, YX, 0, 0, tiled=True)

    partial, columns = call(
        project_kernel,
        (shape(8, 128, 640), shape(384, 384)),
        (normed, weights),
        flops=2 * 1024 * 768 * 576,
    )
    partial = lax.all_to_all(partial, YX, 0, 0, tiled=True)
    columns = lax.all_gather(columns, YX, axis=0)

    own_prev = lax.dynamic_index_in_dim(prev_kv, yh, 1, False)
    first = (8 * x + z) * 64
    earlier = jnp.concatenate(
        [
            lax.dynamic_slice_in_dim(own_prev, first, 64, 1),
            lax.dynamic_slice_in_dim(own_prev, first + 2048, 64, 1),
        ],
        axis=1,
    )
    queries = call(query_kernel, shape(128, 384), (partial, q_gain.reshape(1, HD)))
    far_queries = [
        lax.ppermute(queries, "zo", [(i, (i + k) % 4) for i in range(4)]) for k in (1, 2, 3)
    ]
    kv_pair = call(
        restore_kernel,
        shape(8, 288, 384),
        (partial, earlier, own_package, far_package, k_gain.reshape(1, HD), y_at),
        scalars=(5,),
    )
    kv_pair = lax.all_to_all(kv_pair, ("x", "zi"), 0, 0, tiled=True)
    mixed = call(
        attend_kernel,
        (shape(128, 512),) * 4,
        (queries, *far_queries, kv_pair),
        flops=4 * 512 * 1152 * 384,
    )
    mixed = [mixed[0]] + [
        lax.ppermute(mixed[k], "zo", [(i, (i - k) % 4) for i in range(4)]) for k in (1, 2, 3)
    ]
    own, far = call(combine_kernel, (shape(64, 384),) * 2, (*mixed, y_at), scalars=(4,))
    far = lax.ppermute(far, "yh", [(0, 1), (1, 0)])
    attended = jnp.where(lower, jnp.concatenate([own, far]), jnp.concatenate([far, own]))
    attended = lax.all_gather(attended, H, axis=0)
    return call(
        output_kernel,
        shape(2, 64, 768),
        (attended, columns.reshape(2, 4, 384, 384), gates),
        flops=2 * 128 * 1536 * 768,
    )


def solution(mesh):
    names = ("yh", "x", "zo", "zi", "yl", "c")
    fine = Mesh(mesh.devices.reshape(2, 4, 4, 2, 2, 2), names)
    patch, head = ("yh", "x", "zo", "zi"), ("yl", "c")
    placed = (
        P(None, patch, head),
        P(None, None, patch, head),
        P(None, None, None, head),
        P(None, None, patch, head),
        P(patch, None, head),
        P(head, patch),
        P(None, None, head),
        P(),
        P(),
        P(),
    )
    return jax.shard_map(
        per_device, mesh=fine, in_specs=placed, out_specs=P(None, patch, head), check_vma=False
    )
```

time: 217 us -> 173 us (0.80)
  waiting for transfers between devices: 76.8 us -> 52.1 us
  Pallas kernels: 24.1 us -> 14 us
  between operations: 3.97 us -> 13.5 us
  starting transfers between devices: 48 us -> 39.9 us
  local copies, waits for them, and re-layouts: 8.88 us -> 4.93 us
  blocking collectives: 48.6 us -> 44.9 us
    all_to_all x1, waiting for transfers between devices: 21.2 us -> 0.01 us  [per_device(): kv_pair = lax.all_to_all(kv_pair, ('x', 'zi'), 0, 0, tiled=True)]
    all_to_all x3 -> x0, starting transfers between devices: 21.1 us -> none  [the longest x1 9.33 us: per_device(): products = lax.all_to_all(products, ('yh',) + H, 0, 0, tiled=True)]
    ppermute x3, waiting for transfers between devices: 6.63 us -> 22.7 us  [per_device(): lax.ppermute(queries, 'zo', [(i, (i + k) % 4) for i in range(4)])]
    all_to_all x3 -> x0, waiting for transfers between devices: 15.7 us -> none  [the longest x1 11.7 us: per_device(): products = lax.all_to_all(products, ('yh',) + H, 0, 0, tiled=True)]
    ppermute x1 -> x4, waiting for transfers between devices: 20.6 us -> 5.91 us  [the longest x1 3.59 us: per_device(): far = lax.ppermute(far, 'yh', [(0, 1), (1, 0)])]
    all_to_all x1, blocking collectives: 38.5 us -> 25.4 us  [per_device(): normed = lax.all_to_all(normed, YX, 0, 0, tiled=True)]
    pallas_call x6 -> x8, Pallas kernels: 24.1 us -> 14 us  [call(): pl.pallas_call(kernel, out_shape=out_shapes, in_specs=[pl.BlockSpec(memor...]
    all_gather x0 -> x1, blocking collectives: none -> 9.98 us  [per_device(): attended = lax.all_gather(attended, H, axis=0)]
  transfers between devices with their start and end apart: 12 -> 14, of which waited for: 10 -> 8; matrix products, arithmetic and copies ran while one was open for 2% -> 2% of each run, Pallas kernels for 3% -> 6%
where the time goes in v2:
time: 173 us; the launch traced here: 171 us
  waiting for transfers between devices  52.1 us (30%)
  blocking collectives  44.9 us (26%)
  starting transfers between devices  39.9 us (23%)
  Pallas kernels  14 us (8%)
  between operations  13.5 us (8%)
  local copies, waits for them, and re-layouts  4.93 us (3%)
    all_to_all x1, blocking collectives, per_device(): normed = lax.all_to_all(normed, YX, 0, 0, tiled=True)  25.4 us
    ppermute x3, waiting for transfers between devices, per_device(): lax.ppermute(queries, 'zo', [(i, (i + k) % 4) for i in range(4)])  22.7 us
    pallas_call x8, Pallas kernels, call(): pl.pallas_call(kernel, out_shape=out_shapes, in_specs=[pl.BlockSpec(memor...  14 us
    all_to_all x1, waiting for transfers between devices, per_device(): partial = lax.all_to_all(partial, YX, 0, 0, tiled=True)  12.5 us
    ppermute x3, starting transfers between devices, per_device(): lax.ppermute(queries, 'zo', [(i, (i + k) % 4) for i in range(4)])  10.6 us
    ppermute x3, waiting for transfers between devices, per_device(): lax.ppermute(mixed[k], 'zo', [(i, (i - k) % 4) for i in range(4)])  10.3 us
    all_gather x1, blocking collectives, per_device(): attended = lax.all_gather(attended, H, axis=0)  9.98 us
    all_gather x1, blocking collectives, per_device(): rows = lax.all_gather(rows, H, axis=0)  9.45 us
  transfers between devices with their start and end apart: 14, of which 8 were waited for; matrix products, arithmetic and copies ran while one was open for 2% of the time, Pallas kernels for 6%

profile of v2, /device:TPU:7, one launch (start us, length us, event | category | flops | bytes accessed | tf_op | source)
XLA Modules:
  0.0 170.8 jit_solution(8861165064748424135)
XLA Ops:
  6.5 0.0 copy-start
  6.5 0.0 all-gather.6.cloned.1.call-start
  6.5 5.8 %collective-permute-start.1 = (bf16[48,384]{1,0:T(8,128)(2,1)}, bf16[48,384]{1,0:T(8,128)(2,1)S(1)}, u32[]{:S(2)}, u32[]{:S(2)}) collective-permute-start(bf16[48,384]{1,0:T(8,128)(2,1)} %bitcast.45), channel_id=1, source_target_pairs={{0,0},{1,32},{2,64},{3,96},{32,128},{33,160},{34,192},{35,224},{64... | collective-permute-start | bytes 110600 | tf_op jit(solution)/shard_map/ppermute | solution.py:249
  12.3 0.8 slice_bitcast_fusion.2
  13.2 1.1 collective-permute-start
  14.3 0.0 copy-done
  14.3 1.8 %shard_map.100 = (bf16[144,768]{1,0:T(8,128)(2,1)}, f32[16,768]{1,0:T(8,128)}) custom-call(bf16[128,768]{1,0:T(8,128)(2,1)} %bitcast.40, bf16[3,28,768]{2,1,0:T(8,128)(2,1)} %bitcast.41, s32[2]{0:T(128)} %steps_ref.1), custom_call_target="tpu_custom_call" | custom-call | tf_op jit(solution)/shard_map/pallas_call | solution.py:20
  16.1 0.0 collective-permute-done.1
  16.1 2.3 %collective-permute-done = bf16[48,512]{1,0:T(8,128)(2,1)S(1)} collective-permute-done((bf16[48,512]{1,0:T(8,128)(2,1)S(1)}, bf16[48,512]{1,0:T(8,128)(2,1)S(1)}, u32[]{:S(2)}, u32[]{:S(2)}) %collective-permute-start) | collective-permute-done | bytes 49184 | tf_op jit(solution)/shard_map/ppermute | solution.py:248
  18.4 0.7 pad_maximum_fusion.1
  19.1 0.0 all-gather.6.cloned.1.call-update
  19.1 0.7 fusion.10
  19.8 0.1 copy.16
  20.0 1.1 collective-permute-start.2
  21.1 9.5 %all-gather = bf16[576,768]{1,0:T(8,128)(2,1)S(1)} all-gather(bf16[144,768]{1,0:T(8,128)(2,1)} %get-tuple-element.20), channel_id=2, replica_groups=mesh['yh'=2,'x'=4,'zo'=4,'zi'=2,'yl'=2,'c'=2] {'yl','c'}, dimensions={0}, use_global_device_ids=true | all-gather | bytes 1105920 | tf_op jit(solution)/shard_map/all_gather | solution.py:270
  30.5 0.0 collective-permute-done.2.got_ref
  30.6 0.7 shard_map.101
  31.2 25.4 %all_to_all.15.rows_ref = bf16[8,128,768]{2,1,0:T(8,128)(2,1)S(1)} all-to-all(bf16[8,128,768]{2,1,0:T(8,128)(2,1)S(1)} %shard_map.101), channel_id=1, replica_groups=mesh['yh'=2,'x'=4,'zo'=4,'zi'=2,'yl'=2,'c'=2] {'yh','x'}, dimensions={0} | all-to-all | bytes 3145728 | tf_op jit(solution)/shard_map/all_to_all | solution.py:273
  56.7 0.0 all-gather.6.cloned.1.call-done
  56.7 0.0 copy-start.5
  56.7 1.3 copy-done.5
  57.9 2.5 %shard_map.102 = (bf16[8,128,640]{2,1,0:T(8,128)(2,1)}, bf16[384,384]{1,0:T(8,128)(2,1)}) custom-call(bf16[8,128,768]{2,1,0:T(8,128)(2,1)S(1)} %all_to_all.15.rows_ref, bf16[8,48,1536]{2,1,0:T(8,128)(2,1)S(1)} %bitcast.39), custom_call_target="tpu_custom_call" | custom-call | flops 905969664 | tf_op jit(solution)/shard_map/pallas_call | solution.py:20
  60.5 0.0 copy-start.4
  60.5 6.6 %all-to-all-start.1 = ((bf16[8,128,640]{2,1,0:T(8,128)(2,1)}), bf16[8,128,640]{2,1,0:T(8,128)(2,1)S(1)}, u32[]{:S(2)}, u32[]{:S(2)}) async-start(bf16[8,128,640]{2,1,0:T(8,128)(2,1)} %get-tuple-element.23), calls=%async_computation.1 | async-start | bytes 2621440 | tf_op jit(solution)/shard_map/all_to_all | solution.py:281
  67.0 0.0 all-gather.8.cloned.1.call-start
  67.1 0.7 all-gather.8.cloned.1.call-update
  67.8 1.0 dynamic-slice_bitcast_fusion.1
  68.9 12.5 %all-to-all-done.1.part_ref = bf16[8,128,640]{2,1,0:T(8,128)(2,1)S(1)} async-done(((bf16[8,128,640]{2,1,0:T(8,128)(2,1)}), bf16[8,128,640]{2,1,0:T(8,128)(2,1)S(1)}, u32[]{:S(2)}, u32[]{:S(2)}) %all-to-all-start.1) | async-done | bytes 1310752 | tf_op jit(solution)/shard_map/all_to_all | solution.py:281
  81.4 0.0 copy-done.4
  81.4 1.7 shard_map.104
  83.1 0.0 copy-start.3
  83.1 9.4 %all-to-all-start.2 = ((bf16[8,288,384]{2,1,0:T(8,128)(2,1)}), bf16[8,288,384]{2,1,0:T(8,128)(2,1)S(1)}, u32[]{:S(2)}, u32[]{:S(2)}) async-start(bf16[8,288,384]{2,1,0:T(8,128)(2,1)} %shard_map.104), calls=%async_computation.2 | async-start | bytes 3538944 | tf_op jit(solution)/shard_map/all_to_all | solution.py:303
  92.5 0.0 copy-done.3
  92.5 0.1 shard_map.103.q0_ref
  92.6 0.0 copy-start.2
  92.6 3.1 %collective-permute-start.3 = (bf16[128,384]{1,0:T(8,128)(2,1)S(1)}, bf16[128,384]{1,0:T(8,128)(2,1)S(1)}, u32[]{:S(2)}, u32[]{:S(2)}) collective-permute-start(bf16[128,384]{1,0:T(8,128)(2,1)S(1)} %shard_map.103.q0_ref), channel_id=1, source_target_pairs={{0,8},{8,16},{16,24},{24,0},{1,9},{9,17},{17,25},{25,1},{2,10},{10... | collective-permute-start | bytes 294920 | tf_op jit(solution)/shard_map/ppermute | solution.py:295
  95.8 5.1 %collective-permute-start.4 = (bf16[128,384]{1,0:T(8,128)(2,1)S(1)}, bf16[128,384]{1,0:T(8,128)(2,1)S(1)}, u32[]{:S(2)}, u32[]{:S(2)}) collective-permute-start(bf16[128,384]{1,0:T(8,128)(2,1)S(1)} %shard_map.103.q0_ref), channel_id=1, source_target_pairs={{0,16},{8,24},{16,0},{24,8},{1,17},{9,25},{17,1},{25,9},{2,18},{10... | collective-permute-start | bytes 294920 | tf_op jit(solution)/shard_map/ppermute | solution.py:295
  100.9 2.4 %collective-permute-start.5 = (bf16[128,384]{1,0:T(8,128)(2,1)S(1)}, bf16[128,384]{1,0:T(8,128)(2,1)S(1)}, u32[]{:S(2)}, u32[]{:S(2)}) collective-permute-start(bf16[128,384]{1,0:T(8,128)(2,1)S(1)} %shard_map.103.q0_ref), channel_id=1, source_target_pairs={{0,24},{8,0},{16,8},{24,16},{1,25},{9,1},{17,9},{25,17},{2,26},{10... | collective-permute-start | bytes 294920 | tf_op jit(solution)/shard_map/ppermute | solution.py:295
  103.3 18.7 %collective-permute-done.3.q1_ref = bf16[128,384]{1,0:T(8,128)(2,1)S(1)} collective-permute-done((bf16[128,384]{1,0:T(8,128)(2,1)S(1)}, bf16[128,384]{1,0:T(8,128)(2,1)S(1)}, u32[]{:S(2)}, u32[]{:S(2)}) %collective-permute-start.3) | collective-permute-done | bytes 98336 | tf_op jit(solution)/shard_map/ppermute | solution.py:295
  122.0 4.0 %collective-permute-done.4.q2_ref = bf16[128,384]{1,0:T(8,128)(2,1)S(1)} collective-permute-done((bf16[128,384]{1,0:T(8,128)(2,1)S(1)}, bf16[128,384]{1,0:T(8,128)(2,1)S(1)}, u32[]{:S(2)}, u32[]{:S(2)}) %collective-permute-start.4) | collective-permute-done | bytes 98336 | tf_op jit(solution)/shard_map/ppermute | solution.py:295
  125.9 0.0 collective-permute-done.5.q3_ref
  126.0 0.0 all-to-all-done.2.kv_ref
  126.0 5.1 %shard_map.105 = (bf16[128,512]{1,0:T(8,128)(2,1)S(1)}, bf16[128,512]{1,0:T(8,128)(2,1)S(1)}, bf16[128,512]{1,0:T(8,128)(2,1)S(1)}, bf16[128,512]{1,0:T(8,128)(2,1)S(1)}) custom-call(bf16[128,384]{1,0:T(8,128)(2,1)S(1)} %shard_map.103.q0_ref, bf16[128,384]{1,0:T(8,128)(2,1)S(1)} %collective-permute-done.3.q1_ref, ...), custom_call_target="tpu_custom_call" | custom-call | flops 905969664 | tf_op jit(solution)/shard_map/pallas_call | solution.py:20
  131.0 0.4 collective-permute-start.6
  131.4 4.0 %collective-permute-start.7 = (bf16[128,512]{1,0:T(8,128)(2,1)S(1)}, bf16[128,512]{1,0:T(8,128)(2,1)S(1)}, u32[]{:S(2)}, u32[]{:S(2)}) collective-permute-start(bf16[128,512]{1,0:T(8,128)(2,1)S(1)} %get-tuple-element.27), channel_id=1, source_target_pairs={{0,16},{8,24},{16,0},{24,8},{1,17},{9,25},{17,1},{25,9},{2,18},{10... | collective-permute-start | bytes 393224 | tf_op jit(solution)/shard_map/ppermute | solution.py:311
  135.4 0.0 collective-permute-start.8
  135.4 0.8 collective-permute-done.6.p1_ref
  136.2 6.0 %collective-permute-done.7.p2_ref = bf16[128,512]{1,0:T(8,128)(2,1)S(1)} collective-permute-done((bf16[128,512]{1,0:T(8,128)(2,1)S(1)}, bf16[128,512]{1,0:T(8,128)(2,1)S(1)}, u32[]{:S(2)}, u32[]{:S(2)}) %collective-permute-start.7) | collective-permute-done | bytes 131104 | tf_op jit(solution)/shard_map/ppermute | solution.py:311
  142.2 3.5 %collective-permute-done.8.p3_ref = bf16[128,512]{1,0:T(8,128)(2,1)S(1)} collective-permute-done((bf16[128,512]{1,0:T(8,128)(2,1)S(1)}, bf16[128,512]{1,0:T(8,128)(2,1)S(1)}, u32[]{:S(2)}, u32[]{:S(2)}) %collective-permute-start.8) | collective-permute-done | bytes 131104 | tf_op jit(solution)/shard_map/ppermute | solution.py:311
  145.7 0.5 shard_map.106
  146.2 0.9 collective-permute-start.9
  147.1 3.6 %collective-permute-done.9 = bf16[64,384]{1,0:T(8,128)(2,1)S(1)} collective-permute-done((bf16[64,384]{1,0:T(8,128)(2,1)S(1)}, bf16[64,384]{1,0:T(8,128)(2,1)S(1)}, u32[]{:S(2)}, u32[]{:S(2)}) %collective-permute-start.9) | collective-permute-done | bytes 49184 | tf_op jit(solution)/shard_map/ppermute | solution.py:314
  150.7 10.0 %all_gather.26.attended_ref = bf16[4,128,384]{2,1,0:T(8,128)(2,1)S(1)} all-gather(bf16[1,128,384]{2,1,0:T(8,128)(2,1)S(1)} %maximum_select_fusion), channel_id=1, replica_groups=mesh['yh'=2,'x'=4,'zo'=4,'zi'=2,'yl'=2,'c'=2] {'yl','c'}, dimensions={0}, use_global_device_ids=true | all-gather | bytes 491520 | tf_op jit(solution)/shard_map/all_gather | solution.py:316
  160.7 0.0 all-gather.8.cloned.1.call-done
  160.7 0.0 copy-done.2
  160.7 0.0 copy-start.1
  160.7 1.7 copy-done.1
  162.4 1.6 shard_map.107
  (7 shorter events, 0.1 us)
Async XLA Ops:
  6.5 7.8 %copy-start = (bf16[2,2,8,384]{3,2,1,0:T(8,128)(2,1)S(1)}, bf16[2,2,8,384]{3,2,1,0:T(8,128)(2,1)}, u32[]{:S(2)}) copy-start(bf16[2,2,8,384]{3,2,1,0:T(8,128)(2,1)} %param.11) | copy-start | bytes 73732
  6.5 50.1 %all-gather.6.cloned.1.call-start = ((), (), s32[]{:S(2)}) async-start(), calls=%async_computation.3 | async-start | bytes 1327104 | tf_op jit(solution)/shard_map/all_gather | solution.py:261
  6.5 9.6 %collective-permute-start.1 = (bf16[48,384]{1,0:T(8,128)(2,1)}, bf16[48,384]{1,0:T(8,128)(2,1)S(1)}, u32[]{:S(2)}, u32[]{:S(2)}) collective-permute-start(bf16[48,384]{1,0:T(8,128)(2,1)} %bitcast.45), channel_id=1, source_target_pairs={{0,0},{1,32},{2,64},{3,96},{32,128},{33,160},{34,192},{35,224},{64... | collective-permute-start | bytes 110600 | tf_op jit(solution)/shard_map/ppermute | solution.py:249
  13.2 5.2 %collective-permute-start = (bf16[48,512]{1,0:T(8,128)(2,1)S(1)}, bf16[48,512]{1,0:T(8,128)(2,1)S(1)}, u32[]{:S(2)}, u32[]{:S(2)}) collective-permute-start(bf16[48,512]{1,0:T(8,128)(2,1)S(1)} %get-tuple-element.41), channel_id=1, source_target_pairs={{0,128},{128,0},{1,129},{129,1},{2,130},{130,2},{3,131},{131,3},{4... | collective-permute-start | bytes 147464 | tf_op jit(solution)/shard_map/ppermute | solution.py:248
  20.0 10.5 %collective-permute-start.2 = (bf16[80,384]{1,0:T(8,128)(2,1)S(1)}, bf16[80,384]{1,0:T(8,128)(2,1)S(1)}, u32[]{:S(2)}, u32[]{:S(2)}) collective-permute-start(bf16[80,384]{1,0:T(8,128)(2,1)S(1)} %get-tuple-element.36), channel_id=1, source_target_pairs={{0,128},{128,0},{1,129},{129,1},{2,130},{130,2},{3,131},{131,3},{4... | collective-permute-start | bytes 184328 | tf_op jit(solution)/shard_map/ppermute | solution.py:268
  56.7 1.3 copy-start.5
  60.5 20.9 %copy-start.4 = (f32[128]{0:T(128)S(1)}, f32[128]{0:T(128)}, u32[]{:S(2)}) copy-start(f32[128]{0:T(128)} %param.19) | copy-start | bytes 1540
  60.5 20.9 %all-to-all-start.1 = ((bf16[8,128,640]{2,1,0:T(8,128)(2,1)}), bf16[8,128,640]{2,1,0:T(8,128)(2,1)S(1)}, u32[]{:S(2)}, u32[]{:S(2)}) async-start(bf16[8,128,640]{2,1,0:T(8,128)(2,1)} %get-tuple-element.23), calls=%async_computation.1 | async-start | bytes 2621440 | tf_op jit(solution)/shard_map/all_to_all | solution.py:281
  67.0 93.7 %all-gather.8.cloned.1.call-start = ((), (), s32[]{:S(2)}) async-start(), calls=%async_computation.4 | async-start | bytes 2654208 | tf_op jit(solution)/shard_map/all_gather | solution.py:282
  83.1 9.4 %copy-start.3 = (f32[128]{0:T(128)S(1)}, f32[128]{0:T(128)}, u32[]{:S(2)}) copy-start(f32[128]{0:T(128)} %param.18) | copy-start | bytes 1540
  83.1 42.9 %all-to-all-start.2 = ((bf16[8,288,384]{2,1,0:T(8,128)(2,1)}), bf16[8,288,384]{2,1,0:T(8,128)(2,1)S(1)}, u32[]{:S(2)}, u32[]{:S(2)}) async-start(bf16[8,288,384]{2,1,0:T(8,128)(2,1)} %shard_map.104), calls=%async_computation.2 | async-start | bytes 3538944 | tf_op jit(solution)/shard_map/all_to_all | solution.py:303
  92.6 68.1 %copy-start.2 = (f32[16,768]{1,0:T(8,128)S(1)}, f32[16,768]{1,0:T(8,128)}, u32[]{:S(2)}) copy-start(f32[16,768]{1,0:T(8,128)} %get-tuple-element.32.gate_ref) | copy-start | bytes 147460
  92.6 29.3 %collective-permute-start.3 = (bf16[128,384]{1,0:T(8,128)(2,1)S(1)}, bf16[128,384]{1,0:T(8,128)(2,1)S(1)}, u32[]{:S(2)}, u32[]{:S(2)}) collective-permute-start(bf16[128,384]{1,0:T(8,128)(2,1)S(1)} %shard_map.103.q0_ref), channel_id=1, source_target_pairs={{0,8},{8,16},{16,24},{24,0},{1,9},{9,17},{17,25},{25,1},{2,10},{10... | collective-permute-start | bytes 294920 | tf_op jit(solution)/shard_map/ppermute | solution.py:295
  95.8 30.2 %collective-permute-start.4 = (bf16[128,384]{1,0:T(8,128)(2,1)S(1)}, bf16[128,384]{1,0:T(8,128)(2,1)S(1)}, u32[]{:S(2)}, u32[]{:S(2)}) collective-permute-start(bf16[128,384]{1,0:T(8,128)(2,1)S(1)} %shard_map.103.q0_ref), channel_id=1, source_target_pairs={{0,16},{8,24},{16,0},{24,8},{1,17},{9,25},{17,1},{25,9},{2,18},{10... | collective-permute-start | bytes 294920 | tf_op jit(solution)/shard_map/ppermute | solution.py:295
  100.9 25.1 %collective-permute-start.5 = (bf16[128,384]{1,0:T(8,128)(2,1)S(1)}, bf16[128,384]{1,0:T(8,128)(2,1)S(1)}, u32[]{:S(2)}, u32[]{:S(2)}) collective-permute-start(bf16[128,384]{1,0:T(8,128)(2,1)S(1)} %shard_map.103.q0_ref), channel_id=1, source_target_pairs={{0,24},{8,0},{16,8},{24,16},{1,25},{9,1},{17,9},{25,17},{2,26},{10... | collective-permute-start | bytes 294920 | tf_op jit(solution)/shard_map/ppermute | solution.py:295
  131.0 5.2 %collective-permute-start.6 = (bf16[128,512]{1,0:T(8,128)(2,1)S(1)}, bf16[128,512]{1,0:T(8,128)(2,1)S(1)}, u32[]{:S(2)}, u32[]{:S(2)}) collective-permute-start(bf16[128,512]{1,0:T(8,128)(2,1)S(1)} %get-tuple-element.26), channel_id=1, source_target_pairs={{0,24},{8,0},{16,8},{24,16},{1,25},{9,1},{17,9},{25,17},{2,26},{10... | collective-permute-start | bytes 393224 | tf_op jit(solution)/shard_map/ppermute | solution.py:311
  131.4 10.8 %collective-permute-start.7 = (bf16[128,512]{1,0:T(8,128)(2,1)S(1)}, bf16[128,512]{1,0:T(8,128)(2,1)S(1)}, u32[]{:S(2)}, u32[]{:S(2)}) collective-permute-start(bf16[128,512]{1,0:T(8,128)(2,1)S(1)} %get-tuple-element.27), channel_id=1, source_target_pairs={{0,16},{8,24},{16,0},{24,8},{1,17},{9,25},{17,1},{25,9},{2,18},{10... | collective-permute-start | bytes 393224 | tf_op jit(solution)/shard_map/ppermute | solution.py:311
  135.4 10.3 %collective-permute-start.8 = (bf16[128,512]{1,0:T(8,128)(2,1)S(1)}, bf16[128,512]{1,0:T(8,128)(2,1)S(1)}, u32[]{:S(2)}, u32[]{:S(2)}) collective-permute-start(bf16[128,512]{1,0:T(8,128)(2,1)S(1)} %get-tuple-element.28), channel_id=1, source_target_pairs={{0,8},{8,16},{16,24},{24,0},{1,9},{9,17},{17,25},{25,1},{2,10},{10... | collective-permute-start | bytes 393224 | tf_op jit(solution)/shard_map/ppermute | solution.py:311
  146.2 4.5 %collective-permute-start.9 = (bf16[64,384]{1,0:T(8,128)(2,1)S(1)}, bf16[64,384]{1,0:T(8,128)(2,1)S(1)}, u32[]{:S(2)}, u32[]{:S(2)}) collective-permute-start(bf16[64,384]{1,0:T(8,128)(2,1)S(1)} %get-tuple-element.30), channel_id=1, source_target_pairs={{0,128},{128,0},{1,129},{129,1},{2,130},{130,2},{3,131},{131,3},{4... | collective-permute-start | bytes 147464 | tf_op jit(solution)/shard_map/ppermute | solution.py:314
  160.7 1.7 copy-start.1
Sparse Core Ops, SparseCore 0:
  19.2 35.7 all-gather.5
  70.5 77.9 all-gather.7

commit v3 on v2

--- a/solution.py
+++ b/solution.py
@@ -10,8 +10,10 @@
 CODE_LIMIT = 448.0
 LOG2E = 1.4426950408889634
 VMEM_BYTES = 16 * 1024 * 1024
-
-YX = ("yh", "x")
+WIDE_BYTES = 58 * 1024 * 1024
+
+X = ("xj", "xi")
+YX = ("yh",) + X
 Z = ("zo", "zi")
 H = ("yl", "c")
 
@@ -52,8 +54,9 @@
     gate_ref[...] = gates
 
 
-def norm_kernel(rows_ref, out_ref):
+def norm_kernel(rows_ref, y_ref, out_ref):
     features = 4 * 768
+    lower = y_ref[0] == 0
     for image in range(2):
         shift = rows_ref[:, 128 + 2 * image : 129 + 2 * image, :].astype(jnp.float32)
         scale = 1.0 + rows_ref[:, 129 + 2 * image : 130 + 2 * image, :].astype(jnp.float32)
@@ -64,57 +67,68 @@
             off = hidden - centre[None]
             variance = jnp.sum(jnp.sum(off * off, axis=0), axis=-1, keepdims=True) / features
             normed = (off * lax.rsqrt(variance + EPSILON)[None] * scale + shift).astype(jnp.bfloat16)
-            for y in range(2):
-                for x in range(4):
-                    for place, block in enumerate((4 * y + x, 4 * (1 - y) + x)):
-                        piece = normed[block // 2][:, (block % 2) * 384 : (block % 2) * 384 + 384]
-                        out_ref[4 * y + x, at : at + 16, place * 384 : place * 384 + 384] = piece
-
-
-def project_kernel(rows_ref, weights_ref, out_ref, columns_ref):
-    weights = weights_ref[...].reshape(384, 1536)
-    columns_ref[...] = weights[:, 1152:]
-    for x in range(4):
-        rows = jnp.concatenate([rows_ref[x], rows_ref[4 + x]], axis=0)
-        own, other = rows[:, :384], rows[:, 384:]
-        most = jnp.dot(own, weights[:, :512], preferred_element_type=jnp.float32) + jnp.dot(
-            other, weights[:, 512:1024], preferred_element_type=jnp.float32
-        )
-        rest = jnp.dot(own, weights[:, 1024:1152], preferred_element_type=jnp.float32)
-        both = jnp.concatenate([most, rest], axis=1).astype(jnp.bfloat16)
-        for image in range(2):
-            for y in range(2):
-                piece = both[y * 128 + image * 64 : y * 128 + image * 64 + 64]
-                out_ref[4 * image + x, y * 64 : y * 64 + 64, :] = piece
+            for x in range(4):
+                lanes = slice((x % 2) * 384, (x % 2) * 384 + 384)
+                low, high = normed[x // 2][:, lanes], normed[2 + x // 2][:, lanes]
+                out_ref[x, at : at + 16, 0:384] = jnp.where(lower, low, high)
+                out_ref[x, at : at + 16, 384:768] = jnp.where(lower, high, low)
+
+
+def column_kernel(weights_ref, columns_ref):
+    step = pl.program_id(0)
+
+    @pl.when(step == 0)
+    def _():
+        columns_ref[:, :, 0:128] = weights_ref[:, 0:48, :]
+
+    @pl.when(step == 1)
+    def _():
+        columns_ref[:, :, 128:256] = weights_ref[:, 0:48, :]
+        columns_ref[:, :, 256:384] = weights_ref[:, 48:96, :]
+
+
+def project_kernel(rows_ref, weights_ref, out_ref):
+    for part in range(3):
+        lanes = slice(part * 384, part * 384 + 384)
+        sums = jnp.zeros((512, 384), jnp.float32)
+        for y in range(2):
+            sums = sums + jnp.dot(
+                rows_ref[:, :, y * 384 : y * 384 + 384].reshape(512, 384),
+                weights_ref[:, y * 48 : y * 48 + 48, lanes].reshape(384, 384),
+                preferred_element_type=jnp.float32,
+            )
+        for x in range(4):
+            for image in range(2):
+                at = x * 128 + image * 64
+                place = (x % 2) * 64
+                out_ref[(x // 2) * 2 + image, place : place + 64, lanes] = sums[
+                    at : at + 64
+                ].astype(jnp.bfloat16)
 
 
 def rms_scale(vectors, gain):
     return vectors * lax.rsqrt(jnp.mean(vectors * vectors, axis=-1, keepdims=True) + EPSILON) * gain
 
 
-def summed(part_ref, sources, at):
-    acc = part_ref[sources[0], :, at : at + HD].astype(jnp.float32)
-    for source in sources[1:]:
+def summed(part_ref, at):
+    acc = part_ref[0, :, at : at + HD].astype(jnp.float32)
+    for source in range(1, 4):
         acc = acc + part_ref[source, :, at : at + HD].astype(jnp.float32)
     return acc
-
-
-LOW, HIGH = (0, 1, 2, 3), (4, 5, 6, 7)
 
 
 def query_kernel(part_ref, q_gain_ref, q_ref):
     for head in range(3):
         lanes = slice(head * HD, head * HD + HD)
-        q_ref[:, lanes] = rms_scale(summed(part_ref, LOW, head * HD), q_gain_ref[...]).astype(
+        q_ref[:, lanes] = rms_scale(summed(part_ref, head * HD), q_gain_ref[...]).astype(
             jnp.bfloat16
         )
 
 
-def restore_kernel(part_ref, prev_ref, kept_ref, got_ref, k_gain_ref, y_ref, kv_ref):
-    lower = y_ref[0] == 0
-    key_places = ((LOW, 384), (LOW + HIGH, 512), (HIGH, 384))
+def restore_kernel(part_ref, prev_ref, kept_ref, got_ref, k_gain_ref, image_ref, kv_ref):
+    first = image_ref[0] == 0
     kept, got = (ref[16:80, 0:HD].astype(jnp.float32) for ref in (kept_ref, got_ref))
-    scales = jnp.concatenate([jnp.where(lower, kept, got), jnp.where(lower, got, kept)], axis=0)
+    scales = jnp.concatenate([jnp.where(first, kept, got), jnp.where(first, got, kept)], axis=0)
 
     def restored(fresh, kind, head):
         earlier = prev_ref[kind, :, head * HD : head * HD + HD].astype(jnp.float32)
@@ -126,17 +140,13 @@
 
     for head in range(3):
         lanes = slice(head * HD, head * HD + HD)
-        keys = restored(rms_scale(summed(part_ref, *key_places[head]), k_gain_ref[...]), 0, head)
-        values = restored(summed(part_ref, HIGH, head * HD), 1, head)
-        for peer in range(8):
-            kv_ref[peer, 0:128, lanes] = keys
-            kv_ref[peer, 144:272, lanes] = values
+        keys = rms_scale(summed(part_ref, 384 + head * HD), k_gain_ref[...])
+        kv_ref[0:128, lanes] = restored(keys, 0, head)
+        kv_ref[144:272, lanes] = restored(summed(part_ref, 768 + head * HD), 1, head)
     own, far = (ref[0:16, :].astype(jnp.float32) for ref in (kept_ref, got_ref))
     for kind in range(2):
         text = jnp.concatenate([own[8 * kind : 8 * kind + 8], far[8 * kind : 8 * kind + 8]], axis=0)
-        text = text.astype(jnp.bfloat16)
-        for peer in range(8):
-            kv_ref[peer, 128 + 144 * kind : 144 + 144 * kind, :] = text
+        kv_ref[128 + 144 * kind : 144 + 144 * kind, :] = text.astype(jnp.bfloat16)
 
 
 def split_three(value):
@@ -174,9 +184,9 @@
         o_ref[:, 384:512] = stats[block].astype(jnp.bfloat16)
 
 
-def combine_kernel(p0_ref, p1_ref, p2_ref, p3_ref, y_ref, kept_ref, sent_ref):
+def combine_kernel(p0_ref, p1_ref, p2_ref, p3_ref, image_ref, kept_ref, sent_ref):
     parts = (p0_ref, p1_ref, p2_ref, p3_ref)
-    lower = y_ref[0] == 0
+    first = image_ref[0] == 0
     stats = [ref[:, 384:512].astype(jnp.float32) for ref in parts]
     for head in range(3):
         lanes = slice(head * HD, head * HD + HD)
@@ -193,8 +203,8 @@
         for share, ref in zip(shares[1:], parts[1:]):
             mixed = mixed + share * ref[:, lanes].astype(jnp.float32)
         mixed = (mixed / whole).astype(jnp.bfloat16)
-        kept_ref[:, lanes] = jnp.where(lower, mixed[:64], mixed[64:])
-        sent_ref[:, lanes] = jnp.where(lower, mixed[64:], mixed[:64])
+        kept_ref[:, lanes] = jnp.where(first, mixed[:64], mixed[64:])
+        sent_ref[:, lanes] = jnp.where(first, mixed[64:], mixed[:64])
 
 
 def output_kernel(attended_ref, weights_ref, gate_ref, out_ref):
@@ -204,7 +214,7 @@
         for group in range(4):
             sums = sums + lax.dot_general(
                 attended_ref[group],
-                weights_ref[half, group],
+                weights_ref[group, half].reshape(384, 384),
                 (((1,), (1,)), ((), ())),
                 preferred_element_type=jnp.float32,
             )
@@ -226,37 +236,43 @@
 
 def column_moves():
     moves = []
-    for y in range(2):
+    for yh in range(2):
         for x in range(4):
-            for head in range(4):
-                moves.append(((y * 4 + x) * 4 + head, ((x % 2) * 4 + head) * 4 + 2 * y + x // 2))
+            for yl in range(2):
+                for c in range(2):
+                    there = ((yl * 4 + 2 * c + x % 2) * 2 + yh) * 2 + x // 2
+                    moves.append((((yh * 4 + x) * 2 + yl) * 2 + c, there))
     return moves
 
 
 def per_device(
     image_hidden, text_kv, prev_kv, scale_exp, w_qkv, w_out, mod_table, timesteps, q_gain, k_gain
 ):
-    yh, x = lax.axis_index("yh"), lax.axis_index("x")
+    yh, xj, xi = (lax.axis_index(name) for name in YX)
     z = lax.axis_index(Z)
-    lower = yh == 0
-    y_at = yh.reshape(1)
+    first = xi == 0
+    image_at = xi.reshape(1)
+    swap = [(0, 1), (1, 0)]
     by_part = jnp.transpose(w_qkv, (1, 0, 2))
-    for_low = jnp.concatenate([by_part[0], by_part[1][:, :HD]], axis=1)
-    for_high = jnp.concatenate([by_part[2], by_part[1][:, 2 * HD :]], axis=1)
-    kept, sent = jnp.where(lower, for_low, for_high), jnp.where(lower, for_high, for_low)
-    swap = [(0, 1), (1, 0)]
-    got = lax.ppermute(sent, "yh", swap)
-    columns = lax.ppermute(jnp.transpose(w_out), ("yh", "x") + H, column_moves())
+    got = lax.ppermute(by_part, "yh", swap)
 
     rows, gates = call(
         pack_kernel,
         (shape(144, 768), jax.ShapeDtypeStruct((16, 768), jnp.float32)),
         (image_hidden.reshape(128, 768), jnp.transpose(mod_table, (1, 0, 2)), timesteps),
         scalars=(2,),
-        limit=4 * VMEM_BYTES - 8 * 1024 * 1024,
-    )
-
-    line = jnp.concatenate([kept, got, by_part[1][:, HD : 2 * HD], columns], axis=1)
+        limit=WIDE_BYTES,
+    )
+
+    columns = lax.ppermute(jnp.transpose(w_out), YX + H, column_moves())
+
+    line = jnp.concatenate(
+        [
+            jnp.concatenate([by_part[0], by_part[1], by_part[2], columns[:, :256]], axis=1),
+            jnp.concatenate([got[0], got[1], got[2], columns[:, 128:]], axis=1),
+        ],
+        axis=0,
+    )
     line, rows = lax.optimization_barrier((line, rows))
     weights = lax.all_gather(line, Z, axis=0)
 
@@ -264,43 +280,50 @@
     scales = jnp.pad(scales, ((0, 0), (0, 0), (0, 384 - 6)))
     text = jnp.transpose(text_kv, (1, 0, 2, 3)).reshape(2, 16, 384)
     package = jnp.concatenate([text, scales], axis=1)
-    own_package = jnp.where(lower, package[0], package[1])
-    far_package = lax.ppermute(jnp.where(lower, package[1], package[0]), "yh", swap)
-
+    own_package = jnp.where(first, package[0], package[1])
+    far_package = lax.ppermute(jnp.where(first, package[1], package[0]), "xi", swap)
     rows = lax.all_gather(rows, H, axis=0)
     rows, far_package = lax.optimization_barrier((rows, far_package))
-    normed = call(norm_kernel, shape(8, 128, 768), (rows,))
-    normed = lax.all_to_all(normed, YX, 0, 0, tiled=True)
-
-    partial, columns = call(
-        project_kernel,
-        (shape(8, 128, 640), shape(384, 384)),
-        (normed, weights),
-        flops=2 * 1024 * 768 * 576,
-    )
-    partial = lax.all_to_all(partial, YX, 0, 0, tiled=True)
+    normed = call(norm_kernel, shape(4, 128, 768), (rows, yh.reshape(1)), scalars=(1,))
+    normed = lax.all_to_all(normed, X, 0, 0, tiled=True)
+    columns = pl.pallas_call(
+        column_kernel,
+        out_shape=shape(8, 48, 384),
+        grid=(2,),
+        in_specs=[pl.BlockSpec((8, 96, HD), lambda step: (0, 0, 9 + step))],
+        out_specs=pl.BlockSpec((8, 48, 384), lambda step: (0, 0, 0)),
+        compiler_params=pltpu.CompilerParams(vmem_limit_bytes=WIDE_BYTES),
+    )(weights)
+    normed, columns = lax.optimization_barrier((normed, columns))
     columns = lax.all_gather(columns, YX, axis=0)
-
-    own_prev = lax.dynamic_index_in_dim(prev_kv, yh, 1, False)
-    first = (8 * x + z) * 64
+    partial = call(
+        project_kernel, shape(4, 128, 1152), (normed, weights), flops=2 * 512 * 768 * 1152
+    )
+    partial = lax.all_to_all(partial, X, 0, 0, tiled=True)
+
+    own_prev = lax.dynamic_index_in_dim(prev_kv, xi, 1, False)
+    start = (32 * yh + 16 * xj + z) * 64
     earlier = jnp.concatenate(
         [
-            lax.dynamic_slice_in_dim(own_prev, first, 64, 1),
-            lax.dynamic_slice_in_dim(own_prev, first + 2048, 64, 1),
+            lax.dynamic_slice_in_dim(own_prev, start, 64, 1),
+            lax.dynamic_slice_in_dim(own_prev, start + 512, 64, 1),
         ],
         axis=1,
     )
     queries = call(query_kernel, shape(128, 384), (partial, q_gain.reshape(1, HD)))
+    kv_pair = call(
+        restore_kernel,
+        shape(288, 384),
+        (partial, earlier, own_package, far_package, k_gain.reshape(1, HD), image_at),
+        scalars=(5,),
+    )
+    kv_pair = jnp.stack([kv_pair, lax.ppermute(kv_pair, "zi", swap)])
     far_queries = [
         lax.ppermute(queries, "zo", [(i, (i + k) % 4) for i in range(4)]) for k in (1, 2, 3)
     ]
-    kv_pair = call(
-        restore_kernel,
-        shape(8, 288, 384),
-        (partial, earlier, own_package, far_package, k_gain.reshape(1, HD), y_at),
-        scalars=(5,),
-    )
-    kv_pair = lax.all_to_all(kv_pair, ("x", "zi"), 0, 0, tiled=True)
+    kv_pair = lax.all_to_all(
+        jnp.broadcast_to(kv_pair, (4, 2, 288, 384)), ("yh", "xj"), 0, 0, tiled=True
+    ).reshape(8, 288, 384)
     mixed = call(
         attend_kernel,
         (shape(128, 512),) * 4,
@@ -310,22 +333,22 @@
     mixed = [mixed[0]] + [
         lax.ppermute(mixed[k], "zo", [(i, (i - k) % 4) for i in range(4)]) for k in (1, 2, 3)
     ]
-    own, far = call(combine_kernel, (shape(64, 384),) * 2, (*mixed, y_at), scalars=(4,))
-    far = lax.ppermute(far, "yh", [(0, 1), (1, 0)])
-    attended = jnp.where(lower, jnp.concatenate([own, far]), jnp.concatenate([far, own]))
+    own, far = call(combine_kernel, (shape(64, 384),) * 2, (*mixed, image_at), scalars=(4,))
+    far = lax.ppermute(far, "xi", swap)
+    attended = jnp.where(first, jnp.concatenate([own, far]), jnp.concatenate([far, own]))
     attended = lax.all_gather(attended, H, axis=0)
     return call(
         output_kernel,
         shape(2, 64, 768),
-        (attended, columns.reshape(2, 4, 384, 384), gates),
+        (attended, columns.reshape(4, 2, 8, 48, 384), gates),
         flops=2 * 128 * 1536 * 768,
     )
 
 
 def solution(mesh):
-    names = ("yh", "x", "zo", "zi", "yl", "c")
-    fine = Mesh(mesh.devices.reshape(2, 4, 4, 2, 2, 2), names)
-    patch, head = ("yh", "x", "zo", "zi"), ("yl", "c")
+    names = ("yh", "xj", "xi", "zo", "zi", "yl", "c")
+    fine = Mesh(mesh.devices.reshape(2, 2, 2, 4, 2, 2, 2), names)
+    patch, head = YX + Z, H
     placed = (
         P(None, patch, head),
         P(None, None, patch, head),

time: 173 us -> 155 us (0.90); the launches traced: 171 us -> 155 us
  blocking collectives: 44.9 us -> 31.3 us
  starting transfers between devices: 39.9 us -> 34 us
    all_to_all x1 -> x0, blocking collectives: 25.4 us -> none  [per_device(): normed = lax.all_to_all(normed, YX, 0, 0, tiled=True)]
    all_gather x1, waiting for transfers between devices: 0.01 us -> 21.5 us  [per_device(): weights = lax.all_gather(line, Z, axis=0)]
    ppermute x3, waiting for transfers between devices: 22.7 us -> 4.74 us  [per_device(): lax.ppermute(queries, 'zo', [(i, (i + k) % 4) for i in range(4)])]
    all_gather x1, blocking collectives: 9.98 us -> 18.8 us  [per_device(): attended = lax.all_gather(attended, H, axis=0)]
    ppermute x3, starting transfers between devices: 10.6 us -> 6.01 us  [per_device(): lax.ppermute(queries, 'zo', [(i, (i + k) % 4) for i in range(4)])]
    all_gather x1, blocking collectives: 9.45 us -> 12.5 us  [per_device(): rows = lax.all_gather(rows, H, axis=0)]
    ppermute x4 -> x5, starting transfers between devices: 8.9 us -> 6.19 us  [the longest x1 3.66 us: per_device(): got = lax.ppermute(by_part, 'yh', swap)]
    ppermute x3, waiting for transfers between devices: 10.3 us -> 7.59 us  [per_device(): lax.ppermute(mixed[k], 'zo', [(i, (i - k) % 4) for i in range(4)])]
  transfers between devices with their start and end apart: 14 -> 16, of which waited for: 8 -> 11; matrix products, arithmetic and copies ran while one was open for 2% -> 3% of each run, Pallas kernels for 6% -> 9%
where the time goes in v3:
time: 155 us
  waiting for transfers between devices  53.7 us (35%)
  starting transfers between devices  34 us (22%)
  blocking collectives  31.3 us (20%)
  Pallas kernels  15.5 us (10%)
  between operations  13.5 us (9%)
  local copies, waits for them, and re-layouts  5.03 us (3%)
  other arithmetic  1.6 us (1%)
    all_gather x1, waiting for transfers between devices, per_device(): weights = lax.all_gather(line, Z, axis=0)  21.5 us
    all_gather x1, blocking collectives, per_device(): attended = lax.all_gather(attended, H, axis=0)  18.8 us
    pallas_call x8, Pallas kernels, call(): pl.pallas_call(kernel, out_shape=out_shapes, in_specs=[pl.BlockSpec(memor...  13.5 us
    all_gather x1, blocking collectives, per_device(): rows = lax.all_gather(rows, H, axis=0)  12.5 us
    all_to_all x1, waiting for transfers between devices, per_device(): partial = lax.all_to_all(partial, X, 0, 0, tiled=True)  8.97 us
    ppermute x3, waiting for transfers between devices, per_device(): lax.ppermute(mixed[k], 'zo', [(i, (i - k) % 4) for i in range(4)])  7.59 us
    all_to_all x1, starting transfers between devices, per_device(): lax.all_to_all(jnp.broadcast_to(kv_pair, (4, 2, 288, 384)), ('yh', 'xj'),...  6.62 us
    ppermute x3, starting transfers between devices, per_device(): lax.ppermute(mixed[k], 'zo', [(i, (i - k) % 4) for i in range(4)])  6.12 us
  transfers between devices with their start and end apart: 16, of which 11 were waited for; matrix products, arithmetic and copies ran while one was open for 3% of the time, Pallas kernels for 9%

profile of v3, /device:TPU:7, one launch (start us, length us, event | category | flops | bytes accessed | tf_op | source)
XLA Modules:
  0.0 154.7 jit_solution(15014417753770574686)
XLA Ops:
  6.5 0.0 copy-start
  6.5 0.0 all-gather.6.cloned.1.call-start
  6.5 1.5 collective-permute-start
  8.1 3.7 %collective-permute-start.1 = (bf16[3,48,384]{2,1,0:T(8,128)(2,1)}, bf16[3,48,384]{2,1,0:T(8,128)(2,1)S(1)}, u32[]{:S(2)}, u32[]{:S(2)}) collective-permute-start(bf16[3,48,384]{2,1,0:T(8,128)(2,1)} %bitcast.56), channel_id=1, source_target_pairs={{0,128},{128,0},{1,129},{129,1},{2,130},{130,2},{3,131},{131,3},{4... | collective-permute-start | bytes 331784 | tf_op jit(solution)/shard_map/ppermute | solution.py:257
  11.7 0.8 slice_bitcast_fusion.5
  12.6 1.8 %shard_map.100 = (bf16[144,768]{1,0:T(8,128)(2,1)}, f32[16,768]{1,0:T(8,128)}) custom-call(bf16[128,768]{1,0:T(8,128)(2,1)} %bitcast.54, bf16[3,28,768]{2,1,0:T(8,128)(2,1)} %bitcast.55, s32[2]{0:T(128)} %steps_ref.1), custom_call_target="tpu_custom_call" | custom-call | tf_op jit(solution)/shard_map/pallas_call | solution.py:22
  14.3 0.0 collective-permute-done
  14.4 0.0 collective-permute-done.1
  14.4 0.7 maximum_maximum_fusion
  15.1 0.0 all-gather.6.cloned.1.call-update
  15.2 0.7 fusion.10
  15.9 0.1 copy.16
  16.0 0.0 copy-done
  16.1 0.8 collective-permute-start.2
  16.9 12.5 %all-gather = bf16[576,768]{1,0:T(8,128)(2,1)S(1)} all-gather(bf16[144,768]{1,0:T(8,128)(2,1)} %get-tuple-element.20), channel_id=2, replica_groups=mesh['yh'=2,'xj'=2,'xi'=2,'zo'=4,'zi'=2,'yl'=2,'c'=2] {'yl','c'}, dimensions={0}, use_global_device_ids=true | all-gather | bytes 1105920 | tf_op jit(solution)/shard_map/all_gather | solution.py:285
  29.4 0.0 collective-permute-done.2.got_ref
  29.4 1.5 shard_map.101
  31.0 4.7 %all-to-all-start = ((bf16[4,128,768]{2,1,0:T(8,128)(2,1)}), bf16[4,128,768]{2,1,0:T(8,128)(2,1)S(1)}, u32[]{:S(2)}, u32[]{:S(2)}) async-start(bf16[4,128,768]{2,1,0:T(8,128)(2,1)} %shard_map.101), calls=%async_computation | async-start | bytes 1572864 | tf_op jit(solution)/shard_map/all_to_all | solution.py:288
  35.7 0.0 all-gather.8.cloned.1.call-start
  35.7 21.5 %all-gather.6.cloned.1.call-done = bf16[768,1408]{1,0:T(8,128)(2,1)} async-done(((bf16[96,1408]{1,0:T(8,128)(2,1)}), bf16[768,1408]{1,0:T(8,128)(2,1)}) %all-gather.6.cloned.1.call-update) | async-done | bytes 2162704 | tf_op jit(solution)/shard_map/all_gather | solution.py:277
  57.1 0.0 copy-start.1
  57.1 1.9 %shard_map.102 = bf16[8,48,384]{2,1,0:T(8,128)(2,1)} custom-call(bf16[8,96,1408]{2,1,0:T(8,128)(2,1)} %bitcast.44), custom_call_target="tpu_custom_call" | custom-call | tf_op jit(solution)/shard_map/pallas_call | solution.py:289
  59.1 0.0 all-to-all-done.rows_ref
  59.1 0.0 all-gather.8.cloned.1.call-update
  59.1 0.0 copy-done.1
  59.1 2.6 %shard_map.103 = bf16[4,128,1152]{2,1,0:T(8,128)(2,1)} custom-call(bf16[4,128,768]{2,1,0:T(8,128)(2,1)S(1)} %all-to-all-done.rows_ref, bf16[8,96,1408]{2,1,0:T(8,128)(2,1)S(1)} %bitcast.45), custom_call_target="tpu_custom_call" | custom-call | flops 905969664 | tf_op jit(solution)/shard_map/pallas_call | solution.py:22
  61.7 0.0 copy-start.4
  61.7 4.4 %all-to-all-start.1 = ((bf16[4,128,1152]{2,1,0:T(8,128)(2,1)}), bf16[4,128,1152]{2,1,0:T(8,128)(2,1)S(1)}, u32[]{:S(2)}, u32[]{:S(2)}) async-start(bf16[4,128,1152]{2,1,0:T(8,128)(2,1)} %shard_map.103), calls=%async_computation.1 | async-start | bytes 2359296 | tf_op jit(solution)/shard_map/all_to_all | solution.py:302
  66.1 1.0 dynamic-slice_bitcast_fusion.1
  67.1 9.0 %all-to-all-done.1.part_ref = bf16[4,128,1152]{2,1,0:T(8,128)(2,1)S(1)} async-done(((bf16[4,128,1152]{2,1,0:T(8,128)(2,1)}), bf16[4,128,1152]{2,1,0:T(8,128)(2,1)S(1)}, u32[]{:S(2)}, u32[]{:S(2)}) %all-to-all-start.1) | async-done | bytes 1179680 | tf_op jit(solution)/shard_map/all_to_all | solution.py:302
  76.1 0.0 copy-done.4
  76.1 0.4 shard_map.105
  76.5 0.1 collective-permute-start.6
  76.6 5.2 %collective-permute-done.6 = bf16[288,384]{1,0:T(8,128)(2,1)S(1)} collective-permute-done((bf16[288,384]{1,0:T(8,128)(2,1)S(1)}, bf16[288,384]{1,0:T(8,128)(2,1)S(1)}, u32[]{:S(2)}, u32[]{:S(2)}) %collective-permute-start.6) | collective-permute-done | bytes 221216 | tf_op jit(solution)/shard_map/ppermute | solution.py:320
  81.7 0.1 pad_maximum_fusion
  81.8 1.4 broadcast_in_dim.53
  83.2 0.0 copy-start.5
  83.2 6.6 %all-to-all-start.2 = ((bf16[4,2,288,384]{3,2,1,0:T(8,128)(2,1)}), bf16[4,2,288,384]{3,2,1,0:T(8,128)(2,1)S(1)}, u32[]{:S(2)}, u32[]{:S(2)}) async-start(bf16[4,2,288,384]{3,2,1,0:T(8,128)(2,1)} %broadcast_in_dim.53), calls=%async_computation.2 | async-start | bytes 3538944 | tf_op jit(solution)/shard_map/all_to_all | solution.py:324
  89.8 0.0 copy-done.5
  89.8 0.1 shard_map.104.q0_ref
  89.9 2.2 %collective-permute-start.3 = (bf16[128,384]{1,0:T(8,128)(2,1)S(1)}, bf16[128,384]{1,0:T(8,128)(2,1)S(1)}, u32[]{:S(2)}, u32[]{:S(2)}) collective-permute-start(bf16[128,384]{1,0:T(8,128)(2,1)S(1)} %shard_map.104.q0_ref), channel_id=1, source_target_pairs={{0,8},{8,16},{16,24},{24,0},{1,9},{9,17},{17,25},{25,1},{2,10},{10... | collective-permute-start | bytes 294920 | tf_op jit(solution)/shard_map/ppermute | solution.py:322
  92.2 1.8 %collective-permute-start.4 = (bf16[128,384]{1,0:T(8,128)(2,1)S(1)}, bf16[128,384]{1,0:T(8,128)(2,1)S(1)}, u32[]{:S(2)}, u32[]{:S(2)}) collective-permute-start(bf16[128,384]{1,0:T(8,128)(2,1)S(1)} %shard_map.104.q0_ref), channel_id=1, source_target_pairs={{0,16},{8,24},{16,0},{24,8},{1,17},{9,25},{17,1},{25,9},{2,18},{10... | collective-permute-start | bytes 294920 | tf_op jit(solution)/shard_map/ppermute | solution.py:322
  93.9 2.0 %collective-permute-start.5 = (bf16[128,384]{1,0:T(8,128)(2,1)S(1)}, bf16[128,384]{1,0:T(8,128)(2,1)S(1)}, u32[]{:S(2)}, u32[]{:S(2)}) collective-permute-start(bf16[128,384]{1,0:T(8,128)(2,1)S(1)} %shard_map.104.q0_ref), channel_id=1, source_target_pairs={{0,24},{8,0},{16,8},{24,16},{1,25},{9,1},{17,9},{25,17},{2,26},{10... | collective-permute-start | bytes 294920 | tf_op jit(solution)/shard_map/ppermute | solution.py:322
  95.9 0.1 collective-permute-done.3.q1_ref
  96.0 3.5 %collective-permute-done.4.q2_ref = bf16[128,384]{1,0:T(8,128)(2,1)S(1)} collective-permute-done((bf16[128,384]{1,0:T(8,128)(2,1)S(1)}, bf16[128,384]{1,0:T(8,128)(2,1)S(1)}, u32[]{:S(2)}, u32[]{:S(2)}) %collective-permute-start.4) | collective-permute-done | bytes 98336 | tf_op jit(solution)/shard_map/ppermute | solution.py:322
  99.6 1.1 collective-permute-done.5.q3_ref
  100.7 2.4 %all-to-all-done.2 = bf16[4,2,288,384]{3,2,1,0:T(8,128)(2,1)S(1)} async-done(((bf16[4,2,288,384]{3,2,1,0:T(8,128)(2,1)}), bf16[4,2,288,384]{3,2,1,0:T(8,128)(2,1)S(1)}, u32[]{:S(2)}, u32[]{:S(2)}) %all-to-all-start.2) | async-done | bytes 1769504 | tf_op jit(solution)/shard_map/all_to_all | solution.py:324
  103.1 0.0 copy-start.3
  103.1 5.0 %shard_map.106 = (bf16[128,512]{1,0:T(8,128)(2,1)S(1)}, bf16[128,512]{1,0:T(8,128)(2,1)S(1)}, bf16[128,512]{1,0:T(8,128)(2,1)S(1)}, bf16[128,512]{1,0:T(8,128)(2,1)S(1)}) custom-call(bf16[128,384]{1,0:T(8,128)(2,1)S(1)} %shard_map.104.q0_ref, bf16[128,384]{1,0:T(8,128)(2,1)S(1)} %collective-permute-done.3.q1_ref, ...), custom_call_target="tpu_custom_call" | custom-call | flops 905969664 | tf_op jit(solution)/shard_map/pallas_call | solution.py:22
  108.2 2.6 %collective-permute-start.7 = (bf16[128,512]{1,0:T(8,128)(2,1)S(1)}, bf16[128,512]{1,0:T(8,128)(2,1)S(1)}, u32[]{:S(2)}, u32[]{:S(2)}) collective-permute-start(bf16[128,512]{1,0:T(8,128)(2,1)S(1)} %get-tuple-element.26), channel_id=1, source_target_pairs={{0,24},{8,0},{16,8},{24,16},{1,25},{9,1},{17,9},{25,17},{2,26},{10... | collective-permute-start | bytes 393224 | tf_op jit(solution)/shard_map/ppermute | solution.py:334
  110.8 3.5 %collective-permute-start.8 = (bf16[128,512]{1,0:T(8,128)(2,1)S(1)}, bf16[128,512]{1,0:T(8,128)(2,1)S(1)}, u32[]{:S(2)}, u32[]{:S(2)}) collective-permute-start(bf16[128,512]{1,0:T(8,128)(2,1)S(1)} %get-tuple-element.27), channel_id=1, source_target_pairs={{0,16},{8,24},{16,0},{24,8},{1,17},{9,25},{17,1},{25,9},{2,18},{10... | collective-permute-start | bytes 393224 | tf_op jit(solution)/shard_map/ppermute | solution.py:334
  114.3 0.0 collective-permute-start.9
  114.3 1.8 %collective-permute-done.7.p1_ref = bf16[128,512]{1,0:T(8,128)(2,1)S(1)} collective-permute-done((bf16[128,512]{1,0:T(8,128)(2,1)S(1)}, bf16[128,512]{1,0:T(8,128)(2,1)S(1)}, u32[]{:S(2)}, u32[]{:S(2)}) %collective-permute-start.7) | collective-permute-done | bytes 131104 | tf_op jit(solution)/shard_map/ppermute | solution.py:334
  116.0 5.1 %collective-permute-done.8.p2_ref = bf16[128,512]{1,0:T(8,128)(2,1)S(1)} collective-permute-done((bf16[128,512]{1,0:T(8,128)(2,1)S(1)}, bf16[128,512]{1,0:T(8,128)(2,1)S(1)}, u32[]{:S(2)}, u32[]{:S(2)}) %collective-permute-start.8) | collective-permute-done | bytes 131104 | tf_op jit(solution)/shard_map/ppermute | solution.py:334
  121.2 0.7 collective-permute-done.9.p3_ref
  121.9 0.5 shard_map.107
  122.4 0.1 collective-permute-start.10
  122.5 3.3 %collective-permute-done.10 = bf16[64,384]{1,0:T(8,128)(2,1)S(1)} collective-permute-done((bf16[64,384]{1,0:T(8,128)(2,1)S(1)}, bf16[64,384]{1,0:T(8,128)(2,1)S(1)}, u32[]{:S(2)}, u32[]{:S(2)}) %collective-permute-start.10) | collective-permute-done | bytes 49184 | tf_op jit(solution)/shard_map/ppermute | solution.py:337
  125.8 18.8 %all_gather.26.attended_ref = bf16[4,128,384]{2,1,0:T(8,128)(2,1)S(1)} all-gather(bf16[1,128,384]{2,1,0:T(8,128)(2,1)S(1)} %maximum_select_fusion), channel_id=1, replica_groups=mesh['yh'=2,'xj'=2,'xi'=2,'zo'=4,'zi'=2,'yl'=2,'c'=2] {'yl','c'}, dimensions={0}, use_global_device_ids=true | all-gather | bytes 491520 | tf_op jit(solution)/shard_map/all_gather | solution.py:339
  144.6 0.0 all-gather.8.cloned.1.call-done
  144.6 0.0 copy-done.3
  144.6 0.0 copy-start.2
  144.6 1.7 %copy-done.2 = bf16[64,48,384]{2,1,0:T(8,128)(2,1)S(1)} copy-done((bf16[64,48,384]{2,1,0:T(8,128)(2,1)S(1)}, bf16[64,48,384]{2,1,0:T(8,128)(2,1)}, u32[]{:S(2)}) %copy-start.2) | copy-done | bytes 2359320
  146.2 1.6 %shard_map.108 = bf16[2,64,768]{2,1,0:T(8,128)(2,1)} custom-call(bf16[4,128,384]{2,1,0:T(8,128)(2,1)S(1)} %all_gather.26.attended_ref, bf16[4,2,8,48,384]{4,3,2,1,0:T(8,128)(2,1)S(1)} %bitcast.47, f32[16,768]{1,0:T(8,128)S(1)} %copy-done.3), custom_call_target="tpu_custom_call" | custom-call | flops 301989888 | tf_op jit(solution)/shard_map/pallas_call | solution.py:22
  (7 shorter events, 0.1 us)
Async XLA Ops:
  6.5 9.5 %copy-start = (bf16[2,2,8,384]{3,2,1,0:T(8,128)(2,1)S(1)}, bf16[2,2,8,384]{3,2,1,0:T(8,128)(2,1)}, u32[]{:S(2)}) copy-start(bf16[2,2,8,384]{3,2,1,0:T(8,128)(2,1)} %param.11) | copy-start | bytes 73732
  6.5 50.6 %all-gather.6.cloned.1.call-start = ((), (), s32[]{:S(2)}) async-start(), calls=%async_computation.3 | async-start | bytes 2433024 | tf_op jit(solution)/shard_map/all_gather | solution.py:277
  6.5 7.8 %collective-permute-start = (bf16[48,384]{1,0:T(8,128)(2,1)}, bf16[48,384]{1,0:T(8,128)(2,1)S(1)}, u32[]{:S(2)}, u32[]{:S(2)}) collective-permute-start(bf16[48,384]{1,0:T(8,128)(2,1)} %bitcast.60), channel_id=1, source_target_pairs={{0,0},{1,64},{2,128},{3,192},{32,32},{33,96},{34,160},{35,224},{64... | collective-permute-start | bytes 110600 | tf_op jit(solution)/shard_map/ppermute | solution.py:267
  8.1 6.3 %collective-permute-start.1 = (bf16[3,48,384]{2,1,0:T(8,128)(2,1)}, bf16[3,48,384]{2,1,0:T(8,128)(2,1)S(1)}, u32[]{:S(2)}, u32[]{:S(2)}) collective-permute-start(bf16[3,48,384]{2,1,0:T(8,128)(2,1)} %bitcast.56), channel_id=1, source_target_pairs={{0,128},{128,0},{1,129},{129,1},{2,130},{130,2},{3,131},{131,3},{4... | collective-permute-start | bytes 331784 | tf_op jit(solution)/shard_map/ppermute | solution.py:257
  16.1 13.3 %collective-permute-start.2 = (bf16[80,384]{1,0:T(8,128)(2,1)S(1)}, bf16[80,384]{1,0:T(8,128)(2,1)S(1)}, u32[]{:S(2)}, u32[]{:S(2)}) collective-permute-start(bf16[80,384]{1,0:T(8,128)(2,1)S(1)} %get-tuple-element.36), channel_id=1, source_target_pairs={{0,32},{32,0},{1,33},{33,1},{2,34},{34,2},{3,35},{35,3},{4,36},{36... | collective-permute-start | bytes 184328 | tf_op jit(solution)/shard_map/ppermute | solution.py:284
  31.0 28.1 %all-to-all-start = ((bf16[4,128,768]{2,1,0:T(8,128)(2,1)}), bf16[4,128,768]{2,1,0:T(8,128)(2,1)S(1)}, u32[]{:S(2)}, u32[]{:S(2)}) async-start(bf16[4,128,768]{2,1,0:T(8,128)(2,1)} %shard_map.101), calls=%async_computation | async-start | bytes 1572864 | tf_op jit(solution)/shard_map/all_to_all | solution.py:288
  35.7 108.9 %all-gather.8.cloned.1.call-start = ((), (), s32[]{:S(2)}) async-start(), calls=%async_computation.4 | async-start | bytes 2654208 | tf_op jit(solution)/shard_map/all_gather | solution.py:298
  57.1 2.0 %copy-start.1 = (bf16[768,1408]{1,0:T(8,128)(2,1)S(1)}, bf16[768,1408]{1,0:T(8,128)(2,1)}, u32[]{:S(2)}) copy-start(bf16[768,1408]{1,0:T(8,128)(2,1)} %all-gather.6.cloned.1.call-done) | copy-start | bytes 6488068
  61.7 14.4 %copy-start.4 = (f32[128]{0:T(128)S(1)}, f32[128]{0:T(128)}, u32[]{:S(2)}) copy-start(f32[128]{0:T(128)} %param.19) | copy-start | bytes 1540
  61.7 14.4 %all-to-all-start.1 = ((bf16[4,128,1152]{2,1,0:T(8,128)(2,1)}), bf16[4,128,1152]{2,1,0:T(8,128)(2,1)S(1)}, u32[]{:S(2)}, u32[]{:S(2)}) async-start(bf16[4,128,1152]{2,1,0:T(8,128)(2,1)} %shard_map.103), calls=%async_computation.1 | async-start | bytes 2359296 | tf_op jit(solution)/shard_map/all_to_all | solution.py:302
  76.5 5.3 %collective-permute-start.6 = (bf16[288,384]{1,0:T(8,128)(2,1)S(1)}, bf16[288,384]{1,0:T(8,128)(2,1)S(1)}, u32[]{:S(2)}, u32[]{:S(2)}) collective-permute-start(bf16[288,384]{1,0:T(8,128)(2,1)S(1)} %shard_map.105), channel_id=1, source_target_pairs={{0,4},{4,0},{1,5},{5,1},{2,6},{6,2},{3,7},{7,3},{8,12},{12,8},{9,1... | collective-permute-start | bytes 663560 | tf_op jit(solution)/shard_map/ppermute | solution.py:320
  83.2 6.6 %copy-start.5 = (f32[128]{0:T(128)S(1)}, f32[128]{0:T(128)}, u32[]{:S(2)}) copy-start(f32[128]{0:T(128)} %param.18) | copy-start | bytes 1540
  83.2 19.9 %all-to-all-start.2 = ((bf16[4,2,288,384]{3,2,1,0:T(8,128)(2,1)}), bf16[4,2,288,384]{3,2,1,0:T(8,128)(2,1)S(1)}, u32[]{:S(2)}, u32[]{:S(2)}) async-start(bf16[4,2,288,384]{3,2,1,0:T(8,128)(2,1)} %broadcast_in_dim.53), calls=%async_computation.2 | async-start | bytes 3538944 | tf_op jit(solution)/shard_map/all_to_all | solution.py:324
  89.9 6.1 %collective-permute-start.3 = (bf16[128,384]{1,0:T(8,128)(2,1)S(1)}, bf16[128,384]{1,0:T(8,128)(2,1)S(1)}, u32[]{:S(2)}, u32[]{:S(2)}) collective-permute-start(bf16[128,384]{1,0:T(8,128)(2,1)S(1)} %shard_map.104.q0_ref), channel_id=1, source_target_pairs={{0,8},{8,16},{16,24},{24,0},{1,9},{9,17},{17,25},{25,1},{2,10},{10... | collective-permute-start | bytes 294920 | tf_op jit(solution)/shard_map/ppermute | solution.py:322
  92.2 7.4 %collective-permute-start.4 = (bf16[128,384]{1,0:T(8,128)(2,1)S(1)}, bf16[128,384]{1,0:T(8,128)(2,1)S(1)}, u32[]{:S(2)}, u32[]{:S(2)}) collective-permute-start(bf16[128,384]{1,0:T(8,128)(2,1)S(1)} %shard_map.104.q0_ref), channel_id=1, source_target_pairs={{0,16},{8,24},{16,0},{24,8},{1,17},{9,25},{17,1},{25,9},{2,18},{10... | collective-permute-start | bytes 294920 | tf_op jit(solution)/shard_map/ppermute | solution.py:322
  93.9 6.7 %collective-permute-start.5 = (bf16[128,384]{1,0:T(8,128)(2,1)S(1)}, bf16[128,384]{1,0:T(8,128)(2,1)S(1)}, u32[]{:S(2)}, u32[]{:S(2)}) collective-permute-start(bf16[128,384]{1,0:T(8,128)(2,1)S(1)} %shard_map.104.q0_ref), channel_id=1, source_target_pairs={{0,24},{8,0},{16,8},{24,16},{1,25},{9,1},{17,9},{25,17},{2,26},{10... | collective-permute-start | bytes 294920 | tf_op jit(solution)/shard_map/ppermute | solution.py:322
  103.1 41.5 %copy-start.3 = (f32[16,768]{1,0:T(8,128)S(1)}, f32[16,768]{1,0:T(8,128)}, u32[]{:S(2)}) copy-start(f32[16,768]{1,0:T(8,128)} %get-tuple-element.32.gate_ref) | copy-start | bytes 147460
  108.2 7.9 %collective-permute-start.7 = (bf16[128,512]{1,0:T(8,128)(2,1)S(1)}, bf16[128,512]{1,0:T(8,128)(2,1)S(1)}, u32[]{:S(2)}, u32[]{:S(2)}) collective-permute-start(bf16[128,512]{1,0:T(8,128)(2,1)S(1)} %get-tuple-element.26), channel_id=1, source_target_pairs={{0,24},{8,0},{16,8},{24,16},{1,25},{9,1},{17,9},{25,17},{2,26},{10... | collective-permute-start | bytes 393224 | tf_op jit(solution)/shard_map/ppermute | solution.py:334
  110.8 10.4 %collective-permute-start.8 = (bf16[128,512]{1,0:T(8,128)(2,1)S(1)}, bf16[128,512]{1,0:T(8,128)(2,1)S(1)}, u32[]{:S(2)}, u32[]{:S(2)}) collective-permute-start(bf16[128,512]{1,0:T(8,128)(2,1)S(1)} %get-tuple-element.27), channel_id=1, source_target_pairs={{0,16},{8,24},{16,0},{24,8},{1,17},{9,25},{17,1},{25,9},{2,18},{10... | collective-permute-start | bytes 393224 | tf_op jit(solution)/shard_map/ppermute | solution.py:334
  114.3 7.6 %collective-permute-start.9 = (bf16[128,512]{1,0:T(8,128)(2,1)S(1)}, bf16[128,512]{1,0:T(8,128)(2,1)S(1)}, u32[]{:S(2)}, u32[]{:S(2)}) collective-permute-start(bf16[128,512]{1,0:T(8,128)(2,1)S(1)} %get-tuple-element.28), channel_id=1, source_target_pairs={{0,8},{8,16},{16,24},{24,0},{1,9},{9,17},{17,25},{25,1},{2,10},{10... | collective-permute-start | bytes 393224 | tf_op jit(solution)/shard_map/ppermute | solution.py:334
  122.4 3.4 %collective-permute-start.10 = (bf16[64,384]{1,0:T(8,128)(2,1)S(1)}, bf16[64,384]{1,0:T(8,128)(2,1)S(1)}, u32[]{:S(2)}, u32[]{:S(2)}) collective-permute-start(bf16[64,384]{1,0:T(8,128)(2,1)S(1)} %get-tuple-element.30), channel_id=1, source_target_pairs={{0,32},{32,0},{1,33},{33,1},{2,34},{34,2},{3,35},{35,3},{4,36},{36... | collective-permute-start | bytes 147464 | tf_op jit(solution)/shard_map/ppermute | solution.py:337
  144.6 1.7 %copy-start.2 = (bf16[64,48,384]{2,1,0:T(8,128)(2,1)S(1)}, bf16[64,48,384]{2,1,0:T(8,128)(2,1)}, u32[]{:S(2)}) copy-start(bf16[64,48,384]{2,1,0:T(8,128)(2,1)} %all-gather.8.cloned.1.call-done) | copy-start | bytes 7077892
Sparse Core Ops, SparseCore 0:
  15.3 41.8 all-gather.5
  59.7 79.9 all-gather.7

commit v4 on v3

--- a/solution.py
+++ b/solution.py
@@ -18,12 +18,14 @@
 H = ("yl", "c")
 
 
-def call(kernel, out_shapes, operands, scratch=(), scalars=(), flops=0, limit=VMEM_BYTES):
+def call(kernel, out_shapes, operands, scratch=(), scalars=(), far=(), flops=0, limit=VMEM_BYTES):
     return pl.pallas_call(
         kernel,
         out_shape=out_shapes,
         in_specs=[
-            pl.BlockSpec(memory_space=pltpu.SMEM if at in scalars else pltpu.VMEM)
+            pl.BlockSpec(
+                memory_space=pltpu.SMEM if at in scalars else pltpu.HBM if at in far else pltpu.VMEM
+            )
             for at in range(len(operands))
         ],
         out_specs=jax.tree.map(lambda _: pl.BlockSpec(memory_space=pltpu.VMEM), out_shapes),
@@ -75,26 +77,27 @@
 
 
 def column_kernel(weights_ref, columns_ref):
-    step = pl.program_id(0)
-
-    @pl.when(step == 0)
-    def _():
-        columns_ref[:, :, 0:128] = weights_ref[:, 0:48, :]
-
-    @pl.when(step == 1)
-    def _():
-        columns_ref[:, :, 128:256] = weights_ref[:, 0:48, :]
-        columns_ref[:, :, 256:384] = weights_ref[:, 48:96, :]
-
-
-def project_kernel(rows_ref, weights_ref, out_ref):
+    columns_ref[:, :, 0:256] = weights_ref[:, 0:48, :]
+    columns_ref[:, :, 256:384] = weights_ref[:, 48:96, 128:256]
+
+
+def project_kernel(rows_ref, weights_ref, out_ref, held_ref, arrived):
+    copies = [
+        pltpu.make_async_copy(
+            weights_ref.at[:, :, pl.ds(256 + part * 384, 384)], held_ref.at[part], arrived.at[part]
+        )
+        for part in range(3)
+    ]
+    for copy in copies:
+        copy.start()
     for part in range(3):
         lanes = slice(part * 384, part * 384 + 384)
+        copies[part].wait()
         sums = jnp.zeros((512, 384), jnp.float32)
         for y in range(2):
             sums = sums + jnp.dot(
                 rows_ref[:, :, y * 384 : y * 384 + 384].reshape(512, 384),
-                weights_ref[:, y * 48 : y * 48 + 48, lanes].reshape(384, 384),
+                held_ref[part, :, y * 48 : y * 48 + 48, :].reshape(384, 384),
                 preferred_element_type=jnp.float32,
             )
         for x in range(4):
@@ -157,37 +160,35 @@
     return first, second, third
 
 
-def attend_kernel(q0_ref, q1_ref, q2_ref, q3_ref, kv_ref, o0_ref, o1_ref, o2_ref, o3_ref):
+def attend_kernel(q_ref, kv_ref, o_ref):
     factor = LOG2E * HD**-0.5
     lane = lax.broadcasted_iota(jnp.int32, (128, HD), 1)
-    stats = [jnp.zeros((128, HD), jnp.float32) for _ in range(4)]
+    stat = jnp.zeros((128, HD), jnp.float32)
     for head in range(3):
         lanes = slice(head * HD, head * HD + HD)
         keys = kv_ref[:, 0:144, lanes].reshape(1152, HD)
         values = kv_ref[:, 144:288, lanes].reshape(1152, HD)
-        for block, (q_ref, o_ref) in enumerate(
-            ((q0_ref, o0_ref), (q1_ref, o1_ref), (q2_ref, o2_ref), (q3_ref, o3_ref))
-        ):
-            logits = lax.dot_general(
-                q_ref[:, lanes], keys, (((1,), (1,)), ((), ())), preferred_element_type=jnp.float32
-            )
-            peak = jnp.max(logits, axis=-1, keepdims=True)
-            terms = jnp.exp2((logits - peak) * factor)
-            total = jnp.sum(terms, axis=-1, keepdims=True)
-            mixed = jnp.dot(terms.astype(jnp.bfloat16), values, preferred_element_type=jnp.float32)
-            o_ref[:, lanes] = (mixed / total).astype(jnp.bfloat16)
-            for place, part in enumerate(split_three(peak * factor + jnp.log2(total))):
-                stats[block] = jnp.where(
-                    lane == head * 3 + place, part.astype(jnp.float32), stats[block]
-                )
-    for block, o_ref in enumerate((o0_ref, o1_ref, o2_ref, o3_ref)):
-        o_ref[:, 384:512] = stats[block].astype(jnp.bfloat16)
+        logits = lax.dot_general(
+            q_ref[:, lanes], keys, (((1,), (1,)), ((), ())), preferred_element_type=jnp.float32
+        )
+        peak = jnp.max(logits, axis=-1, keepdims=True)
+        terms = jnp.exp2((logits - peak) * factor)
+        total = jnp.sum(terms, axis=-1, keepdims=True)
+        mixed = jnp.dot(terms.astype(jnp.bfloat16), values, preferred_element_type=jnp.float32)
+        o_ref[0:128, lanes] = (mixed / total).astype(jnp.bfloat16)
+        for place, part in enumerate(split_three(peak * factor + jnp.log2(total))):
+            stat = jnp.where(lane == head * 3 + place, part.astype(jnp.float32), stat)
+    o_ref[128:144, 0:HD] = stat.T[0:16].astype(jnp.bfloat16)
+    o_ref[128:144, HD:384] = jnp.zeros((16, 2 * HD), jnp.bfloat16)
 
 
 def combine_kernel(p0_ref, p1_ref, p2_ref, p3_ref, image_ref, kept_ref, sent_ref):
     parts = (p0_ref, p1_ref, p2_ref, p3_ref)
     first = image_ref[0] == 0
-    stats = [ref[:, 384:512].astype(jnp.float32) for ref in parts]
+    blank = jnp.zeros((112, HD), jnp.float32)
+    stats = [
+        jnp.concatenate([ref[128:144, 0:HD].astype(jnp.float32), blank], axis=0).T for ref in parts
+    ]
     for head in range(3):
         lanes = slice(head * HD, head * HD + HD)
         sizes = [
@@ -199,9 +200,9 @@
         top = jnp.maximum(jnp.maximum(sizes[0], sizes[1]), jnp.maximum(sizes[2], sizes[3]))
         shares = [jnp.exp2(size - top) for size in sizes]
         whole = shares[0] + shares[1] + shares[2] + shares[3]
-        mixed = shares[0] * parts[0][:, lanes].astype(jnp.float32)
+        mixed = shares[0] * parts[0][0:128, lanes].astype(jnp.float32)
         for share, ref in zip(shares[1:], parts[1:]):
-            mixed = mixed + share * ref[:, lanes].astype(jnp.float32)
+            mixed = mixed + share * ref[0:128, lanes].astype(jnp.float32)
         mixed = (mixed / whole).astype(jnp.bfloat16)
         kept_ref[:, lanes] = jnp.where(first, mixed[:64], mixed[64:])
         sent_ref[:, lanes] = jnp.where(first, mixed[64:], mixed[:64])
@@ -268,8 +269,8 @@
 
     line = jnp.concatenate(
         [
-            jnp.concatenate([by_part[0], by_part[1], by_part[2], columns[:, :256]], axis=1),
-            jnp.concatenate([got[0], got[1], got[2], columns[:, 128:]], axis=1),
+            jnp.concatenate([columns[:, :256], by_part[0], by_part[1], by_part[2]], axis=1),
+            jnp.concatenate([columns[:, 128:], got[0], got[1], got[2]], axis=1),
         ],
         axis=0,
     )
@@ -289,15 +290,23 @@
     columns = pl.pallas_call(
         column_kernel,
         out_shape=shape(8, 48, 384),
-        grid=(2,),
-        in_specs=[pl.BlockSpec((8, 96, HD), lambda step: (0, 0, 9 + step))],
+        grid=(1,),
+        in_specs=[pl.BlockSpec((8, 96, 2 * HD), lambda step: (0, 0, 0))],
         out_specs=pl.BlockSpec((8, 48, 384), lambda step: (0, 0, 0)),
         compiler_params=pltpu.CompilerParams(vmem_limit_bytes=WIDE_BYTES),
     )(weights)
     normed, columns = lax.optimization_barrier((normed, columns))
-    columns = lax.all_gather(columns, YX, axis=0)
+    columns = lax.all_gather(columns.reshape(384, 384), YX, axis=0, tiled=True)
     partial = call(
-        project_kernel, shape(4, 128, 1152), (normed, weights), flops=2 * 512 * 768 * 1152
+        project_kernel,
+        shape(4, 128, 1152),
+        (normed, weights),
+        scratch=[
+            pltpu.VMEM((3, 8, 96, 384), jnp.bfloat16),
+            pltpu.SemaphoreType.DMA((3,)),
+        ],
+        far=(1,),
+        flops=2 * 512 * 768 * 1152,
     )
     partial = lax.all_to_all(partial, X, 0, 0, tiled=True)
 
@@ -319,20 +328,17 @@
     )
     kv_pair = jnp.stack([kv_pair, lax.ppermute(kv_pair, "zi", swap)])
     far_queries = [
-        lax.ppermute(queries, "zo", [(i, (i + k) % 4) for i in range(4)]) for k in (1, 2, 3)
+        lax.ppermute(queries, "zo", [(i, (i + k) % 4) for i in range(4)]) for k in (2, 1, 3)
     ]
     kv_pair = lax.all_to_all(
         jnp.broadcast_to(kv_pair, (4, 2, 288, 384)), ("yh", "xj"), 0, 0, tiled=True
     ).reshape(8, 288, 384)
-    mixed = call(
-        attend_kernel,
-        (shape(128, 512),) * 4,
-        (queries, *far_queries, kv_pair),
-        flops=4 * 512 * 1152 * 384,
-    )
-    mixed = [mixed[0]] + [
-        lax.ppermute(mixed[k], "zo", [(i, (i - k) % 4) for i in range(4)]) for k in (1, 2, 3)
-    ]
+    mixed = []
+    for k, block in enumerate((*far_queries, queries)):
+        part = call(attend_kernel, shape(144, 384), (block, kv_pair), flops=4 * 128 * 1152 * 384)
+        if k < 3:
+            part = lax.ppermute(part, "zo", [(i, (i - (2, 1, 3)[k]) % 4) for i in range(4)])
+        mixed.append(part)
     own, far = call(combine_kernel, (shape(64, 384),) * 2, (*mixed, image_at), scalars=(4,))
     far = lax.ppermute(far, "xi", swap)
     attended = jnp.where(first, jnp.concatenate([own, far]), jnp.concatenate([far, own]))

time: 155 us -> 153 us (0.987)
  waiting for transfers between devices: 53.7 us -> 50.2 us
    ppermute x3, waiting for transfers between devices: 7.59 us -> 4.42 us  [per_device(): lax.ppermute(part, 'zo', [(i, (i - (2, 1, 3)[k]) % 4) for i in range(4)])]
    all_to_all x1, waiting for transfers between devices: 2.43 us -> 5.51 us  [per_device(): lax.all_to_all(jnp.broadcast_to(kv_pair, (4, 2, 288, 384)), ('yh', 'xj'),...]
    ppermute x3, waiting for transfers between devices: 4.74 us -> 1.66 us  [per_device(): lax.ppermute(queries, 'zo', [(i, (i + k) % 4) for i in range(4)])]
    pallas_call x8 -> x11, Pallas kernels: 13.5 us -> 14.6 us  [call(): pl.pallas_call(kernel, out_shape=out_shapes, in_specs=[pl.BlockSpec(memor...]
  transfers between devices with their start and end apart: 16 -> 16, of which waited for: 11 -> 8; matrix products, arithmetic and copies ran while one was open for 3% -> 3% of each run, Pallas kernels for 9% -> 10%
where the time goes in v4:
time: 153 us; the launch traced here: 152 us
  waiting for transfers between devices  50.2 us (33%)
  blocking collectives  32.6 us (21%)
  starting transfers between devices  32.5 us (21%)
  Pallas kernels  16.5 us (11%)
  between operations  13.6 us (9%)
  local copies, waits for them, and re-layouts  5.02 us (3%)
  other arithmetic  1.6 us (1%)
    all_gather x1, waiting for transfers between devices, per_device(): weights = lax.all_gather(line, Z, axis=0)  21.1 us
    all_gather x1, blocking collectives, per_device(): attended = lax.all_gather(attended, H, axis=0)  19.1 us
    pallas_call x11, Pallas kernels, call(): pl.pallas_call(kernel, out_shape=out_shapes, in_specs=[pl.BlockSpec(memor...  14.6 us
    all_gather x1, blocking collectives, per_device(): rows = lax.all_gather(rows, H, axis=0)  13.4 us
    all_to_all x1, waiting for transfers between devices, per_device(): partial = lax.all_to_all(partial, X, 0, 0, tiled=True)  8.97 us
    all_to_all x1, starting transfers between devices, per_device(): lax.all_to_all(jnp.broadcast_to(kv_pair, (4, 2, 288, 384)), ('yh', 'xj'),...  6.63 us
    ppermute x3, starting transfers between devices, per_device(): lax.ppermute(queries, 'zo', [(i, (i + k) % 4) for i in range(4)])  6 us
    ppermute x3, starting transfers between devices, per_device(): lax.ppermute(part, 'zo', [(i, (i - (2, 1, 3)[k]) % 4) for i in range(4)])  5.88 us
  transfers between devices with their start and end apart: 16, of which 8 were waited for; matrix products, arithmetic and copies ran while one was open for 3% of the time, Pallas kernels for 10%

profile of v4, /device:TPU:7, one launch (start us, length us, event | category | flops | bytes accessed | tf_op | source)
XLA Modules:
  0.0 152.0 jit_solution(14322458129623110866)
XLA Ops:
  6.5 0.0 copy-start
  6.5 0.0 all-gather.7.cloned.1.call-start
  6.5 2.9 %collective-permute-start.1 = (bf16[3,48,384]{2,1,0:T(8,128)(2,1)}, bf16[3,48,384]{2,1,0:T(8,128)(2,1)S(1)}, u32[]{:S(2)}, u32[]{:S(2)}) collective-permute-start(bf16[3,48,384]{2,1,0:T(8,128)(2,1)} %bitcast.61), channel_id=1, source_target_pairs={{0,128},{128,0},{1,129},{129,1},{2,130},{130,2},{3,131},{131,3},{4... | collective-permute-start | bytes 331784 | tf_op jit(solution)/shard_map/ppermute | solution.py:258
  9.5 1.4 collective-permute-start
  10.9 0.8 slice_bitcast_fusion.5
  11.7 1.8 %shard_map.100 = (bf16[144,768]{1,0:T(8,128)(2,1)}, f32[16,768]{1,0:T(8,128)}) custom-call(bf16[128,768]{1,0:T(8,128)(2,1)} %bitcast.59, bf16[3,28,768]{2,1,0:T(8,128)(2,1)} %bitcast.60, s32[2]{0:T(128)} %steps_ref.1), custom_call_target="tpu_custom_call" | custom-call | tf_op jit(solution)/shard_map/pallas_call | solution.py:22
  13.5 0.0 collective-permute-done
  13.5 0.0 collective-permute-done.1
  13.5 0.7 maximum_maximum_fusion
  14.3 0.0 all-gather.7.cloned.1.call-update
  14.3 0.7 fusion.10
  15.0 0.1 copy.16
  15.1 0.0 copy-done
  15.2 0.6 collective-permute-start.2
  15.8 13.4 %all-gather = bf16[576,768]{1,0:T(8,128)(2,1)S(1)} all-gather(bf16[144,768]{1,0:T(8,128)(2,1)} %get-tuple-element.16), channel_id=2, replica_groups=mesh['yh'=2,'xj'=2,'xi'=2,'zo'=4,'zi'=2,'yl'=2,'c'=2] {'yl','c'}, dimensions={0}, use_global_device_ids=true | all-gather | bytes 1105920 | tf_op jit(solution)/shard_map/all_gather | solution.py:286
  29.3 0.0 collective-permute-done.2.got_ref
  29.3 1.5 %shard_map.101 = bf16[4,128,768]{2,1,0:T(8,128)(2,1)} custom-call(bf16[4,144,768]{2,1,0:T(8,128)(2,1)S(1)} %bitcast.51, s32[1]{0:T(128)} %bitcast.16.y_ref), custom_call_target="tpu_custom_call" | custom-call | tf_op jit(solution)/shard_map/pallas_call | solution.py:22
  30.8 4.6 %all-to-all-start = ((bf16[4,128,768]{2,1,0:T(8,128)(2,1)}), bf16[4,128,768]{2,1,0:T(8,128)(2,1)S(1)}, u32[]{:S(2)}, u32[]{:S(2)}) async-start(bf16[4,128,768]{2,1,0:T(8,128)(2,1)} %shard_map.101), calls=%async_computation | async-start | bytes 1572864 | tf_op jit(solution)/shard_map/all_to_all | solution.py:289
  35.4 0.0 all-gather.5.cloned.1.call-start
  35.4 21.1 %all-gather.7.cloned.1.call-done = bf16[768,1408]{1,0:T(8,128)(2,1)} async-done(((bf16[96,1408]{1,0:T(8,128)(2,1)}), bf16[768,1408]{1,0:T(8,128)(2,1)}) %all-gather.7.cloned.1.call-update) | async-done | bytes 2162704 | tf_op jit(solution)/shard_map/all_gather | solution.py:278
  56.5 0.0 copy-start.1
  56.5 1.9 %shard_map.102 = bf16[8,48,384]{2,1,0:T(8,128)(2,1)} custom-call(bf16[8,96,1408]{2,1,0:T(8,128)(2,1)} %bitcast.49), custom_call_target="tpu_custom_call" | custom-call | tf_op jit(solution)/shard_map/pallas_call | solution.py:290
  58.4 0.0 all-to-all-done.rows_ref
  58.4 0.0 all-gather.5.cloned.1.call-update
  58.4 0.0 copy-done.1
  58.4 3.3 %shard_map.103 = bf16[4,128,1152]{2,1,0:T(8,128)(2,1)} custom-call(bf16[4,128,768]{2,1,0:T(8,128)(2,1)S(1)} %all-to-all-done.rows_ref, bf16[8,96,1408]{2,1,0:T(8,128)(2,1)S(1)} %bitcast.50), custom_call_target="tpu_custom_call" | custom-call | flops 905969664 | tf_op jit(solution)/shard_map/pallas_call | solution.py:22
  61.7 0.0 copy-start.4
  61.7 4.2 %all-to-all-start.1 = ((bf16[4,128,1152]{2,1,0:T(8,128)(2,1)}), bf16[4,128,1152]{2,1,0:T(8,128)(2,1)S(1)}, u32[]{:S(2)}, u32[]{:S(2)}) async-start(bf16[4,128,1152]{2,1,0:T(8,128)(2,1)} %shard_map.103), calls=%async_computation.1 | async-start | bytes 2359296 | tf_op jit(solution)/shard_map/all_to_all | solution.py:311
  66.0 1.0 dynamic-slice_bitcast_fusion.1
  67.0 9.0 %all-to-all-done.1.part_ref = bf16[4,128,1152]{2,1,0:T(8,128)(2,1)S(1)} async-done(((bf16[4,128,1152]{2,1,0:T(8,128)(2,1)}), bf16[4,128,1152]{2,1,0:T(8,128)(2,1)S(1)}, u32[]{:S(2)}, u32[]{:S(2)}) %all-to-all-start.1) | async-done | bytes 1179680 | tf_op jit(solution)/shard_map/all_to_all | solution.py:311
  76.0 0.0 copy-done.4
  76.0 0.4 shard_map.105
  76.3 0.1 collective-permute-start.4
  76.4 5.2 %collective-permute-done.4 = bf16[288,384]{1,0:T(8,128)(2,1)S(1)} collective-permute-done((bf16[288,384]{1,0:T(8,128)(2,1)S(1)}, bf16[288,384]{1,0:T(8,128)(2,1)S(1)}, u32[]{:S(2)}, u32[]{:S(2)}) %collective-permute-start.4) | collective-permute-done | bytes 221216 | tf_op jit(solution)/shard_map/ppermute | solution.py:329
  81.6 0.1 pad_maximum_fusion
  81.7 1.4 broadcast_in_dim.53
  83.0 6.6 %all-to-all-start.2 = ((bf16[4,2,288,384]{3,2,1,0:T(8,128)(2,1)}), bf16[4,2,288,384]{3,2,1,0:T(8,128)(2,1)S(1)}, u32[]{:S(2)}, u32[]{:S(2)}) async-start(bf16[4,2,288,384]{3,2,1,0:T(8,128)(2,1)} %broadcast_in_dim.53), calls=%async_computation.2 | async-start | bytes 3538944 | tf_op jit(solution)/shard_map/all_to_all | solution.py:333
  89.7 0.0 copy-done.5
  89.7 0.1 shard_map.104.q_ref
  89.8 2.4 %collective-permute-start.3 = (bf16[128,384]{1,0:T(8,128)(2,1)S(1)}, bf16[128,384]{1,0:T(8,128)(2,1)S(1)}, u32[]{:S(2)}, u32[]{:S(2)}) collective-permute-start(bf16[128,384]{1,0:T(8,128)(2,1)S(1)} %shard_map.104.q_ref), channel_id=1, source_target_pairs={{0,16},{8,24},{16,0},{24,8},{1,17},{9,25},{17,1},{25,9},{2,18},{10... | collective-permute-start | bytes 294920 | tf_op jit(solution)/shard_map/ppermute | solution.py:331
  92.3 1.6 %collective-permute-start.6 = (bf16[128,384]{1,0:T(8,128)(2,1)S(1)}, bf16[128,384]{1,0:T(8,128)(2,1)S(1)}, u32[]{:S(2)}, u32[]{:S(2)}) collective-permute-start(bf16[128,384]{1,0:T(8,128)(2,1)S(1)} %shard_map.104.q_ref), channel_id=1, source_target_pairs={{0,8},{8,16},{16,24},{24,0},{1,9},{9,17},{17,25},{25,1},{2,10},{10... | collective-permute-start | bytes 294920 | tf_op jit(solution)/shard_map/ppermute | solution.py:331
  93.8 2.0 %collective-permute-start.8 = (bf16[128,384]{1,0:T(8,128)(2,1)S(1)}, bf16[128,384]{1,0:T(8,128)(2,1)S(1)}, u32[]{:S(2)}, u32[]{:S(2)}) collective-permute-start(bf16[128,384]{1,0:T(8,128)(2,1)S(1)} %shard_map.104.q_ref), channel_id=1, source_target_pairs={{0,24},{8,0},{16,8},{24,16},{1,25},{9,1},{17,9},{25,17},{2,26},{10... | collective-permute-start | bytes 294920 | tf_op jit(solution)/shard_map/ppermute | solution.py:331
  95.8 1.7 %collective-permute-done.3.q_ref = bf16[128,384]{1,0:T(8,128)(2,1)S(1)} collective-permute-done((bf16[128,384]{1,0:T(8,128)(2,1)S(1)}, bf16[128,384]{1,0:T(8,128)(2,1)S(1)}, u32[]{:S(2)}, u32[]{:S(2)}) %collective-permute-start.3) | collective-permute-done | bytes 98336 | tf_op jit(solution)/shard_map/ppermute | solution.py:331
  97.5 5.5 %all-to-all-done.2 = bf16[4,2,288,384]{3,2,1,0:T(8,128)(2,1)S(1)} async-done(((bf16[4,2,288,384]{3,2,1,0:T(8,128)(2,1)}), bf16[4,2,288,384]{3,2,1,0:T(8,128)(2,1)S(1)}, u32[]{:S(2)}, u32[]{:S(2)}) %all-to-all-start.2) | async-done | bytes 1769504 | tf_op jit(solution)/shard_map/all_to_all | solution.py:333
  103.0 1.3 shard_map.106
  104.4 2.5 %collective-permute-start.5 = (bf16[144,384]{1,0:T(8,128)(2,1)S(1)}, bf16[144,384]{1,0:T(8,128)(2,1)S(1)}, u32[]{:S(2)}, u32[]{:S(2)}) collective-permute-start(bf16[144,384]{1,0:T(8,128)(2,1)S(1)} %shard_map.106), channel_id=1, source_target_pairs={{0,16},{8,24},{16,0},{24,8},{1,17},{9,25},{17,1},{25,9},{2,18},{10... | collective-permute-start | bytes 331784 | tf_op jit(solution)/shard_map/ppermute | solution.py:340
  106.9 0.0 collective-permute-done.6.q_ref
  106.9 1.3 shard_map.107
  108.2 0.0 copy-start.3
  108.3 3.3 %collective-permute-start.7 = (bf16[144,384]{1,0:T(8,128)(2,1)S(1)}, bf16[144,384]{1,0:T(8,128)(2,1)S(1)}, u32[]{:S(2)}, u32[]{:S(2)}) collective-permute-start(bf16[144,384]{1,0:T(8,128)(2,1)S(1)} %shard_map.107), channel_id=1, source_target_pairs={{0,24},{8,0},{16,8},{24,16},{1,25},{9,1},{17,9},{25,17},{2,26},{10... | collective-permute-start | bytes 331784 | tf_op jit(solution)/shard_map/ppermute | solution.py:340
  111.5 0.0 collective-permute-done.8.q_ref
  111.5 1.4 shard_map.108
  112.9 0.1 collective-permute-start.9
  113.0 1.3 shard_map.109.p3_ref
  114.3 0.0 collective-permute-done.5.p0_ref
  114.3 0.2 collective-permute-done.7.p1_ref
  114.5 4.2 %collective-permute-done.9.p2_ref = bf16[144,384]{1,0:T(8,128)(2,1)S(1)} collective-permute-done((bf16[144,384]{1,0:T(8,128)(2,1)S(1)}, bf16[144,384]{1,0:T(8,128)(2,1)S(1)}, u32[]{:S(2)}, u32[]{:S(2)}) %collective-permute-start.9) | collective-permute-done | bytes 110624 | tf_op jit(solution)/shard_map/ppermute | solution.py:340
  118.8 0.6 shard_map.110
  119.3 0.1 collective-permute-start.10
  119.4 3.3 %collective-permute-done.10 = bf16[64,384]{1,0:T(8,128)(2,1)S(1)} collective-permute-done((bf16[64,384]{1,0:T(8,128)(2,1)S(1)}, bf16[64,384]{1,0:T(8,128)(2,1)S(1)}, u32[]{:S(2)}, u32[]{:S(2)}) %collective-permute-start.10) | collective-permute-done | bytes 49184 | tf_op jit(solution)/shard_map/ppermute | solution.py:343
  122.8 19.1 %all_gather.23.attended_ref = bf16[4,128,384]{2,1,0:T(8,128)(2,1)S(1)} all-gather(bf16[1,128,384]{2,1,0:T(8,128)(2,1)S(1)} %maximum_select_fusion), channel_id=1, replica_groups=mesh['yh'=2,'xj'=2,'xi'=2,'zo'=4,'zi'=2,'yl'=2,'c'=2] {'yl','c'}, dimensions={0}, use_global_device_ids=true | all-gather | bytes 491520 | tf_op jit(solution)/shard_map/all_gather | solution.py:345
  141.9 0.0 copy-done.3
  141.9 1.7 %copy-done.2 = bf16[3072,384]{1,0:T(8,128)(2,1)S(1)} copy-done((bf16[3072,384]{1,0:T(8,128)(2,1)S(1)}, bf16[3072,384]{1,0:T(8,128)(2,1)}, u32[]{:S(2)}) %copy-start.2) | copy-done | bytes 2359320
  143.6 1.6 %shard_map.111 = bf16[2,64,768]{2,1,0:T(8,128)(2,1)} custom-call(bf16[4,128,384]{2,1,0:T(8,128)(2,1)S(1)} %all_gather.23.attended_ref, bf16[4,2,8,48,384]{4,3,2,1,0:T(8,128)(2,1)S(1)} %bitcast.52, f32[16,768]{1,0:T(8,128)S(1)} %copy-done.3), custom_call_target="tpu_custom_call" | custom-call | flops 301989888 | tf_op jit(solution)/shard_map/pallas_call | solution.py:22
  (10 shorter events, 0.1 us)
Async XLA Ops:
  6.5 8.6 %copy-start = (bf16[2,2,8,384]{3,2,1,0:T(8,128)(2,1)S(1)}, bf16[2,2,8,384]{3,2,1,0:T(8,128)(2,1)}, u32[]{:S(2)}) copy-start(bf16[2,2,8,384]{3,2,1,0:T(8,128)(2,1)} %param.11) | copy-start | bytes 73732
  6.5 50.0 %all-gather.7.cloned.1.call-start = ((), (), s32[]{:S(2)}) async-start(), calls=%async_computation.4 | async-start | bytes 2433024 | tf_op jit(solution)/shard_map/all_gather | solution.py:278
  6.5 6.9 %collective-permute-start.1 = (bf16[3,48,384]{2,1,0:T(8,128)(2,1)}, bf16[3,48,384]{2,1,0:T(8,128)(2,1)S(1)}, u32[]{:S(2)}, u32[]{:S(2)}) collective-permute-start(bf16[3,48,384]{2,1,0:T(8,128)(2,1)} %bitcast.61), channel_id=1, source_target_pairs={{0,128},{128,0},{1,129},{129,1},{2,130},{130,2},{3,131},{131,3},{4... | collective-permute-start | bytes 331784 | tf_op jit(solution)/shard_map/ppermute | solution.py:258
  9.5 4.0 %collective-permute-start = (bf16[48,384]{1,0:T(8,128)(2,1)}, bf16[48,384]{1,0:T(8,128)(2,1)S(1)}, u32[]{:S(2)}, u32[]{:S(2)}) collective-permute-start(bf16[48,384]{1,0:T(8,128)(2,1)} %bitcast.65), channel_id=1, source_target_pairs={{0,0},{1,64},{2,128},{3,192},{32,32},{33,96},{34,160},{35,224},{64... | collective-permute-start | bytes 110600 | tf_op jit(solution)/shard_map/ppermute | solution.py:268
  15.2 14.1 %collective-permute-start.2 = (bf16[80,384]{1,0:T(8,128)(2,1)S(1)}, bf16[80,384]{1,0:T(8,128)(2,1)S(1)}, u32[]{:S(2)}, u32[]{:S(2)}) collective-permute-start(bf16[80,384]{1,0:T(8,128)(2,1)S(1)} %get-tuple-element.28), channel_id=1, source_target_pairs={{0,32},{32,0},{1,33},{33,1},{2,34},{34,2},{3,35},{35,3},{4,36},{36... | collective-permute-start | bytes 184328 | tf_op jit(solution)/shard_map/ppermute | solution.py:285
  30.8 27.6 %all-to-all-start = ((bf16[4,128,768]{2,1,0:T(8,128)(2,1)}), bf16[4,128,768]{2,1,0:T(8,128)(2,1)S(1)}, u32[]{:S(2)}, u32[]{:S(2)}) async-start(bf16[4,128,768]{2,1,0:T(8,128)(2,1)} %shard_map.101), calls=%async_computation | async-start | bytes 1572864 | tf_op jit(solution)/shard_map/all_to_all | solution.py:289
  35.4 106.5 %all-gather.5.cloned.1.call-start = ((), (), s32[]{:S(2)}) async-start(), calls=%async_computation.3 | async-start | bytes 2654208 | tf_op jit(solution)/shard_map/all_gather | solution.py:299
  56.5 1.9 %copy-start.1 = (bf16[768,1408]{1,0:T(8,128)(2,1)S(1)}, bf16[768,1408]{1,0:T(8,128)(2,1)}, u32[]{:S(2)}) copy-start(bf16[768,1408]{1,0:T(8,128)(2,1)} %all-gather.7.cloned.1.call-done) | copy-start | bytes 6488068
  61.7 14.3 %copy-start.4 = (f32[128]{0:T(128)S(1)}, f32[128]{0:T(128)}, u32[]{:S(2)}) copy-start(f32[128]{0:T(128)} %param.19) | copy-start | bytes 1540
  61.7 14.2 %all-to-all-start.1 = ((bf16[4,128,1152]{2,1,0:T(8,128)(2,1)}), bf16[4,128,1152]{2,1,0:T(8,128)(2,1)S(1)}, u32[]{:S(2)}, u32[]{:S(2)}) async-start(bf16[4,128,1152]{2,1,0:T(8,128)(2,1)} %shard_map.103), calls=%async_computation.1 | async-start | bytes 2359296 | tf_op jit(solution)/shard_map/all_to_all | solution.py:311
  76.3 5.3 %collective-permute-start.4 = (bf16[288,384]{1,0:T(8,128)(2,1)S(1)}, bf16[288,384]{1,0:T(8,128)(2,1)S(1)}, u32[]{:S(2)}, u32[]{:S(2)}) collective-permute-start(bf16[288,384]{1,0:T(8,128)(2,1)S(1)} %shard_map.105), channel_id=1, source_target_pairs={{0,4},{4,0},{1,5},{5,1},{2,6},{6,2},{3,7},{7,3},{8,12},{12,8},{9,1... | collective-permute-start | bytes 663560 | tf_op jit(solution)/shard_map/ppermute | solution.py:329
  83.0 6.6 %copy-start.5 = (f32[128]{0:T(128)S(1)}, f32[128]{0:T(128)}, u32[]{:S(2)}) copy-start(f32[128]{0:T(128)} %param.18) | copy-start | bytes 1540
  83.0 20.0 %all-to-all-start.2 = ((bf16[4,2,288,384]{3,2,1,0:T(8,128)(2,1)}), bf16[4,2,288,384]{3,2,1,0:T(8,128)(2,1)S(1)}, u32[]{:S(2)}, u32[]{:S(2)}) async-start(bf16[4,2,288,384]{3,2,1,0:T(8,128)(2,1)} %broadcast_in_dim.53), calls=%async_computation.2 | async-start | bytes 3538944 | tf_op jit(solution)/shard_map/all_to_all | solution.py:333
  89.8 7.7 %collective-permute-start.3 = (bf16[128,384]{1,0:T(8,128)(2,1)S(1)}, bf16[128,384]{1,0:T(8,128)(2,1)S(1)}, u32[]{:S(2)}, u32[]{:S(2)}) collective-permute-start(bf16[128,384]{1,0:T(8,128)(2,1)S(1)} %shard_map.104.q_ref), channel_id=1, source_target_pairs={{0,16},{8,24},{16,0},{24,8},{1,17},{9,25},{17,1},{25,9},{2,18},{10... | collective-permute-start | bytes 294920 | tf_op jit(solution)/shard_map/ppermute | solution.py:331
  92.3 14.6 %collective-permute-start.6 = (bf16[128,384]{1,0:T(8,128)(2,1)S(1)}, bf16[128,384]{1,0:T(8,128)(2,1)S(1)}, u32[]{:S(2)}, u32[]{:S(2)}) collective-permute-start(bf16[128,384]{1,0:T(8,128)(2,1)S(1)} %shard_map.104.q_ref), channel_id=1, source_target_pairs={{0,8},{8,16},{16,24},{24,0},{1,9},{9,17},{17,25},{25,1},{2,10},{10... | collective-permute-start | bytes 294920 | tf_op jit(solution)/shard_map/ppermute | solution.py:331
  93.8 17.7 %collective-permute-start.8 = (bf16[128,384]{1,0:T(8,128)(2,1)S(1)}, bf16[128,384]{1,0:T(8,128)(2,1)S(1)}, u32[]{:S(2)}, u32[]{:S(2)}) collective-permute-start(bf16[128,384]{1,0:T(8,128)(2,1)S(1)} %shard_map.104.q_ref), channel_id=1, source_target_pairs={{0,24},{8,0},{16,8},{24,16},{1,25},{9,1},{17,9},{25,17},{2,26},{10... | collective-permute-start | bytes 294920 | tf_op jit(solution)/shard_map/ppermute | solution.py:331
  104.4 10.0 %collective-permute-start.5 = (bf16[144,384]{1,0:T(8,128)(2,1)S(1)}, bf16[144,384]{1,0:T(8,128)(2,1)S(1)}, u32[]{:S(2)}, u32[]{:S(2)}) collective-permute-start(bf16[144,384]{1,0:T(8,128)(2,1)S(1)} %shard_map.106), channel_id=1, source_target_pairs={{0,16},{8,24},{16,0},{24,8},{1,17},{9,25},{17,1},{25,9},{2,18},{10... | collective-permute-start | bytes 331784 | tf_op jit(solution)/shard_map/ppermute | solution.py:340
  108.2 33.7 %copy-start.3 = (f32[16,768]{1,0:T(8,128)S(1)}, f32[16,768]{1,0:T(8,128)}, u32[]{:S(2)}) copy-start(f32[16,768]{1,0:T(8,128)} %get-tuple-element.24.gate_ref) | copy-start | bytes 147460
  108.3 6.3 %collective-permute-start.7 = (bf16[144,384]{1,0:T(8,128)(2,1)S(1)}, bf16[144,384]{1,0:T(8,128)(2,1)S(1)}, u32[]{:S(2)}, u32[]{:S(2)}) collective-permute-start(bf16[144,384]{1,0:T(8,128)(2,1)S(1)} %shard_map.107), channel_id=1, source_target_pairs={{0,24},{8,0},{16,8},{24,16},{1,25},{9,1},{17,9},{25,17},{2,26},{10... | collective-permute-start | bytes 331784 | tf_op jit(solution)/shard_map/ppermute | solution.py:340
  112.9 5.9 %collective-permute-start.9 = (bf16[144,384]{1,0:T(8,128)(2,1)S(1)}, bf16[144,384]{1,0:T(8,128)(2,1)S(1)}, u32[]{:S(2)}, u32[]{:S(2)}) collective-permute-start(bf16[144,384]{1,0:T(8,128)(2,1)S(1)} %shard_map.108), channel_id=1, source_target_pairs={{0,8},{8,16},{16,24},{24,0},{1,9},{9,17},{17,25},{25,1},{2,10},{10... | collective-permute-start | bytes 331784 | tf_op jit(solution)/shard_map/ppermute | solution.py:340
  119.3 3.4 %collective-permute-start.10 = (bf16[64,384]{1,0:T(8,128)(2,1)S(1)}, bf16[64,384]{1,0:T(8,128)(2,1)S(1)}, u32[]{:S(2)}, u32[]{:S(2)}) collective-permute-start(bf16[64,384]{1,0:T(8,128)(2,1)S(1)} %get-tuple-element.22), channel_id=1, source_target_pairs={{0,32},{32,0},{1,33},{33,1},{2,34},{34,2},{3,35},{35,3},{4,36},{36... | collective-permute-start | bytes 147464 | tf_op jit(solution)/shard_map/ppermute | solution.py:343
  141.9 1.7 %copy-start.2 = (bf16[3072,384]{1,0:T(8,128)(2,1)S(1)}, bf16[3072,384]{1,0:T(8,128)(2,1)}, u32[]{:S(2)}) copy-start(bf16[3072,384]{1,0:T(8,128)(2,1)} %all-gather.5.cloned.1.call-done) | copy-start | bytes 7077892
Sparse Core Ops, SparseCore 0:
  14.4 42.0 all-gather.6
  59.1 80.2 all-gather.4

commit v5 on v4

--- a/solution.py
+++ b/solution.py
@@ -59,9 +59,10 @@
 def norm_kernel(rows_ref, y_ref, out_ref):
     features = 4 * 768
     lower = y_ref[0] == 0
+    modulation = rows_ref[:, 128:144, :].astype(jnp.float32)
     for image in range(2):
-        shift = rows_ref[:, 128 + 2 * image : 129 + 2 * image, :].astype(jnp.float32)
-        scale = 1.0 + rows_ref[:, 129 + 2 * image : 130 + 2 * image, :].astype(jnp.float32)
+        shift = modulation[:, 2 * image : 2 * image + 1]
+        scale = 1.0 + modulation[:, 2 * image + 1 : 2 * image + 2]
         for start in range(0, 64, 16):
             at = image * 64 + start
             hidden = rows_ref[:, at : at + 16, :].astype(jnp.float32)

time: 153 us -> 153 us (level)
  no operation moved by 1% of the time
where the time goes in v5:
time: 153 us; the launch traced here: 152 us
  waiting for transfers between devices  50.2 us (33%)
  blocking collectives  32.6 us (21%)
  starting transfers between devices  32.5 us (21%)
  Pallas kernels  16.5 us (11%)
  between operations  13.6 us (9%)
  local copies, waits for them, and re-layouts  5.02 us (3%)
  other arithmetic  1.6 us (1%)
    all_gather x1, waiting for transfers between devices, per_device(): weights = lax.all_gather(line, Z, axis=0)  21.1 us
    all_gather x1, blocking collectives, per_device(): attended = lax.all_gather(attended, H, axis=0)  19.1 us
    pallas_call x11, Pallas kernels, call(): pl.pallas_call(kernel, out_shape=out_shapes, in_specs=[pl.BlockSpec(memor...  14.6 us
    all_gather x1, blocking collectives, per_device(): rows = lax.all_gather(rows, H, axis=0)  13.4 us
    all_to_all x1, waiting for transfers between devices, per_device(): partial = lax.all_to_all(partial, X, 0, 0, tiled=True)  8.97 us
    all_to_all x1, starting transfers between devices, per_device(): lax.all_to_all(jnp.broadcast_to(kv_pair, (4, 2, 288, 384)), ('yh', 'xj'),...  6.63 us
    ppermute x3, starting transfers between devices, per_device(): lax.ppermute(queries, 'zo', [(i, (i + k) % 4) for i in range(4)])  6 us
    ppermute x3, starting transfers between devices, per_device(): lax.ppermute(part, 'zo', [(i, (i - (2, 1, 3)[k]) % 4) for i in range(4)])  5.88 us
  transfers between devices with their start and end apart: 16, of which 8 were waited for; matrix products, arithmetic and copies ran while one was open for 3% of the time, Pallas kernels for 10%

profile of v5, /device:TPU:7, one launch (start us, length us, event | category | flops | bytes accessed | tf_op | source)
XLA Modules:
  0.0 152.0 jit_solution(12597991146871408563)
XLA Ops:
  6.5 0.0 copy-start
  6.5 0.0 all-gather.7.cloned.1.call-start
  6.5 2.9 %collective-permute-start.1 = (bf16[3,48,384]{2,1,0:T(8,128)(2,1)}, bf16[3,48,384]{2,1,0:T(8,128)(2,1)S(1)}, u32[]{:S(2)}, u32[]{:S(2)}) collective-permute-start(bf16[3,48,384]{2,1,0:T(8,128)(2,1)} %bitcast.61), channel_id=1, source_target_pairs={{0,128},{128,0},{1,129},{129,1},{2,130},{130,2},{3,131},{131,3},{4... | collective-permute-start | bytes 331784 | tf_op jit(solution)/shard_map/ppermute | solution.py:259
  9.5 1.4 collective-permute-start
  10.9 0.8 slice_bitcast_fusion.5
  11.7 1.8 %shard_map.100 = (bf16[144,768]{1,0:T(8,128)(2,1)}, f32[16,768]{1,0:T(8,128)}) custom-call(bf16[128,768]{1,0:T(8,128)(2,1)} %bitcast.59, bf16[3,28,768]{2,1,0:T(8,128)(2,1)} %bitcast.60, s32[2]{0:T(128)} %steps_ref.1), custom_call_target="tpu_custom_call" | custom-call | tf_op jit(solution)/shard_map/pallas_call | solution.py:22
  13.5 0.0 collective-permute-done
  13.5 0.0 collective-permute-done.1
  13.5 0.7 maximum_maximum_fusion
  14.3 0.0 all-gather.7.cloned.1.call-update
  14.3 0.7 fusion.10
  15.0 0.1 copy.16
  15.1 0.0 copy-done
  15.2 0.6 collective-permute-start.2
  15.8 13.4 %all-gather = bf16[576,768]{1,0:T(8,128)(2,1)S(1)} all-gather(bf16[144,768]{1,0:T(8,128)(2,1)} %get-tuple-element.16), channel_id=2, replica_groups=mesh['yh'=2,'xj'=2,'xi'=2,'zo'=4,'zi'=2,'yl'=2,'c'=2] {'yl','c'}, dimensions={0}, use_global_device_ids=true | all-gather | bytes 1105920 | tf_op jit(solution)/shard_map/all_gather | solution.py:287
  29.3 0.0 collective-permute-done.2.got_ref
  29.3 1.5 %shard_map.101 = bf16[4,128,768]{2,1,0:T(8,128)(2,1)} custom-call(bf16[4,144,768]{2,1,0:T(8,128)(2,1)S(1)} %bitcast.51, s32[1]{0:T(128)} %bitcast.16.y_ref), custom_call_target="tpu_custom_call" | custom-call | tf_op jit(solution)/shard_map/pallas_call | solution.py:22
  30.8 4.6 %all-to-all-start = ((bf16[4,128,768]{2,1,0:T(8,128)(2,1)}), bf16[4,128,768]{2,1,0:T(8,128)(2,1)S(1)}, u32[]{:S(2)}, u32[]{:S(2)}) async-start(bf16[4,128,768]{2,1,0:T(8,128)(2,1)} %shard_map.101), calls=%async_computation | async-start | bytes 1572864 | tf_op jit(solution)/shard_map/all_to_all | solution.py:290
  35.4 0.0 all-gather.5.cloned.1.call-start
  35.4 21.1 %all-gather.7.cloned.1.call-done = bf16[768,1408]{1,0:T(8,128)(2,1)} async-done(((bf16[96,1408]{1,0:T(8,128)(2,1)}), bf16[768,1408]{1,0:T(8,128)(2,1)}) %all-gather.7.cloned.1.call-update) | async-done | bytes 2162704 | tf_op jit(solution)/shard_map/all_gather | solution.py:279
  56.5 0.0 copy-start.1
  56.5 1.9 %shard_map.102 = bf16[8,48,384]{2,1,0:T(8,128)(2,1)} custom-call(bf16[8,96,1408]{2,1,0:T(8,128)(2,1)} %bitcast.49), custom_call_target="tpu_custom_call" | custom-call | tf_op jit(solution)/shard_map/pallas_call | solution.py:291
  58.4 0.0 all-to-all-done.rows_ref
  58.4 0.0 all-gather.5.cloned.1.call-update
  58.4 0.0 copy-done.1
  58.4 3.3 %shard_map.103 = bf16[4,128,1152]{2,1,0:T(8,128)(2,1)} custom-call(bf16[4,128,768]{2,1,0:T(8,128)(2,1)S(1)} %all-to-all-done.rows_ref, bf16[8,96,1408]{2,1,0:T(8,128)(2,1)S(1)} %bitcast.50), custom_call_target="tpu_custom_call" | custom-call | flops 905969664 | tf_op jit(solution)/shard_map/pallas_call | solution.py:22
  61.7 0.0 copy-start.4
  61.7 4.2 %all-to-all-start.1 = ((bf16[4,128,1152]{2,1,0:T(8,128)(2,1)}), bf16[4,128,1152]{2,1,0:T(8,128)(2,1)S(1)}, u32[]{:S(2)}, u32[]{:S(2)}) async-start(bf16[4,128,1152]{2,1,0:T(8,128)(2,1)} %shard_map.103), calls=%async_computation.1 | async-start | bytes 2359296 | tf_op jit(solution)/shard_map/all_to_all | solution.py:312
  66.0 1.0 dynamic-slice_bitcast_fusion.1
  67.0 9.0 %all-to-all-done.1.part_ref = bf16[4,128,1152]{2,1,0:T(8,128)(2,1)S(1)} async-done(((bf16[4,128,1152]{2,1,0:T(8,128)(2,1)}), bf16[4,128,1152]{2,1,0:T(8,128)(2,1)S(1)}, u32[]{:S(2)}, u32[]{:S(2)}) %all-to-all-start.1) | async-done | bytes 1179680 | tf_op jit(solution)/shard_map/all_to_all | solution.py:312
  76.0 0.0 copy-done.4
  76.0 0.4 shard_map.105
  76.3 0.1 collective-permute-start.4
  76.4 5.2 %collective-permute-done.4 = bf16[288,384]{1,0:T(8,128)(2,1)S(1)} collective-permute-done((bf16[288,384]{1,0:T(8,128)(2,1)S(1)}, bf16[288,384]{1,0:T(8,128)(2,1)S(1)}, u32[]{:S(2)}, u32[]{:S(2)}) %collective-permute-start.4) | collective-permute-done | bytes 221216 | tf_op jit(solution)/shard_map/ppermute | solution.py:330
  81.6 0.1 pad_maximum_fusion
  81.7 1.4 broadcast_in_dim.53
  83.0 6.6 %all-to-all-start.2 = ((bf16[4,2,288,384]{3,2,1,0:T(8,128)(2,1)}), bf16[4,2,288,384]{3,2,1,0:T(8,128)(2,1)S(1)}, u32[]{:S(2)}, u32[]{:S(2)}) async-start(bf16[4,2,288,384]{3,2,1,0:T(8,128)(2,1)} %broadcast_in_dim.53), calls=%async_computation.2 | async-start | bytes 3538944 | tf_op jit(solution)/shard_map/all_to_all | solution.py:334
  89.7 0.0 copy-done.5
  89.7 0.1 shard_map.104.q_ref
  89.8 2.4 %collective-permute-start.3 = (bf16[128,384]{1,0:T(8,128)(2,1)S(1)}, bf16[128,384]{1,0:T(8,128)(2,1)S(1)}, u32[]{:S(2)}, u32[]{:S(2)}) collective-permute-start(bf16[128,384]{1,0:T(8,128)(2,1)S(1)} %shard_map.104.q_ref), channel_id=1, source_target_pairs={{0,16},{8,24},{16,0},{24,8},{1,17},{9,25},{17,1},{25,9},{2,18},{10... | collective-permute-start | bytes 294920 | tf_op jit(solution)/shard_map/ppermute | solution.py:332
  92.3 1.6 %collective-permute-start.6 = (bf16[128,384]{1,0:T(8,128)(2,1)S(1)}, bf16[128,384]{1,0:T(8,128)(2,1)S(1)}, u32[]{:S(2)}, u32[]{:S(2)}) collective-permute-start(bf16[128,384]{1,0:T(8,128)(2,1)S(1)} %shard_map.104.q_ref), channel_id=1, source_target_pairs={{0,8},{8,16},{16,24},{24,0},{1,9},{9,17},{17,25},{25,1},{2,10},{10... | collective-permute-start | bytes 294920 | tf_op jit(solution)/shard_map/ppermute | solution.py:332
  93.8 2.0 %collective-permute-start.8 = (bf16[128,384]{1,0:T(8,128)(2,1)S(1)}, bf16[128,384]{1,0:T(8,128)(2,1)S(1)}, u32[]{:S(2)}, u32[]{:S(2)}) collective-permute-start(bf16[128,384]{1,0:T(8,128)(2,1)S(1)} %shard_map.104.q_ref), channel_id=1, source_target_pairs={{0,24},{8,0},{16,8},{24,16},{1,25},{9,1},{17,9},{25,17},{2,26},{10... | collective-permute-start | bytes 294920 | tf_op jit(solution)/shard_map/ppermute | solution.py:332
  95.8 1.7 %collective-permute-done.3.q_ref = bf16[128,384]{1,0:T(8,128)(2,1)S(1)} collective-permute-done((bf16[128,384]{1,0:T(8,128)(2,1)S(1)}, bf16[128,384]{1,0:T(8,128)(2,1)S(1)}, u32[]{:S(2)}, u32[]{:S(2)}) %collective-permute-start.3) | collective-permute-done | bytes 98336 | tf_op jit(solution)/shard_map/ppermute | solution.py:332
  97.5 5.5 %all-to-all-done.2 = bf16[4,2,288,384]{3,2,1,0:T(8,128)(2,1)S(1)} async-done(((bf16[4,2,288,384]{3,2,1,0:T(8,128)(2,1)}), bf16[4,2,288,384]{3,2,1,0:T(8,128)(2,1)S(1)}, u32[]{:S(2)}, u32[]{:S(2)}) %all-to-all-start.2) | async-done | bytes 1769504 | tf_op jit(solution)/shard_map/all_to_all | solution.py:334
  103.0 1.3 shard_map.106
  104.4 2.5 %collective-permute-start.5 = (bf16[144,384]{1,0:T(8,128)(2,1)S(1)}, bf16[144,384]{1,0:T(8,128)(2,1)S(1)}, u32[]{:S(2)}, u32[]{:S(2)}) collective-permute-start(bf16[144,384]{1,0:T(8,128)(2,1)S(1)} %shard_map.106), channel_id=1, source_target_pairs={{0,16},{8,24},{16,0},{24,8},{1,17},{9,25},{17,1},{25,9},{2,18},{10... | collective-permute-start | bytes 331784 | tf_op jit(solution)/shard_map/ppermute | solution.py:341
  106.9 0.0 collective-permute-done.6.q_ref
  106.9 1.3 shard_map.107
  108.2 0.0 copy-start.3
  108.3 3.3 %collective-permute-start.7 = (bf16[144,384]{1,0:T(8,128)(2,1)S(1)}, bf16[144,384]{1,0:T(8,128)(2,1)S(1)}, u32[]{:S(2)}, u32[]{:S(2)}) collective-permute-start(bf16[144,384]{1,0:T(8,128)(2,1)S(1)} %shard_map.107), channel_id=1, source_target_pairs={{0,24},{8,0},{16,8},{24,16},{1,25},{9,1},{17,9},{25,17},{2,26},{10... | collective-permute-start | bytes 331784 | tf_op jit(solution)/shard_map/ppermute | solution.py:341
  111.5 0.0 collective-permute-done.8.q_ref
  111.5 1.4 shard_map.108
  112.9 0.1 collective-permute-start.9
  113.0 1.3 shard_map.109.p3_ref
  114.3 0.0 collective-permute-done.5.p0_ref
  114.3 0.2 collective-permute-done.7.p1_ref
  114.5 4.2 %collective-permute-done.9.p2_ref = bf16[144,384]{1,0:T(8,128)(2,1)S(1)} collective-permute-done((bf16[144,384]{1,0:T(8,128)(2,1)S(1)}, bf16[144,384]{1,0:T(8,128)(2,1)S(1)}, u32[]{:S(2)}, u32[]{:S(2)}) %collective-permute-start.9) | collective-permute-done | bytes 110624 | tf_op jit(solution)/shard_map/ppermute | solution.py:341
  118.8 0.6 shard_map.110
  119.3 0.1 collective-permute-start.10
  119.4 3.3 %collective-permute-done.10 = bf16[64,384]{1,0:T(8,128)(2,1)S(1)} collective-permute-done((bf16[64,384]{1,0:T(8,128)(2,1)S(1)}, bf16[64,384]{1,0:T(8,128)(2,1)S(1)}, u32[]{:S(2)}, u32[]{:S(2)}) %collective-permute-start.10) | collective-permute-done | bytes 49184 | tf_op jit(solution)/shard_map/ppermute | solution.py:344
  122.8 19.1 %all_gather.23.attended_ref = bf16[4,128,384]{2,1,0:T(8,128)(2,1)S(1)} all-gather(bf16[1,128,384]{2,1,0:T(8,128)(2,1)S(1)} %maximum_select_fusion), channel_id=1, replica_groups=mesh['yh'=2,'xj'=2,'xi'=2,'zo'=4,'zi'=2,'yl'=2,'c'=2] {'yl','c'}, dimensions={0}, use_global_device_ids=true | all-gather | bytes 491520 | tf_op jit(solution)/shard_map/all_gather | solution.py:346
  141.9 0.0 copy-done.3
  141.9 1.7 %copy-done.2 = bf16[3072,384]{1,0:T(8,128)(2,1)S(1)} copy-done((bf16[3072,384]{1,0:T(8,128)(2,1)S(1)}, bf16[3072,384]{1,0:T(8,128)(2,1)}, u32[]{:S(2)}) %copy-start.2) | copy-done | bytes 2359320
  143.6 1.6 %shard_map.111 = bf16[2,64,768]{2,1,0:T(8,128)(2,1)} custom-call(bf16[4,128,384]{2,1,0:T(8,128)(2,1)S(1)} %all_gather.23.attended_ref, bf16[4,2,8,48,384]{4,3,2,1,0:T(8,128)(2,1)S(1)} %bitcast.52, f32[16,768]{1,0:T(8,128)S(1)} %copy-done.3), custom_call_target="tpu_custom_call" | custom-call | flops 301989888 | tf_op jit(solution)/shard_map/pallas_call | solution.py:22
  (10 shorter events, 0.1 us)
Async XLA Ops:
  6.5 8.6 %copy-start = (bf16[2,2,8,384]{3,2,1,0:T(8,128)(2,1)S(1)}, bf16[2,2,8,384]{3,2,1,0:T(8,128)(2,1)}, u32[]{:S(2)}) copy-start(bf16[2,2,8,384]{3,2,1,0:T(8,128)(2,1)} %param.11) | copy-start | bytes 73732
  6.5 50.0 %all-gather.7.cloned.1.call-start = ((), (), s32[]{:S(2)}) async-start(), calls=%async_computation.4 | async-start | bytes 2433024 | tf_op jit(solution)/shard_map/all_gather | solution.py:279
  6.5 6.9 %collective-permute-start.1 = (bf16[3,48,384]{2,1,0:T(8,128)(2,1)}, bf16[3,48,384]{2,1,0:T(8,128)(2,1)S(1)}, u32[]{:S(2)}, u32[]{:S(2)}) collective-permute-start(bf16[3,48,384]{2,1,0:T(8,128)(2,1)} %bitcast.61), channel_id=1, source_target_pairs={{0,128},{128,0},{1,129},{129,1},{2,130},{130,2},{3,131},{131,3},{4... | collective-permute-start | bytes 331784 | tf_op jit(solution)/shard_map/ppermute | solution.py:259
  9.5 4.0 %collective-permute-start = (bf16[48,384]{1,0:T(8,128)(2,1)}, bf16[48,384]{1,0:T(8,128)(2,1)S(1)}, u32[]{:S(2)}, u32[]{:S(2)}) collective-permute-start(bf16[48,384]{1,0:T(8,128)(2,1)} %bitcast.65), channel_id=1, source_target_pairs={{0,0},{1,64},{2,128},{3,192},{32,32},{33,96},{34,160},{35,224},{64... | collective-permute-start | bytes 110600 | tf_op jit(solution)/shard_map/ppermute | solution.py:269
  15.2 14.1 %collective-permute-start.2 = (bf16[80,384]{1,0:T(8,128)(2,1)S(1)}, bf16[80,384]{1,0:T(8,128)(2,1)S(1)}, u32[]{:S(2)}, u32[]{:S(2)}) collective-permute-start(bf16[80,384]{1,0:T(8,128)(2,1)S(1)} %get-tuple-element.28), channel_id=1, source_target_pairs={{0,32},{32,0},{1,33},{33,1},{2,34},{34,2},{3,35},{35,3},{4,36},{36... | collective-permute-start | bytes 184328 | tf_op jit(solution)/shard_map/ppermute | solution.py:286
  30.8 27.6 %all-to-all-start = ((bf16[4,128,768]{2,1,0:T(8,128)(2,1)}), bf16[4,128,768]{2,1,0:T(8,128)(2,1)S(1)}, u32[]{:S(2)}, u32[]{:S(2)}) async-start(bf16[4,128,768]{2,1,0:T(8,128)(2,1)} %shard_map.101), calls=%async_computation | async-start | bytes 1572864 | tf_op jit(solution)/shard_map/all_to_all | solution.py:290
  35.4 106.5 %all-gather.5.cloned.1.call-start = ((), (), s32[]{:S(2)}) async-start(), calls=%async_computation.3 | async-start | bytes 2654208 | tf_op jit(solution)/shard_map/all_gather | solution.py:300
  56.5 1.9 %copy-start.1 = (bf16[768,1408]{1,0:T(8,128)(2,1)S(1)}, bf16[768,1408]{1,0:T(8,128)(2,1)}, u32[]{:S(2)}) copy-start(bf16[768,1408]{1,0:T(8,128)(2,1)} %all-gather.7.cloned.1.call-done) | copy-start | bytes 6488068
  61.7 14.3 %copy-start.4 = (f32[128]{0:T(128)S(1)}, f32[128]{0:T(128)}, u32[]{:S(2)}) copy-start(f32[128]{0:T(128)} %param.19) | copy-start | bytes 1540
  61.7 14.2 %all-to-all-start.1 = ((bf16[4,128,1152]{2,1,0:T(8,128)(2,1)}), bf16[4,128,1152]{2,1,0:T(8,128)(2,1)S(1)}, u32[]{:S(2)}, u32[]{:S(2)}) async-start(bf16[4,128,1152]{2,1,0:T(8,128)(2,1)} %shard_map.103), calls=%async_computation.1 | async-start | bytes 2359296 | tf_op jit(solution)/shard_map/all_to_all | solution.py:312
  76.3 5.3 %collective-permute-start.4 = (bf16[288,384]{1,0:T(8,128)(2,1)S(1)}, bf16[288,384]{1,0:T(8,128)(2,1)S(1)}, u32[]{:S(2)}, u32[]{:S(2)}) collective-permute-start(bf16[288,384]{1,0:T(8,128)(2,1)S(1)} %shard_map.105), channel_id=1, source_target_pairs={{0,4},{4,0},{1,5},{5,1},{2,6},{6,2},{3,7},{7,3},{8,12},{12,8},{9,1... | collective-permute-start | bytes 663560 | tf_op jit(solution)/shard_map/ppermute | solution.py:330
  83.0 6.6 %copy-start.5 = (f32[128]{0:T(128)S(1)}, f32[128]{0:T(128)}, u32[]{:S(2)}) copy-start(f32[128]{0:T(128)} %param.18) | copy-start | bytes 1540
  83.0 20.0 %all-to-all-start.2 = ((bf16[4,2,288,384]{3,2,1,0:T(8,128)(2,1)}), bf16[4,2,288,384]{3,2,1,0:T(8,128)(2,1)S(1)}, u32[]{:S(2)}, u32[]{:S(2)}) async-start(bf16[4,2,288,384]{3,2,1,0:T(8,128)(2,1)} %broadcast_in_dim.53), calls=%async_computation.2 | async-start | bytes 3538944 | tf_op jit(solution)/shard_map/all_to_all | solution.py:334
  89.8 7.7 %collective-permute-start.3 = (bf16[128,384]{1,0:T(8,128)(2,1)S(1)}, bf16[128,384]{1,0:T(8,128)(2,1)S(1)}, u32[]{:S(2)}, u32[]{:S(2)}) collective-permute-start(bf16[128,384]{1,0:T(8,128)(2,1)S(1)} %shard_map.104.q_ref), channel_id=1, source_target_pairs={{0,16},{8,24},{16,0},{24,8},{1,17},{9,25},{17,1},{25,9},{2,18},{10... | collective-permute-start | bytes 294920 | tf_op jit(solution)/shard_map/ppermute | solution.py:332
  92.3 14.6 %collective-permute-start.6 = (bf16[128,384]{1,0:T(8,128)(2,1)S(1)}, bf16[128,384]{1,0:T(8,128)(2,1)S(1)}, u32[]{:S(2)}, u32[]{:S(2)}) collective-permute-start(bf16[128,384]{1,0:T(8,128)(2,1)S(1)} %shard_map.104.q_ref), channel_id=1, source_target_pairs={{0,8},{8,16},{16,24},{24,0},{1,9},{9,17},{17,25},{25,1},{2,10},{10... | collective-permute-start | bytes 294920 | tf_op jit(solution)/shard_map/ppermute | solution.py:332
  93.8 17.7 %collective-permute-start.8 = (bf16[128,384]{1,0:T(8,128)(2,1)S(1)}, bf16[128,384]{1,0:T(8,128)(2,1)S(1)}, u32[]{:S(2)}, u32[]{:S(2)}) collective-permute-start(bf16[128,384]{1,0:T(8,128)(2,1)S(1)} %shard_map.104.q_ref), channel_id=1, source_target_pairs={{0,24},{8,0},{16,8},{24,16},{1,25},{9,1},{17,9},{25,17},{2,26},{10... | collective-permute-start | bytes 294920 | tf_op jit(solution)/shard_map/ppermute | solution.py:332
  104.4 10.0 %collective-permute-start.5 = (bf16[144,384]{1,0:T(8,128)(2,1)S(1)}, bf16[144,384]{1,0:T(8,128)(2,1)S(1)}, u32[]{:S(2)}, u32[]{:S(2)}) collective-permute-start(bf16[144,384]{1,0:T(8,128)(2,1)S(1)} %shard_map.106), channel_id=1, source_target_pairs={{0,16},{8,24},{16,0},{24,8},{1,17},{9,25},{17,1},{25,9},{2,18},{10... | collective-permute-start | bytes 331784 | tf_op jit(solution)/shard_map/ppermute | solution.py:341
  108.2 33.7 %copy-start.3 = (f32[16,768]{1,0:T(8,128)S(1)}, f32[16,768]{1,0:T(8,128)}, u32[]{:S(2)}) copy-start(f32[16,768]{1,0:T(8,128)} %get-tuple-element.24.gate_ref) | copy-start | bytes 147460
  108.3 6.3 %collective-permute-start.7 = (bf16[144,384]{1,0:T(8,128)(2,1)S(1)}, bf16[144,384]{1,0:T(8,128)(2,1)S(1)}, u32[]{:S(2)}, u32[]{:S(2)}) collective-permute-start(bf16[144,384]{1,0:T(8,128)(2,1)S(1)} %shard_map.107), channel_id=1, source_target_pairs={{0,24},{8,0},{16,8},{24,16},{1,25},{9,1},{17,9},{25,17},{2,26},{10... | collective-permute-start | bytes 331784 | tf_op jit(solution)/shard_map/ppermute | solution.py:341
  112.9 5.9 %collective-permute-start.9 = (bf16[144,384]{1,0:T(8,128)(2,1)S(1)}, bf16[144,384]{1,0:T(8,128)(2,1)S(1)}, u32[]{:S(2)}, u32[]{:S(2)}) collective-permute-start(bf16[144,384]{1,0:T(8,128)(2,1)S(1)} %shard_map.108), channel_id=1, source_target_pairs={{0,8},{8,16},{16,24},{24,0},{1,9},{9,17},{17,25},{25,1},{2,10},{10... | collective-permute-start | bytes 331784 | tf_op jit(solution)/shard_map/ppermute | solution.py:341
  119.3 3.4 %collective-permute-start.10 = (bf16[64,384]{1,0:T(8,128)(2,1)S(1)}, bf16[64,384]{1,0:T(8,128)(2,1)S(1)}, u32[]{:S(2)}, u32[]{:S(2)}) collective-permute-start(bf16[64,384]{1,0:T(8,128)(2,1)S(1)} %get-tuple-element.22), channel_id=1, source_target_pairs={{0,32},{32,0},{1,33},{33,1},{2,34},{34,2},{3,35},{35,3},{4,36},{36... | collective-permute-start | bytes 147464 | tf_op jit(solution)/shard_map/ppermute | solution.py:344
  141.9 1.7 %copy-start.2 = (bf16[3072,384]{1,0:T(8,128)(2,1)S(1)}, bf16[3072,384]{1,0:T(8,128)(2,1)}, u32[]{:S(2)}) copy-start(bf16[3072,384]{1,0:T(8,128)(2,1)} %all-gather.5.cloned.1.call-done) | copy-start | bytes 7077892
Sparse Core Ops, SparseCore 0:
  14.4 42.0 all-gather.6
  59.1 80.2 all-gather.4

commit v6 on v5

--- a/solution.py
+++ b/solution.py
@@ -210,19 +210,17 @@
 
 
 def output_kernel(attended_ref, weights_ref, gate_ref, out_ref):
-    for half in range(2):
-        lanes = slice(half * 384, half * 384 + 384)
-        sums = jnp.zeros((128, 384), jnp.float32)
-        for group in range(4):
-            sums = sums + lax.dot_general(
-                attended_ref[group],
-                weights_ref[group, half].reshape(384, 384),
-                (((1,), (1,)), ((), ())),
-                preferred_element_type=jnp.float32,
-            )
-        for image in range(2):
-            rows = gate_ref[image : image + 1, lanes] * sums[64 * image : 64 * image + 64]
-            out_ref[image, :, lanes] = rows.astype(jnp.bfloat16)
+    sums = jnp.zeros((128, 384), jnp.float32)
+    for group in range(4):
+        sums = sums + lax.dot_general(
+            attended_ref[group],
+            weights_ref[group].reshape(384, 384),
+            (((1,), (1,)), ((), ())),
+            preferred_element_type=jnp.float32,
+        )
+    for image in range(2):
+        rows = gate_ref[image : image + 1, :] * sums[64 * image : 64 * image + 64]
+        out_ref[image] = rows.astype(jnp.bfloat16)
 
 
 def power_two(exponents):
@@ -332,7 +330,7 @@
         lax.ppermute(queries, "zo", [(i, (i + k) % 4) for i in range(4)]) for k in (2, 1, 3)
     ]
     kv_pair = lax.all_to_all(
-        jnp.broadcast_to(kv_pair, (4, 2, 288, 384)), ("yh", "xj"), 0, 0, tiled=True
+        jnp.broadcast_to(kv_pair, (4, 2, 288, 384)), ("xj", "yh"), 0, 0, tiled=True
     ).reshape(8, 288, 384)
     mixed = []
     for k, block in enumerate((*far_queries, queries)):
@@ -344,12 +342,21 @@
     far = lax.ppermute(far, "xi", swap)
     attended = jnp.where(first, jnp.concatenate([own, far]), jnp.concatenate([far, own]))
     attended = lax.all_gather(attended, H, axis=0)
-    return call(
+    return pl.pallas_call(
         output_kernel,
-        shape(2, 64, 768),
-        (attended, columns.reshape(4, 2, 8, 48, 384), gates),
-        flops=2 * 128 * 1536 * 768,
-    )
+        out_shape=shape(2, 64, 768),
+        grid=(2,),
+        in_specs=[
+            pl.BlockSpec((4, 128, 384), lambda half: (0, 0, 0)),
+            pl.BlockSpec((4, None, 8, 48, 384), lambda half: (0, half, 0, 0, 0)),
+            pl.BlockSpec((16, 384), lambda half: (0, half)),
+        ],
+        out_specs=pl.BlockSpec((2, 64, 384), lambda half: (0, 0, half)),
+        compiler_params=pltpu.CompilerParams(vmem_limit_bytes=WIDE_BYTES),
+        cost_estimate=pl.CostEstimate(
+            flops=2 * 128 * 1536 * 768, bytes_accessed=0, transcendentals=0
+        ),
+    )(attended, columns.reshape(4, 2, 8, 48, 384), gates)
 
 
 def solution(mesh):

time: 153 us -> 153 us (level)
  starting transfers between devices: 32.5 us -> 36.5 us
  waiting for transfers between devices: 50.2 us -> 48.4 us
  blocking collectives: 32.6 us -> 30.8 us
  local copies, waits for them, and re-layouts: 5.02 us -> 3.34 us
    ppermute x3, starting transfers between devices: 5.88 us -> 9.93 us  [per_device(): lax.ppermute(part, 'zo', [(i, (i - (2, 1, 3)[k]) % 4) for i in range(4)])]
    pallas_call x0 -> x1, Pallas kernels: none -> 3.08 us  [per_device(): pl.pallas_call(output_kernel, out_shape=shape(2, 64, 768), grid=(2,), in_...]
    ppermute x3, waiting for transfers between devices: 4.42 us -> 2.67 us  [per_device(): lax.ppermute(part, 'zo', [(i, (i - (2, 1, 3)[k]) % 4) for i in range(4)])]
    all_gather x1, blocking collectives: 19.1 us -> 17.4 us  [per_device(): attended = lax.all_gather(attended, H, axis=0)]
    unnamed x12 -> x8, local copies, waits for them, and re-layouts: 1.69 us -> 0.02 us
    pallas_call x11 -> x10, Pallas kernels: 14.6 us -> 13.1 us  [call(): pl.pallas_call(kernel, out_shape=out_shapes, in_specs=[pl.BlockSpec(memor...]
  transfers between devices with their start and end apart: 16 -> 16, of which waited for: 8 -> 7; matrix products, arithmetic and copies ran while one was open for 3% -> 3% of each run, Pallas kernels for 10% -> 10%
where the time goes in v6:
time: 153 us; the launch traced here: 152 us
  waiting for transfers between devices  48.4 us (32%)
  starting transfers between devices  36.5 us (24%)
  blocking collectives  30.8 us (20%)
  Pallas kernels  18 us (12%)
  between operations  13.6 us (9%)
  local copies, waits for them, and re-layouts  3.34 us (2%)
  other arithmetic  1.6 us (1%)
    all_gather x1, waiting for transfers between devices, per_device(): weights = lax.all_gather(line, Z, axis=0)  21.1 us
    all_gather x1, blocking collectives, per_device(): attended = lax.all_gather(attended, H, axis=0)  17.4 us
    all_gather x1, blocking collectives, per_device(): rows = lax.all_gather(rows, H, axis=0)  13.4 us
    pallas_call x10, Pallas kernels, call(): pl.pallas_call(kernel, out_shape=out_shapes, in_specs=[pl.BlockSpec(memor...  13.1 us
    ppermute x3, starting transfers between devices, per_device(): lax.ppermute(part, 'zo', [(i, (i - (2, 1, 3)[k]) % 4) for i in range(4)])  9.93 us
    all_to_all x1, waiting for transfers between devices, per_device(): partial = lax.all_to_all(partial, X, 0, 0, tiled=True)  8.97 us
    all_to_all x1, starting transfers between devices, per_device(): lax.all_to_all(jnp.broadcast_to(kv_pair, (4, 2, 288, 384)), ('xj', 'yh'),...  6.61 us
    ppermute x3, starting transfers between devices, per_device(): lax.ppermute(queries, 'zo', [(i, (i + k) % 4) for i in range(4)])  6.02 us
  transfers between devices with their start and end apart: 16, of which 7 were waited for; matrix products, arithmetic and copies ran while one was open for 3% of the time, Pallas kernels for 10%

profile of v6, /device:TPU:7, one launch (start us, length us, event | category | flops | bytes accessed | tf_op | source)
XLA Modules:
  0.0 152.4 jit_solution(14918711368601882951)
XLA Ops:
  6.5 0.0 copy-start
  6.5 0.0 all-gather.7.cloned.1.call-start
  6.5 2.9 %collective-permute-start.1 = (bf16[3,48,384]{2,1,0:T(8,128)(2,1)}, bf16[3,48,384]{2,1,0:T(8,128)(2,1)S(1)}, u32[]{:S(2)}, u32[]{:S(2)}) collective-permute-start(bf16[3,48,384]{2,1,0:T(8,128)(2,1)} %bitcast.61), channel_id=1, source_target_pairs={{0,128},{128,0},{1,129},{129,1},{2,130},{130,2},{3,131},{131,3},{4... | collective-permute-start | bytes 331784 | tf_op jit(solution)/shard_map/ppermute | solution.py:257
  9.5 1.4 collective-permute-start
  10.9 0.8 slice_bitcast_fusion.5
  11.7 1.8 %shard_map.100 = (bf16[144,768]{1,0:T(8,128)(2,1)}, f32[16,768]{1,0:T(8,128)}) custom-call(bf16[128,768]{1,0:T(8,128)(2,1)} %bitcast.59, bf16[3,28,768]{2,1,0:T(8,128)(2,1)} %bitcast.60, s32[2]{0:T(128)} %steps_ref.1), custom_call_target="tpu_custom_call" | custom-call | tf_op jit(solution)/shard_map/pallas_call | solution.py:22
  13.5 0.0 collective-permute-done
  13.5 0.0 collective-permute-done.1
  13.5 0.7 maximum_maximum_fusion
  14.3 0.0 all-gather.7.cloned.1.call-update
  14.3 0.7 fusion.10
  15.0 0.1 copy.16
  15.1 0.0 copy-done
  15.2 0.6 collective-permute-start.2
  15.9 13.4 %all-gather = bf16[576,768]{1,0:T(8,128)(2,1)S(1)} all-gather(bf16[144,768]{1,0:T(8,128)(2,1)} %get-tuple-element.16), channel_id=2, replica_groups=mesh['yh'=2,'xj'=2,'xi'=2,'zo'=4,'zi'=2,'yl'=2,'c'=2] {'yl','c'}, dimensions={0}, use_global_device_ids=true | all-gather | bytes 1105920 | tf_op jit(solution)/shard_map/all_gather | solution.py:285
  29.3 0.0 collective-permute-done.2.got_ref
  29.3 1.5 %shard_map.101 = bf16[4,128,768]{2,1,0:T(8,128)(2,1)} custom-call(bf16[4,144,768]{2,1,0:T(8,128)(2,1)S(1)} %bitcast.51, s32[1]{0:T(128)} %bitcast.16.y_ref), custom_call_target="tpu_custom_call" | custom-call | tf_op jit(solution)/shard_map/pallas_call | solution.py:22
  30.8 4.6 %all-to-all-start = ((bf16[4,128,768]{2,1,0:T(8,128)(2,1)}), bf16[4,128,768]{2,1,0:T(8,128)(2,1)S(1)}, u32[]{:S(2)}, u32[]{:S(2)}) async-start(bf16[4,128,768]{2,1,0:T(8,128)(2,1)} %shard_map.101), calls=%async_computation | async-start | bytes 1572864 | tf_op jit(solution)/shard_map/all_to_all | solution.py:288
  35.4 0.0 all-gather.5.cloned.1.call-start
  35.4 21.1 %all-gather.7.cloned.1.call-done = bf16[768,1408]{1,0:T(8,128)(2,1)} async-done(((bf16[96,1408]{1,0:T(8,128)(2,1)}), bf16[768,1408]{1,0:T(8,128)(2,1)}) %all-gather.7.cloned.1.call-update) | async-done | bytes 2162704 | tf_op jit(solution)/shard_map/all_gather | solution.py:277
  56.5 0.0 copy-start.1
  56.5 1.9 %shard_map.102 = bf16[8,48,384]{2,1,0:T(8,128)(2,1)} custom-call(bf16[8,96,1408]{2,1,0:T(8,128)(2,1)} %bitcast.49), custom_call_target="tpu_custom_call" | custom-call | tf_op jit(solution)/shard_map/pallas_call | solution.py:289
  58.4 0.0 all-to-all-done.rows_ref
  58.4 0.0 all-gather.5.cloned.1.call-update
  58.4 0.0 copy-done.1
  58.4 3.3 %shard_map.103 = bf16[4,128,1152]{2,1,0:T(8,128)(2,1)} custom-call(bf16[4,128,768]{2,1,0:T(8,128)(2,1)S(1)} %all-to-all-done.rows_ref, bf16[8,96,1408]{2,1,0:T(8,128)(2,1)S(1)} %bitcast.50), custom_call_target="tpu_custom_call" | custom-call | flops 905969664 | tf_op jit(solution)/shard_map/pallas_call | solution.py:22
  61.7 0.0 copy-start.2
  61.7 4.2 %all-to-all-start.1 = ((bf16[4,128,1152]{2,1,0:T(8,128)(2,1)}), bf16[4,128,1152]{2,1,0:T(8,128)(2,1)S(1)}, u32[]{:S(2)}, u32[]{:S(2)}) async-start(bf16[4,128,1152]{2,1,0:T(8,128)(2,1)} %shard_map.103), calls=%async_computation.1 | async-start | bytes 2359296 | tf_op jit(solution)/shard_map/all_to_all | solution.py:310
  66.0 1.0 dynamic-slice_bitcast_fusion.1
  67.0 9.0 %all-to-all-done.1.part_ref = bf16[4,128,1152]{2,1,0:T(8,128)(2,1)S(1)} async-done(((bf16[4,128,1152]{2,1,0:T(8,128)(2,1)}), bf16[4,128,1152]{2,1,0:T(8,128)(2,1)S(1)}, u32[]{:S(2)}, u32[]{:S(2)}) %all-to-all-start.1) | async-done | bytes 1179680 | tf_op jit(solution)/shard_map/all_to_all | solution.py:310
  76.0 0.0 copy-done.2
  76.0 0.4 shard_map.105
  76.4 0.1 collective-permute-start.4
  76.5 5.2 %collective-permute-done.4 = bf16[288,384]{1,0:T(8,128)(2,1)S(1)} collective-permute-done((bf16[288,384]{1,0:T(8,128)(2,1)S(1)}, bf16[288,384]{1,0:T(8,128)(2,1)S(1)}, u32[]{:S(2)}, u32[]{:S(2)}) %collective-permute-start.4) | collective-permute-done | bytes 221216 | tf_op jit(solution)/shard_map/ppermute | solution.py:328
  81.6 0.1 pad_maximum_fusion
  81.7 1.4 broadcast_in_dim.53
  83.1 0.0 copy-start.3
  83.1 6.6 %all-to-all-start.2 = ((bf16[4,2,288,384]{3,2,1,0:T(8,128)(2,1)}), bf16[4,2,288,384]{3,2,1,0:T(8,128)(2,1)S(1)}, u32[]{:S(2)}, u32[]{:S(2)}) async-start(bf16[4,2,288,384]{3,2,1,0:T(8,128)(2,1)} %broadcast_in_dim.53), calls=%async_computation.2 | async-start | bytes 3538944 | tf_op jit(solution)/shard_map/all_to_all | solution.py:332
  89.7 0.0 copy-done.3
  89.7 0.1 shard_map.104.q_ref
  89.8 2.4 %collective-permute-start.3 = (bf16[128,384]{1,0:T(8,128)(2,1)S(1)}, bf16[128,384]{1,0:T(8,128)(2,1)S(1)}, u32[]{:S(2)}, u32[]{:S(2)}) collective-permute-start(bf16[128,384]{1,0:T(8,128)(2,1)S(1)} %shard_map.104.q_ref), channel_id=1, source_target_pairs={{0,16},{8,24},{16,0},{24,8},{1,17},{9,25},{17,1},{25,9},{2,18},{10... | collective-permute-start | bytes 294920 | tf_op jit(solution)/shard_map/ppermute | solution.py:330
  92.3 1.6 %collective-permute-start.6 = (bf16[128,384]{1,0:T(8,128)(2,1)S(1)}, bf16[128,384]{1,0:T(8,128)(2,1)S(1)}, u32[]{:S(2)}, u32[]{:S(2)}) collective-permute-start(bf16[128,384]{1,0:T(8,128)(2,1)S(1)} %shard_map.104.q_ref), channel_id=1, source_target_pairs={{0,8},{8,16},{16,24},{24,0},{1,9},{9,17},{17,25},{25,1},{2,10},{10... | collective-permute-start | bytes 294920 | tf_op jit(solution)/shard_map/ppermute | solution.py:330
  93.8 2.0 %collective-permute-start.8 = (bf16[128,384]{1,0:T(8,128)(2,1)S(1)}, bf16[128,384]{1,0:T(8,128)(2,1)S(1)}, u32[]{:S(2)}, u32[]{:S(2)}) collective-permute-start(bf16[128,384]{1,0:T(8,128)(2,1)S(1)} %shard_map.104.q_ref), channel_id=1, source_target_pairs={{0,24},{8,0},{16,8},{24,16},{1,25},{9,1},{17,9},{25,17},{2,26},{10... | collective-permute-start | bytes 294920 | tf_op jit(solution)/shard_map/ppermute | solution.py:330
  95.8 1.6 %collective-permute-done.3.q_ref = bf16[128,384]{1,0:T(8,128)(2,1)S(1)} collective-permute-done((bf16[128,384]{1,0:T(8,128)(2,1)S(1)}, bf16[128,384]{1,0:T(8,128)(2,1)S(1)}, u32[]{:S(2)}, u32[]{:S(2)}) %collective-permute-start.3) | collective-permute-done | bytes 98336 | tf_op jit(solution)/shard_map/ppermute | solution.py:330
  97.5 5.5 %all-to-all-done.2 = bf16[4,2,288,384]{3,2,1,0:T(8,128)(2,1)S(1)} async-done(((bf16[4,2,288,384]{3,2,1,0:T(8,128)(2,1)}), bf16[4,2,288,384]{3,2,1,0:T(8,128)(2,1)S(1)}, u32[]{:S(2)}, u32[]{:S(2)}) %all-to-all-start.2) | async-done | bytes 1769504 | tf_op jit(solution)/shard_map/all_to_all | solution.py:332
  103.0 1.3 shard_map.106
  104.3 2.9 %collective-permute-start.5 = (bf16[144,384]{1,0:T(8,128)(2,1)S(1)}, bf16[144,384]{1,0:T(8,128)(2,1)S(1)}, u32[]{:S(2)}, u32[]{:S(2)}) collective-permute-start(bf16[144,384]{1,0:T(8,128)(2,1)S(1)} %shard_map.106), channel_id=1, source_target_pairs={{0,16},{8,24},{16,0},{24,8},{1,17},{9,25},{17,1},{25,9},{2,18},{10... | collective-permute-start | bytes 331784 | tf_op jit(solution)/shard_map/ppermute | solution.py:339
  107.3 0.0 collective-permute-done.6.q_ref
  107.3 1.3 shard_map.107
  108.6 4.8 %collective-permute-start.7 = (bf16[144,384]{1,0:T(8,128)(2,1)S(1)}, bf16[144,384]{1,0:T(8,128)(2,1)S(1)}, u32[]{:S(2)}, u32[]{:S(2)}) collective-permute-start(bf16[144,384]{1,0:T(8,128)(2,1)S(1)} %shard_map.107), channel_id=1, source_target_pairs={{0,24},{8,0},{16,8},{24,16},{1,25},{9,1},{17,9},{25,17},{2,26},{10... | collective-permute-start | bytes 331784 | tf_op jit(solution)/shard_map/ppermute | solution.py:339
  113.5 0.0 collective-permute-done.8.q_ref
  113.5 1.3 shard_map.108
  114.8 2.2 %collective-permute-start.9 = (bf16[144,384]{1,0:T(8,128)(2,1)S(1)}, bf16[144,384]{1,0:T(8,128)(2,1)S(1)}, u32[]{:S(2)}, u32[]{:S(2)}) collective-permute-start(bf16[144,384]{1,0:T(8,128)(2,1)S(1)} %shard_map.108), channel_id=1, source_target_pairs={{0,8},{8,16},{16,24},{24,0},{1,9},{9,17},{17,25},{25,1},{2,10},{10... | collective-permute-start | bytes 331784 | tf_op jit(solution)/shard_map/ppermute | solution.py:339
  117.0 1.3 shard_map.109.p3_ref
  118.3 0.0 collective-permute-done.5.p0_ref
  118.3 0.0 collective-permute-done.7.p1_ref
  118.4 2.7 %collective-permute-done.9.p2_ref = bf16[144,384]{1,0:T(8,128)(2,1)S(1)} collective-permute-done((bf16[144,384]{1,0:T(8,128)(2,1)S(1)}, bf16[144,384]{1,0:T(8,128)(2,1)S(1)}, u32[]{:S(2)}, u32[]{:S(2)}) %collective-permute-start.9) | collective-permute-done | bytes 110624 | tf_op jit(solution)/shard_map/ppermute | solution.py:339
  121.0 0.6 shard_map.110
  121.6 0.1 collective-permute-start.10
  121.7 3.3 %collective-permute-done.10 = bf16[64,384]{1,0:T(8,128)(2,1)S(1)} collective-permute-done((bf16[64,384]{1,0:T(8,128)(2,1)S(1)}, bf16[64,384]{1,0:T(8,128)(2,1)S(1)}, u32[]{:S(2)}, u32[]{:S(2)}) %collective-permute-start.10) | collective-permute-done | bytes 49184 | tf_op jit(solution)/shard_map/ppermute | solution.py:342
  125.0 17.4 %all_gather.23.attended_ref = bf16[4,128,384]{2,1,0:T(8,128)(2,1)} all-gather(bf16[1,128,384]{2,1,0:T(8,128)(2,1)S(1)} %maximum_select_fusion), channel_id=1, replica_groups=mesh['yh'=2,'xj'=2,'xi'=2,'zo'=4,'zi'=2,'yl'=2,'c'=2] {'yl','c'}, dimensions={0}, use_global_device_ids=true | all-gather | bytes 491520 | tf_op jit(solution)/shard_map/all_gather | solution.py:344
  142.4 0.0 all-gather.5.cloned.1.call-done
  142.4 3.1 %shard_map.111 = bf16[2,64,768]{2,1,0:T(8,128)(2,1)} custom-call(bf16[4,128,384]{2,1,0:T(8,128)(2,1)} %all_gather.23.attended_ref, bf16[4,2,8,48,384]{4,3,2,1,0:T(8,128)(2,1)} %bitcast.56, f32[16,768]{1,0:T(8,128)} %get-tuple-element.24.gate_ref), custom_call_target="tpu_custom_call" | custom-call | flops 301989888 | tf_op jit(solution)/shard_map/pallas_call | solution.py:345
  (7 shorter events, 0.1 us)
Async XLA Ops:
  6.5 8.6 %copy-start = (bf16[2,2,8,384]{3,2,1,0:T(8,128)(2,1)S(1)}, bf16[2,2,8,384]{3,2,1,0:T(8,128)(2,1)}, u32[]{:S(2)}) copy-start(bf16[2,2,8,384]{3,2,1,0:T(8,128)(2,1)} %param.11) | copy-start | bytes 73732
  6.5 50.0 %all-gather.7.cloned.1.call-start = ((), (), s32[]{:S(2)}) async-start(), calls=%async_computation.4 | async-start | bytes 2433024 | tf_op jit(solution)/shard_map/all_gather | solution.py:277
  6.5 7.0 %collective-permute-start.1 = (bf16[3,48,384]{2,1,0:T(8,128)(2,1)}, bf16[3,48,384]{2,1,0:T(8,128)(2,1)S(1)}, u32[]{:S(2)}, u32[]{:S(2)}) collective-permute-start(bf16[3,48,384]{2,1,0:T(8,128)(2,1)} %bitcast.61), channel_id=1, source_target_pairs={{0,128},{128,0},{1,129},{129,1},{2,130},{130,2},{3,131},{131,3},{4... | collective-permute-start | bytes 331784 | tf_op jit(solution)/shard_map/ppermute | solution.py:257
  9.5 4.0 %collective-permute-start = (bf16[48,384]{1,0:T(8,128)(2,1)}, bf16[48,384]{1,0:T(8,128)(2,1)S(1)}, u32[]{:S(2)}, u32[]{:S(2)}) collective-permute-start(bf16[48,384]{1,0:T(8,128)(2,1)} %bitcast.65), channel_id=1, source_target_pairs={{0,0},{1,64},{2,128},{3,192},{32,32},{33,96},{34,160},{35,224},{64... | collective-permute-start | bytes 110600 | tf_op jit(solution)/shard_map/ppermute | solution.py:267
  15.2 14.1 %collective-permute-start.2 = (bf16[80,384]{1,0:T(8,128)(2,1)S(1)}, bf16[80,384]{1,0:T(8,128)(2,1)S(1)}, u32[]{:S(2)}, u32[]{:S(2)}) collective-permute-start(bf16[80,384]{1,0:T(8,128)(2,1)S(1)} %get-tuple-element.28), channel_id=1, source_target_pairs={{0,32},{32,0},{1,33},{33,1},{2,34},{34,2},{3,35},{35,3},{4,36},{36... | collective-permute-start | bytes 184328 | tf_op jit(solution)/shard_map/ppermute | solution.py:284
  30.8 27.6 %all-to-all-start = ((bf16[4,128,768]{2,1,0:T(8,128)(2,1)}), bf16[4,128,768]{2,1,0:T(8,128)(2,1)S(1)}, u32[]{:S(2)}, u32[]{:S(2)}) async-start(bf16[4,128,768]{2,1,0:T(8,128)(2,1)} %shard_map.101), calls=%async_computation | async-start | bytes 1572864 | tf_op jit(solution)/shard_map/all_to_all | solution.py:288
  35.4 107.0 %all-gather.5.cloned.1.call-start = ((), (), s32[]{:S(2)}) async-start(), calls=%async_computation.3 | async-start | bytes 2654208 | tf_op jit(solution)/shard_map/all_gather | solution.py:298
  56.5 1.9 %copy-start.1 = (bf16[768,1408]{1,0:T(8,128)(2,1)S(1)}, bf16[768,1408]{1,0:T(8,128)(2,1)}, u32[]{:S(2)}) copy-start(bf16[768,1408]{1,0:T(8,128)(2,1)} %all-gather.7.cloned.1.call-done) | copy-start | bytes 6488068
  61.7 14.3 %copy-start.2 = (f32[128]{0:T(128)S(1)}, f32[128]{0:T(128)}, u32[]{:S(2)}) copy-start(f32[128]{0:T(128)} %param.19) | copy-start | bytes 1540
  61.7 14.2 %all-to-all-start.1 = ((bf16[4,128,1152]{2,1,0:T(8,128)(2,1)}), bf16[4,128,1152]{2,1,0:T(8,128)(2,1)S(1)}, u32[]{:S(2)}, u32[]{:S(2)}) async-start(bf16[4,128,1152]{2,1,0:T(8,128)(2,1)} %shard_map.103), calls=%async_computation.1 | async-start | bytes 2359296 | tf_op jit(solution)/shard_map/all_to_all | solution.py:310
  76.4 5.3 %collective-permute-start.4 = (bf16[288,384]{1,0:T(8,128)(2,1)S(1)}, bf16[288,384]{1,0:T(8,128)(2,1)S(1)}, u32[]{:S(2)}, u32[]{:S(2)}) collective-permute-start(bf16[288,384]{1,0:T(8,128)(2,1)S(1)} %shard_map.105), channel_id=1, source_target_pairs={{0,4},{4,0},{1,5},{5,1},{2,6},{6,2},{3,7},{7,3},{8,12},{12,8},{9,1... | collective-permute-start | bytes 663560 | tf_op jit(solution)/shard_map/ppermute | solution.py:328
  83.1 6.6 %copy-start.3 = (f32[128]{0:T(128)S(1)}, f32[128]{0:T(128)}, u32[]{:S(2)}) copy-start(f32[128]{0:T(128)} %param.18) | copy-start | bytes 1540
  83.1 19.9 %all-to-all-start.2 = ((bf16[4,2,288,384]{3,2,1,0:T(8,128)(2,1)}), bf16[4,2,288,384]{3,2,1,0:T(8,128)(2,1)S(1)}, u32[]{:S(2)}, u32[]{:S(2)}) async-start(bf16[4,2,288,384]{3,2,1,0:T(8,128)(2,1)} %broadcast_in_dim.53), calls=%async_computation.2 | async-start | bytes 3538944 | tf_op jit(solution)/shard_map/all_to_all | solution.py:332
  89.8 7.7 %collective-permute-start.3 = (bf16[128,384]{1,0:T(8,128)(2,1)S(1)}, bf16[128,384]{1,0:T(8,128)(2,1)S(1)}, u32[]{:S(2)}, u32[]{:S(2)}) collective-permute-start(bf16[128,384]{1,0:T(8,128)(2,1)S(1)} %shard_map.104.q_ref), channel_id=1, source_target_pairs={{0,16},{8,24},{16,0},{24,8},{1,17},{9,25},{17,1},{25,9},{2,18},{10... | collective-permute-start | bytes 294920 | tf_op jit(solution)/shard_map/ppermute | solution.py:330
  92.3 15.0 %collective-permute-start.6 = (bf16[128,384]{1,0:T(8,128)(2,1)S(1)}, bf16[128,384]{1,0:T(8,128)(2,1)S(1)}, u32[]{:S(2)}, u32[]{:S(2)}) collective-permute-start(bf16[128,384]{1,0:T(8,128)(2,1)S(1)} %shard_map.104.q_ref), channel_id=1, source_target_pairs={{0,8},{8,16},{16,24},{24,0},{1,9},{9,17},{17,25},{25,1},{2,10},{10... | collective-permute-start | bytes 294920 | tf_op jit(solution)/shard_map/ppermute | solution.py:330
  93.8 19.6 %collective-permute-start.8 = (bf16[128,384]{1,0:T(8,128)(2,1)S(1)}, bf16[128,384]{1,0:T(8,128)(2,1)S(1)}, u32[]{:S(2)}, u32[]{:S(2)}) collective-permute-start(bf16[128,384]{1,0:T(8,128)(2,1)S(1)} %shard_map.104.q_ref), channel_id=1, source_target_pairs={{0,24},{8,0},{16,8},{24,16},{1,25},{9,1},{17,9},{25,17},{2,26},{10... | collective-permute-start | bytes 294920 | tf_op jit(solution)/shard_map/ppermute | solution.py:330
  104.3 14.0 %collective-permute-start.5 = (bf16[144,384]{1,0:T(8,128)(2,1)S(1)}, bf16[144,384]{1,0:T(8,128)(2,1)S(1)}, u32[]{:S(2)}, u32[]{:S(2)}) collective-permute-start(bf16[144,384]{1,0:T(8,128)(2,1)S(1)} %shard_map.106), channel_id=1, source_target_pairs={{0,16},{8,24},{16,0},{24,8},{1,17},{9,25},{17,1},{25,9},{2,18},{10... | collective-permute-start | bytes 331784 | tf_op jit(solution)/shard_map/ppermute | solution.py:339
  108.6 9.7 %collective-permute-start.7 = (bf16[144,384]{1,0:T(8,128)(2,1)S(1)}, bf16[144,384]{1,0:T(8,128)(2,1)S(1)}, u32[]{:S(2)}, u32[]{:S(2)}) collective-permute-start(bf16[144,384]{1,0:T(8,128)(2,1)S(1)} %shard_map.107), channel_id=1, source_target_pairs={{0,24},{8,0},{16,8},{24,16},{1,25},{9,1},{17,9},{25,17},{2,26},{10... | collective-permute-start | bytes 331784 | tf_op jit(solution)/shard_map/ppermute | solution.py:339
  114.8 6.2 %collective-permute-start.9 = (bf16[144,384]{1,0:T(8,128)(2,1)S(1)}, bf16[144,384]{1,0:T(8,128)(2,1)S(1)}, u32[]{:S(2)}, u32[]{:S(2)}) collective-permute-start(bf16[144,384]{1,0:T(8,128)(2,1)S(1)} %shard_map.108), channel_id=1, source_target_pairs={{0,8},{8,16},{16,24},{24,0},{1,9},{9,17},{17,25},{25,1},{2,10},{10... | collective-permute-start | bytes 331784 | tf_op jit(solution)/shard_map/ppermute | solution.py:339
  121.6 3.4 %collective-permute-start.10 = (bf16[64,384]{1,0:T(8,128)(2,1)S(1)}, bf16[64,384]{1,0:T(8,128)(2,1)S(1)}, u32[]{:S(2)}, u32[]{:S(2)}) collective-permute-start(bf16[64,384]{1,0:T(8,128)(2,1)S(1)} %get-tuple-element.22), channel_id=1, source_target_pairs={{0,32},{32,0},{1,33},{33,1},{2,34},{34,2},{3,35},{35,3},{4,36},{36... | collective-permute-start | bytes 147464 | tf_op jit(solution)/shard_map/ppermute | solution.py:342
Sparse Core Ops, SparseCore 0:
  14.4 42.0 all-gather.6
  59.1 80.2 all-gather.4

commit v7 on v5

--- a/solution.py
+++ b/solution.py
@@ -332,7 +332,7 @@
         lax.ppermute(queries, "zo", [(i, (i + k) % 4) for i in range(4)]) for k in (2, 1, 3)
     ]
     kv_pair = lax.all_to_all(
-        jnp.broadcast_to(kv_pair, (4, 2, 288, 384)), ("yh", "xj"), 0, 0, tiled=True
+        jnp.broadcast_to(kv_pair, (4, 2, 288, 384)), ("xj", "yh"), 0, 0, tiled=True
     ).reshape(8, 288, 384)
     mixed = []
     for k, block in enumerate((*far_queries, queries)):

time: 153 us -> 153 us (level)
  starting transfers between devices: 32.5 us -> 36.5 us
  blocking collectives: 32.6 us -> 30.4 us
  waiting for transfers between devices: 50.2 us -> 48.5 us
    ppermute x3, starting transfers between devices: 5.88 us -> 9.9 us  [per_device(): lax.ppermute(part, 'zo', [(i, (i - (2, 1, 3)[k]) % 4) for i in range(4)])]
    all_gather x1, blocking collectives: 19.1 us -> 16.9 us  [per_device(): attended = lax.all_gather(attended, H, axis=0)]
    ppermute x3, waiting for transfers between devices: 4.42 us -> 2.67 us  [per_device(): lax.ppermute(part, 'zo', [(i, (i - (2, 1, 3)[k]) % 4) for i in range(4)])]
  transfers between devices with their start and end apart: 16 -> 16, of which waited for: 8 -> 7; matrix products, arithmetic and copies ran while one was open for 3% -> 3% of each run, Pallas kernels for 10% -> 10%
where the time goes in v7:
time: 153 us; the launch traced here: 152 us
  waiting for transfers between devices  48.5 us (32%)
  starting transfers between devices  36.5 us (24%)
  blocking collectives  30.4 us (20%)
  Pallas kernels  16.5 us (11%)
  between operations  13.6 us (9%)
  local copies, waits for them, and re-layouts  5.02 us (3%)
  other arithmetic  1.6 us (1%)
    all_gather x1, waiting for transfers between devices, per_device(): weights = lax.all_gather(line, Z, axis=0)  21.1 us
    all_gather x1, blocking collectives, per_device(): attended = lax.all_gather(attended, H, axis=0)  16.9 us
    pallas_call x11, Pallas kernels, call(): pl.pallas_call(kernel, out_shape=out_shapes, in_specs=[pl.BlockSpec(memor...  14.6 us
    all_gather x1, blocking collectives, per_device(): rows = lax.all_gather(rows, H, axis=0)  13.4 us
    ppermute x3, starting transfers between devices, per_device(): lax.ppermute(part, 'zo', [(i, (i - (2, 1, 3)[k]) % 4) for i in range(4)])  9.9 us
    all_to_all x1, waiting for transfers between devices, per_device(): partial = lax.all_to_all(partial, X, 0, 0, tiled=True)  8.97 us
    all_to_all x1, starting transfers between devices, per_device(): lax.all_to_all(jnp.broadcast_to(kv_pair, (4, 2, 288, 384)), ('xj', 'yh'),...  6.63 us
    ppermute x3, starting transfers between devices, per_device(): lax.ppermute(queries, 'zo', [(i, (i + k) % 4) for i in range(4)])  6 us
  transfers between devices with their start and end apart: 16, of which 7 were waited for; matrix products, arithmetic and copies ran while one was open for 3% of the time, Pallas kernels for 10%

profile of v7, /device:TPU:7, one launch (start us, length us, event | category | flops | bytes accessed | tf_op | source)
XLA Modules:
  0.0 152.1 jit_solution(2525496810837684461)
XLA Ops:
  6.5 0.0 copy-start
  6.5 0.0 all-gather.7.cloned.1.call-start
  6.5 2.9 %collective-permute-start.1 = (bf16[3,48,384]{2,1,0:T(8,128)(2,1)}, bf16[3,48,384]{2,1,0:T(8,128)(2,1)S(1)}, u32[]{:S(2)}, u32[]{:S(2)}) collective-permute-start(bf16[3,48,384]{2,1,0:T(8,128)(2,1)} %bitcast.61), channel_id=1, source_target_pairs={{0,128},{128,0},{1,129},{129,1},{2,130},{130,2},{3,131},{131,3},{4... | collective-permute-start | bytes 331784 | tf_op jit(solution)/shard_map/ppermute | solution.py:259
  9.5 1.4 collective-permute-start
  10.9 0.8 slice_bitcast_fusion.5
  11.7 1.8 %shard_map.100 = (bf16[144,768]{1,0:T(8,128)(2,1)}, f32[16,768]{1,0:T(8,128)}) custom-call(bf16[128,768]{1,0:T(8,128)(2,1)} %bitcast.59, bf16[3,28,768]{2,1,0:T(8,128)(2,1)} %bitcast.60, s32[2]{0:T(128)} %steps_ref.1), custom_call_target="tpu_custom_call" | custom-call | tf_op jit(solution)/shard_map/pallas_call | solution.py:22
  13.5 0.0 collective-permute-done
  13.5 0.0 collective-permute-done.1
  13.5 0.7 maximum_maximum_fusion
  14.3 0.0 all-gather.7.cloned.1.call-update
  14.3 0.7 fusion.10
  15.0 0.1 copy.16
  15.1 0.0 copy-done
  15.2 0.6 collective-permute-start.2
  15.8 13.4 %all-gather = bf16[576,768]{1,0:T(8,128)(2,1)S(1)} all-gather(bf16[144,768]{1,0:T(8,128)(2,1)} %get-tuple-element.16), channel_id=2, replica_groups=mesh['yh'=2,'xj'=2,'xi'=2,'zo'=4,'zi'=2,'yl'=2,'c'=2] {'yl','c'}, dimensions={0}, use_global_device_ids=true | all-gather | bytes 1105920 | tf_op jit(solution)/shard_map/all_gather | solution.py:287
  29.3 0.0 collective-permute-done.2.got_ref
  29.3 1.5 %shard_map.101 = bf16[4,128,768]{2,1,0:T(8,128)(2,1)} custom-call(bf16[4,144,768]{2,1,0:T(8,128)(2,1)S(1)} %bitcast.51, s32[1]{0:T(128)} %bitcast.16.y_ref), custom_call_target="tpu_custom_call" | custom-call | tf_op jit(solution)/shard_map/pallas_call | solution.py:22
  30.8 4.6 %all-to-all-start = ((bf16[4,128,768]{2,1,0:T(8,128)(2,1)}), bf16[4,128,768]{2,1,0:T(8,128)(2,1)S(1)}, u32[]{:S(2)}, u32[]{:S(2)}) async-start(bf16[4,128,768]{2,1,0:T(8,128)(2,1)} %shard_map.101), calls=%async_computation | async-start | bytes 1572864 | tf_op jit(solution)/shard_map/all_to_all | solution.py:290
  35.4 0.0 all-gather.5.cloned.1.call-start
  35.4 21.1 %all-gather.7.cloned.1.call-done = bf16[768,1408]{1,0:T(8,128)(2,1)} async-done(((bf16[96,1408]{1,0:T(8,128)(2,1)}), bf16[768,1408]{1,0:T(8,128)(2,1)}) %all-gather.7.cloned.1.call-update) | async-done | bytes 2162704 | tf_op jit(solution)/shard_map/all_gather | solution.py:279
  56.5 0.0 copy-start.1
  56.5 1.9 %shard_map.102 = bf16[8,48,384]{2,1,0:T(8,128)(2,1)} custom-call(bf16[8,96,1408]{2,1,0:T(8,128)(2,1)} %bitcast.49), custom_call_target="tpu_custom_call" | custom-call | tf_op jit(solution)/shard_map/pallas_call | solution.py:291
  58.4 0.0 all-to-all-done.rows_ref
  58.4 0.0 all-gather.5.cloned.1.call-update
  58.4 0.0 copy-done.1
  58.4 3.3 %shard_map.103 = bf16[4,128,1152]{2,1,0:T(8,128)(2,1)} custom-call(bf16[4,128,768]{2,1,0:T(8,128)(2,1)S(1)} %all-to-all-done.rows_ref, bf16[8,96,1408]{2,1,0:T(8,128)(2,1)S(1)} %bitcast.50), custom_call_target="tpu_custom_call" | custom-call | flops 905969664 | tf_op jit(solution)/shard_map/pallas_call | solution.py:22
  61.7 0.0 copy-start.4
  61.7 4.2 %all-to-all-start.1 = ((bf16[4,128,1152]{2,1,0:T(8,128)(2,1)}), bf16[4,128,1152]{2,1,0:T(8,128)(2,1)S(1)}, u32[]{:S(2)}, u32[]{:S(2)}) async-start(bf16[4,128,1152]{2,1,0:T(8,128)(2,1)} %shard_map.103), calls=%async_computation.1 | async-start | bytes 2359296 | tf_op jit(solution)/shard_map/all_to_all | solution.py:312
  66.0 1.0 dynamic-slice_bitcast_fusion.1
  67.0 9.0 %all-to-all-done.1.part_ref = bf16[4,128,1152]{2,1,0:T(8,128)(2,1)S(1)} async-done(((bf16[4,128,1152]{2,1,0:T(8,128)(2,1)}), bf16[4,128,1152]{2,1,0:T(8,128)(2,1)S(1)}, u32[]{:S(2)}, u32[]{:S(2)}) %all-to-all-start.1) | async-done | bytes 1179680 | tf_op jit(solution)/shard_map/all_to_all | solution.py:312
  76.0 0.0 copy-done.4
  76.0 0.4 shard_map.105
  76.3 0.1 collective-permute-start.4
  76.4 5.2 %collective-permute-done.4 = bf16[288,384]{1,0:T(8,128)(2,1)S(1)} collective-permute-done((bf16[288,384]{1,0:T(8,128)(2,1)S(1)}, bf16[288,384]{1,0:T(8,128)(2,1)S(1)}, u32[]{:S(2)}, u32[]{:S(2)}) %collective-permute-start.4) | collective-permute-done | bytes 221216 | tf_op jit(solution)/shard_map/ppermute | solution.py:330
  81.6 0.1 pad_maximum_fusion
  81.7 1.4 broadcast_in_dim.53
  83.0 6.6 %all-to-all-start.2 = ((bf16[4,2,288,384]{3,2,1,0:T(8,128)(2,1)}), bf16[4,2,288,384]{3,2,1,0:T(8,128)(2,1)S(1)}, u32[]{:S(2)}, u32[]{:S(2)}) async-start(bf16[4,2,288,384]{3,2,1,0:T(8,128)(2,1)} %broadcast_in_dim.53), calls=%async_computation.2 | async-start | bytes 3538944 | tf_op jit(solution)/shard_map/all_to_all | solution.py:334
  89.7 0.0 copy-done.5
  89.7 0.1 shard_map.104.q_ref
  89.8 2.4 %collective-permute-start.3 = (bf16[128,384]{1,0:T(8,128)(2,1)S(1)}, bf16[128,384]{1,0:T(8,128)(2,1)S(1)}, u32[]{:S(2)}, u32[]{:S(2)}) collective-permute-start(bf16[128,384]{1,0:T(8,128)(2,1)S(1)} %shard_map.104.q_ref), channel_id=1, source_target_pairs={{0,16},{8,24},{16,0},{24,8},{1,17},{9,25},{17,1},{25,9},{2,18},{10... | collective-permute-start | bytes 294920 | tf_op jit(solution)/shard_map/ppermute | solution.py:332
  92.3 1.6 %collective-permute-start.6 = (bf16[128,384]{1,0:T(8,128)(2,1)S(1)}, bf16[128,384]{1,0:T(8,128)(2,1)S(1)}, u32[]{:S(2)}, u32[]{:S(2)}) collective-permute-start(bf16[128,384]{1,0:T(8,128)(2,1)S(1)} %shard_map.104.q_ref), channel_id=1, source_target_pairs={{0,8},{8,16},{16,24},{24,0},{1,9},{9,17},{17,25},{25,1},{2,10},{10... | collective-permute-start | bytes 294920 | tf_op jit(solution)/shard_map/ppermute | solution.py:332
  93.8 2.0 %collective-permute-start.8 = (bf16[128,384]{1,0:T(8,128)(2,1)S(1)}, bf16[128,384]{1,0:T(8,128)(2,1)S(1)}, u32[]{:S(2)}, u32[]{:S(2)}) collective-permute-start(bf16[128,384]{1,0:T(8,128)(2,1)S(1)} %shard_map.104.q_ref), channel_id=1, source_target_pairs={{0,24},{8,0},{16,8},{24,16},{1,25},{9,1},{17,9},{25,17},{2,26},{10... | collective-permute-start | bytes 294920 | tf_op jit(solution)/shard_map/ppermute | solution.py:332
  95.8 1.7 %collective-permute-done.3.q_ref = bf16[128,384]{1,0:T(8,128)(2,1)S(1)} collective-permute-done((bf16[128,384]{1,0:T(8,128)(2,1)S(1)}, bf16[128,384]{1,0:T(8,128)(2,1)S(1)}, u32[]{:S(2)}, u32[]{:S(2)}) %collective-permute-start.3) | collective-permute-done | bytes 98336 | tf_op jit(solution)/shard_map/ppermute | solution.py:332
  97.5 5.5 %all-to-all-done.2 = bf16[4,2,288,384]{3,2,1,0:T(8,128)(2,1)S(1)} async-done(((bf16[4,2,288,384]{3,2,1,0:T(8,128)(2,1)}), bf16[4,2,288,384]{3,2,1,0:T(8,128)(2,1)S(1)}, u32[]{:S(2)}, u32[]{:S(2)}) %all-to-all-start.2) | async-done | bytes 1769504 | tf_op jit(solution)/shard_map/all_to_all | solution.py:334
  103.0 1.3 shard_map.106
  104.4 2.9 %collective-permute-start.5 = (bf16[144,384]{1,0:T(8,128)(2,1)S(1)}, bf16[144,384]{1,0:T(8,128)(2,1)S(1)}, u32[]{:S(2)}, u32[]{:S(2)}) collective-permute-start(bf16[144,384]{1,0:T(8,128)(2,1)S(1)} %shard_map.106), channel_id=1, source_target_pairs={{0,16},{8,24},{16,0},{24,8},{1,17},{9,25},{17,1},{25,9},{2,18},{10... | collective-permute-start | bytes 331784 | tf_op jit(solution)/shard_map/ppermute | solution.py:341
  107.3 0.0 collective-permute-done.6.q_ref
  107.3 1.3 shard_map.107
  108.6 0.0 copy-start.3
  108.7 4.8 %collective-permute-start.7 = (bf16[144,384]{1,0:T(8,128)(2,1)S(1)}, bf16[144,384]{1,0:T(8,128)(2,1)S(1)}, u32[]{:S(2)}, u32[]{:S(2)}) collective-permute-start(bf16[144,384]{1,0:T(8,128)(2,1)S(1)} %shard_map.107), channel_id=1, source_target_pairs={{0,24},{8,0},{16,8},{24,16},{1,25},{9,1},{17,9},{25,17},{2,26},{10... | collective-permute-start | bytes 331784 | tf_op jit(solution)/shard_map/ppermute | solution.py:341
  113.5 0.0 collective-permute-done.8.q_ref
  113.5 1.4 shard_map.108
  114.8 2.2 %collective-permute-start.9 = (bf16[144,384]{1,0:T(8,128)(2,1)S(1)}, bf16[144,384]{1,0:T(8,128)(2,1)S(1)}, u32[]{:S(2)}, u32[]{:S(2)}) collective-permute-start(bf16[144,384]{1,0:T(8,128)(2,1)S(1)} %shard_map.108), channel_id=1, source_target_pairs={{0,8},{8,16},{16,24},{24,0},{1,9},{9,17},{17,25},{25,1},{2,10},{10... | collective-permute-start | bytes 331784 | tf_op jit(solution)/shard_map/ppermute | solution.py:341
  117.0 1.3 shard_map.109.p3_ref
  118.3 0.0 collective-permute-done.5.p0_ref
  118.3 0.0 collective-permute-done.7.p1_ref
  118.4 2.7 %collective-permute-done.9.p2_ref = bf16[144,384]{1,0:T(8,128)(2,1)S(1)} collective-permute-done((bf16[144,384]{1,0:T(8,128)(2,1)S(1)}, bf16[144,384]{1,0:T(8,128)(2,1)S(1)}, u32[]{:S(2)}, u32[]{:S(2)}) %collective-permute-start.9) | collective-permute-done | bytes 110624 | tf_op jit(solution)/shard_map/ppermute | solution.py:341
  121.0 0.6 shard_map.110
  121.6 0.1 collective-permute-start.10
  121.7 3.3 %collective-permute-done.10 = bf16[64,384]{1,0:T(8,128)(2,1)S(1)} collective-permute-done((bf16[64,384]{1,0:T(8,128)(2,1)S(1)}, bf16[64,384]{1,0:T(8,128)(2,1)S(1)}, u32[]{:S(2)}, u32[]{:S(2)}) %collective-permute-start.10) | collective-permute-done | bytes 49184 | tf_op jit(solution)/shard_map/ppermute | solution.py:344
  125.0 16.9 %all_gather.23.attended_ref = bf16[4,128,384]{2,1,0:T(8,128)(2,1)S(1)} all-gather(bf16[1,128,384]{2,1,0:T(8,128)(2,1)S(1)} %maximum_select_fusion), channel_id=1, replica_groups=mesh['yh'=2,'xj'=2,'xi'=2,'zo'=4,'zi'=2,'yl'=2,'c'=2] {'yl','c'}, dimensions={0}, use_global_device_ids=true | all-gather | bytes 491520 | tf_op jit(solution)/shard_map/all_gather | solution.py:346
  142.0 0.0 copy-done.3
  142.0 1.7 %copy-done.2 = bf16[3072,384]{1,0:T(8,128)(2,1)S(1)} copy-done((bf16[3072,384]{1,0:T(8,128)(2,1)S(1)}, bf16[3072,384]{1,0:T(8,128)(2,1)}, u32[]{:S(2)}) %copy-start.2) | copy-done | bytes 2359320
  143.7 1.6 %shard_map.111 = bf16[2,64,768]{2,1,0:T(8,128)(2,1)} custom-call(bf16[4,128,384]{2,1,0:T(8,128)(2,1)S(1)} %all_gather.23.attended_ref, bf16[4,2,8,48,384]{4,3,2,1,0:T(8,128)(2,1)S(1)} %bitcast.52, f32[16,768]{1,0:T(8,128)S(1)} %copy-done.3), custom_call_target="tpu_custom_call" | custom-call | flops 301989888 | tf_op jit(solution)/shard_map/pallas_call | solution.py:22
  (10 shorter events, 0.1 us)
Async XLA Ops:
  6.5 8.6 %copy-start = (bf16[2,2,8,384]{3,2,1,0:T(8,128)(2,1)S(1)}, bf16[2,2,8,384]{3,2,1,0:T(8,128)(2,1)}, u32[]{:S(2)}) copy-start(bf16[2,2,8,384]{3,2,1,0:T(8,128)(2,1)} %param.11) | copy-start | bytes 73732
  6.5 50.0 %all-gather.7.cloned.1.call-start = ((), (), s32[]{:S(2)}) async-start(), calls=%async_computation.4 | async-start | bytes 2433024 | tf_op jit(solution)/shard_map/all_gather | solution.py:279
  6.5 6.9 %collective-permute-start.1 = (bf16[3,48,384]{2,1,0:T(8,128)(2,1)}, bf16[3,48,384]{2,1,0:T(8,128)(2,1)S(1)}, u32[]{:S(2)}, u32[]{:S(2)}) collective-permute-start(bf16[3,48,384]{2,1,0:T(8,128)(2,1)} %bitcast.61), channel_id=1, source_target_pairs={{0,128},{128,0},{1,129},{129,1},{2,130},{130,2},{3,131},{131,3},{4... | collective-permute-start | bytes 331784 | tf_op jit(solution)/shard_map/ppermute | solution.py:259
  9.5 4.0 %collective-permute-start = (bf16[48,384]{1,0:T(8,128)(2,1)}, bf16[48,384]{1,0:T(8,128)(2,1)S(1)}, u32[]{:S(2)}, u32[]{:S(2)}) collective-permute-start(bf16[48,384]{1,0:T(8,128)(2,1)} %bitcast.65), channel_id=1, source_target_pairs={{0,0},{1,64},{2,128},{3,192},{32,32},{33,96},{34,160},{35,224},{64... | collective-permute-start | bytes 110600 | tf_op jit(solution)/shard_map/ppermute | solution.py:269
  15.2 14.1 %collective-permute-start.2 = (bf16[80,384]{1,0:T(8,128)(2,1)S(1)}, bf16[80,384]{1,0:T(8,128)(2,1)S(1)}, u32[]{:S(2)}, u32[]{:S(2)}) collective-permute-start(bf16[80,384]{1,0:T(8,128)(2,1)S(1)} %get-tuple-element.28), channel_id=1, source_target_pairs={{0,32},{32,0},{1,33},{33,1},{2,34},{34,2},{3,35},{35,3},{4,36},{36... | collective-permute-start | bytes 184328 | tf_op jit(solution)/shard_map/ppermute | solution.py:286
  30.8 27.6 %all-to-all-start = ((bf16[4,128,768]{2,1,0:T(8,128)(2,1)}), bf16[4,128,768]{2,1,0:T(8,128)(2,1)S(1)}, u32[]{:S(2)}, u32[]{:S(2)}) async-start(bf16[4,128,768]{2,1,0:T(8,128)(2,1)} %shard_map.101), calls=%async_computation | async-start | bytes 1572864 | tf_op jit(solution)/shard_map/all_to_all | solution.py:290
  35.4 106.6 %all-gather.5.cloned.1.call-start = ((), (), s32[]{:S(2)}) async-start(), calls=%async_computation.3 | async-start | bytes 2654208 | tf_op jit(solution)/shard_map/all_gather | solution.py:300
  56.5 1.9 %copy-start.1 = (bf16[768,1408]{1,0:T(8,128)(2,1)S(1)}, bf16[768,1408]{1,0:T(8,128)(2,1)}, u32[]{:S(2)}) copy-start(bf16[768,1408]{1,0:T(8,128)(2,1)} %all-gather.7.cloned.1.call-done) | copy-start | bytes 6488068
  61.7 14.3 %copy-start.4 = (f32[128]{0:T(128)S(1)}, f32[128]{0:T(128)}, u32[]{:S(2)}) copy-start(f32[128]{0:T(128)} %param.19) | copy-start | bytes 1540
  61.7 14.2 %all-to-all-start.1 = ((bf16[4,128,1152]{2,1,0:T(8,128)(2,1)}), bf16[4,128,1152]{2,1,0:T(8,128)(2,1)S(1)}, u32[]{:S(2)}, u32[]{:S(2)}) async-start(bf16[4,128,1152]{2,1,0:T(8,128)(2,1)} %shard_map.103), calls=%async_computation.1 | async-start | bytes 2359296 | tf_op jit(solution)/shard_map/all_to_all | solution.py:312
  76.3 5.3 %collective-permute-start.4 = (bf16[288,384]{1,0:T(8,128)(2,1)S(1)}, bf16[288,384]{1,0:T(8,128)(2,1)S(1)}, u32[]{:S(2)}, u32[]{:S(2)}) collective-permute-start(bf16[288,384]{1,0:T(8,128)(2,1)S(1)} %shard_map.105), channel_id=1, source_target_pairs={{0,4},{4,0},{1,5},{5,1},{2,6},{6,2},{3,7},{7,3},{8,12},{12,8},{9,1... | collective-permute-start | bytes 663560 | tf_op jit(solution)/shard_map/ppermute | solution.py:330
  83.0 6.6 %copy-start.5 = (f32[128]{0:T(128)S(1)}, f32[128]{0:T(128)}, u32[]{:S(2)}) copy-start(f32[128]{0:T(128)} %param.18) | copy-start | bytes 1540
  83.0 20.0 %all-to-all-start.2 = ((bf16[4,2,288,384]{3,2,1,0:T(8,128)(2,1)}), bf16[4,2,288,384]{3,2,1,0:T(8,128)(2,1)S(1)}, u32[]{:S(2)}, u32[]{:S(2)}) async-start(bf16[4,2,288,384]{3,2,1,0:T(8,128)(2,1)} %broadcast_in_dim.53), calls=%async_computation.2 | async-start | bytes 3538944 | tf_op jit(solution)/shard_map/all_to_all | solution.py:334
  89.8 7.7 %collective-permute-start.3 = (bf16[128,384]{1,0:T(8,128)(2,1)S(1)}, bf16[128,384]{1,0:T(8,128)(2,1)S(1)}, u32[]{:S(2)}, u32[]{:S(2)}) collective-permute-start(bf16[128,384]{1,0:T(8,128)(2,1)S(1)} %shard_map.104.q_ref), channel_id=1, source_target_pairs={{0,16},{8,24},{16,0},{24,8},{1,17},{9,25},{17,1},{25,9},{2,18},{10... | collective-permute-start | bytes 294920 | tf_op jit(solution)/shard_map/ppermute | solution.py:332
  92.3 15.0 %collective-permute-start.6 = (bf16[128,384]{1,0:T(8,128)(2,1)S(1)}, bf16[128,384]{1,0:T(8,128)(2,1)S(1)}, u32[]{:S(2)}, u32[]{:S(2)}) collective-permute-start(bf16[128,384]{1,0:T(8,128)(2,1)S(1)} %shard_map.104.q_ref), channel_id=1, source_target_pairs={{0,8},{8,16},{16,24},{24,0},{1,9},{9,17},{17,25},{25,1},{2,10},{10... | collective-permute-start | bytes 294920 | tf_op jit(solution)/shard_map/ppermute | solution.py:332
  93.8 19.6 %collective-permute-start.8 = (bf16[128,384]{1,0:T(8,128)(2,1)S(1)}, bf16[128,384]{1,0:T(8,128)(2,1)S(1)}, u32[]{:S(2)}, u32[]{:S(2)}) collective-permute-start(bf16[128,384]{1,0:T(8,128)(2,1)S(1)} %shard_map.104.q_ref), channel_id=1, source_target_pairs={{0,24},{8,0},{16,8},{24,16},{1,25},{9,1},{17,9},{25,17},{2,26},{10... | collective-permute-start | bytes 294920 | tf_op jit(solution)/shard_map/ppermute | solution.py:332
  104.4 14.0 %collective-permute-start.5 = (bf16[144,384]{1,0:T(8,128)(2,1)S(1)}, bf16[144,384]{1,0:T(8,128)(2,1)S(1)}, u32[]{:S(2)}, u32[]{:S(2)}) collective-permute-start(bf16[144,384]{1,0:T(8,128)(2,1)S(1)} %shard_map.106), channel_id=1, source_target_pairs={{0,16},{8,24},{16,0},{24,8},{1,17},{9,25},{17,1},{25,9},{2,18},{10... | collective-permute-start | bytes 331784 | tf_op jit(solution)/shard_map/ppermute | solution.py:341
  108.6 33.3 %copy-start.3 = (f32[16,768]{1,0:T(8,128)S(1)}, f32[16,768]{1,0:T(8,128)}, u32[]{:S(2)}) copy-start(f32[16,768]{1,0:T(8,128)} %get-tuple-element.24.gate_ref) | copy-start | bytes 147460
  108.7 9.7 %collective-permute-start.7 = (bf16[144,384]{1,0:T(8,128)(2,1)S(1)}, bf16[144,384]{1,0:T(8,128)(2,1)S(1)}, u32[]{:S(2)}, u32[]{:S(2)}) collective-permute-start(bf16[144,384]{1,0:T(8,128)(2,1)S(1)} %shard_map.107), channel_id=1, source_target_pairs={{0,24},{8,0},{16,8},{24,16},{1,25},{9,1},{17,9},{25,17},{2,26},{10... | collective-permute-start | bytes 331784 | tf_op jit(solution)/shard_map/ppermute | solution.py:341
  114.8 6.2 %collective-permute-start.9 = (bf16[144,384]{1,0:T(8,128)(2,1)S(1)}, bf16[144,384]{1,0:T(8,128)(2,1)S(1)}, u32[]{:S(2)}, u32[]{:S(2)}) collective-permute-start(bf16[144,384]{1,0:T(8,128)(2,1)S(1)} %shard_map.108), channel_id=1, source_target_pairs={{0,8},{8,16},{16,24},{24,0},{1,9},{9,17},{17,25},{25,1},{2,10},{10... | collective-permute-start | bytes 331784 | tf_op jit(solution)/shard_map/ppermute | solution.py:341
  121.6 3.4 %collective-permute-start.10 = (bf16[64,384]{1,0:T(8,128)(2,1)S(1)}, bf16[64,384]{1,0:T(8,128)(2,1)S(1)}, u32[]{:S(2)}, u32[]{:S(2)}) collective-permute-start(bf16[64,384]{1,0:T(8,128)(2,1)S(1)} %get-tuple-element.22), channel_id=1, source_target_pairs={{0,32},{32,0},{1,33},{33,1},{2,34},{34,2},{3,35},{35,3},{4,36},{36... | collective-permute-start | bytes 147464 | tf_op jit(solution)/shard_map/ppermute | solution.py:344
  142.0 1.7 %copy-start.2 = (bf16[3072,384]{1,0:T(8,128)(2,1)S(1)}, bf16[3072,384]{1,0:T(8,128)(2,1)}, u32[]{:S(2)}) copy-start(bf16[3072,384]{1,0:T(8,128)(2,1)} %all-gather.5.cloned.1.call-done) | copy-start | bytes 7077892
Sparse Core Ops, SparseCore 0:
  14.4 42.0 all-gather.6
  59.1 80.2 all-gather.4
